TPU v7x, 32 devices: a whole 2x2x4 slice. The times are simulated.
32 devices in a mesh: row: 8 (over z, y), col: 4 (over x, core).
Axes of the slice: x: 2, y: 2, z: 4, core: 2. Of those that a mesh axis runs over, the one named last changes fastest.
Arguments:
- tensor: bfloat16 [4, 4096, 8192], P(None, 'row', 'col'), may hold values from -6 to 6
- second_factor: float32 [8192, 128], P(('col', 'row')), as said below
- time_factor: float32 [4, 128], replicated, may hold values from 0.5 to 1.5
Outputs:
- first_factor: float32 [4096, 128], P(('row', 'col'))
- column_scales: float32 [128], replicated
Inputs may be any that keep to these rules, and one draw needn't show every extreme that they name: `second_factor`: real numbers of magnitude at most 120 / sqrt(8192).
All inputs are finite; a program needn't handle non-finite values.
Results may differ from a plain program's by a relative error of at most 0.0056.
Values may be sent and summed in bfloat16 or wider, within the bound.
No kernel may reach another device: no remote copies, remote signals or barrier semaphores. Data moves between devices by JAX's collectives and lax.ppermute only.
A program may use at most 64 MiB of HBM per device.

v0:
```python
import jax
import jax.numpy as jnp
from jax import lax
from jax.sharding import PartitionSpec as P


def per_device(tensor, second_factor, time_factor):
    snaps, own_rows, own_cols = tensor.shape
    total_rows = own_rows * lax.axis_size("row")
    time_gram = jnp.dot(
        time_factor.T,
        time_factor,
        precision=lax.Precision.HIGHEST,
        preferred_element_type=jnp.float32,
    )
    low_factor = second_factor.astype(jnp.bfloat16)
    partial_terms = jnp.einsum(
        "kij,jr->kir",
        tensor,
        lax.all_gather(low_factor, "row", axis=0, tiled=True),
        preferred_element_type=jnp.float32,
    )
    mttkrp = jnp.sum(partial_terms * time_factor[:, None, :], axis=0)
    local = lax.psum_scatter(mttkrp, "col", scatter_dimension=0, tiled=True)
    own_gram = jnp.dot(
        second_factor.T,
        second_factor,
        precision=lax.Precision.HIGHEST,
        preferred_element_type=jnp.float32,
    )
    gram = lax.psum(own_gram, ("row", "col"))
    lower = jnp.linalg.cholesky(gram * time_gram)
    lower, solved = (lower, jax.scipy.linalg.cho_solve((lower, True), local.T).T)
    squares = lax.psum(jnp.sum(solved * solved, axis=0), ("row", "col"))
    column_scales = jnp.sqrt(squares / total_rows + 1e-06)
    return (solved / column_scales[None, :], column_scales)


def solution(mesh):
    in_specs = (P(None, "row", "col"), P(("col", "row"), None), P())
    out_specs = (P(("row", "col"), None), P())
    return jax.shard_map(
        per_device, mesh=mesh, in_specs=in_specs, out_specs=out_specs, check_vma=False
    )
```

profile of v0, /device:TPU:0, one launch (start us, length us, event | category | flops | bytes accessed | tf_op | source)
XLA Modules:
  0.0 211.5 jit_solution(10027389327383607792)
XLA Ops:
  8.0 0.0 copy-start
  8.0 0.0 all-reduce.2.cloned.1.call-start
  8.1 2.0 fusion.8
  10.1 0.0 all-reduce.2.cloned.1.call-update
  10.1 0.0 reduce-scatter.2.cloned.1.call-start
  10.1 0.9 convert_element_type.3
  11.0 33.2 %all_gather.3 = bf16[2048,128]{1,0:T(8,128)(2,1)S(1)} all-gather(bf16[256,128]{1,0:T(8,128)(2,1)S(1)} %convert_element_type.3), channel_id=1, replica_groups=mesh['row'=8,'col'=4] {'row'}, dimensions={0}, use_global_device_ids=true | all-gather | bytes 589824 | tf_op jit(solution)/shard_map/all_gather | solution.py:20
  44.3 6.5 %fusion = f32[512,128]{1,0:T(8,128)} fusion(bf16[4,512,2048]{2,1,0:T(8,128)(2,1)} %param.3, bf16[2048,128]{1,0:T(8,128)(2,1)S(1)} %all_gather.3, f32[4,128]{1,0:T(4,128)} %param.5), kind=kOutput, calls=%fused_computation.1 | convolution fusion | flops 1074200576 | bytes 9177088 | tf_op jit(solution)/shard_map/kij,jr->kir/dot_general | solution.py:17
  50.7 0.0 reduce-scatter.2.cloned.1.call-update
  50.8 86.1 %all-reduce.2.cloned.1.call-done = f32[128,128]{0,1:T(8,128)} async-done(((f32[128,128]{0,1:T(8,128)}), f32[128,128]{0,1:T(8,128)}) %all-reduce.2.cloned.1.call-update) | async-done | bytes 65552 | tf_op jit(solution)/shard_map/psum | solution.py:31
  136.9 0.0 copy-done
  136.9 1.1 convolution_multiply_fusion.1
  138.1 0.1 copy.10
  138.2 11.7 %cholesky.16 = f32[128,128]{1,0:T(8,128)S(1)} custom-call(f32[128,128]{1,0:T(8,128)S(1)} %fusion.7), custom_call_target="Cholesky" | custom-call | tf_op jit(solution)/shard_map/jit(cholesky)/cholesky | solution.py:32
  149.9 0.6 compare_reduce_fusion
  150.6 0.7 fusion.2
  151.2 9.8 %custom-call.10 = f32[1,128,128]{1,2,0:T(8,128)S(1)} custom-call(f32[1,128,128]{2,1,0:T(8,128)S(1)} %fusion.2), custom_call_target="InvertDiagBlocksLowerTriangular" | custom-call | tf_op jit(solution)/shard_map/jit(_cho_solve)/triangular_solve | solution.py:33
  161.0 0.0 reduce-scatter.2.cloned.1.call-done
  161.1 1.1 fusion.5
  162.2 0.3 multiply_reduce_fusion
  162.5 40.9 %psum.15 = f32[128]{0:T(128)S(1)} all-reduce(f32[128]{0:T(128)S(1)} %get-tuple-element.2), channel_id=1, replica_groups=mesh['row'=8,'col'=4] {'row','col'}, use_global_device_ids=true, to_apply=%region_6.7 | all-reduce | flops 128 | bytes 1024 | tf_op jit(solution)/shard_map/psum | solution.py:34
  203.4 0.0 copy-start.1
  203.4 0.6 broadcast_divide_fusion
  204.1 0.0 copy-done.1
  (3 shorter events, 0.1 us)
Async XLA Ops:
  8.0 128.9 %copy-start = (f32[4,128]{1,0:T(4,128)S(1)}, f32[4,128]{1,0:T(4,128)}, u32[]{:S(2)}) copy-start(f32[4,128]{1,0:T(4,128)} %param.5) | copy-start | bytes 6148
  8.0 128.9 %all-reduce.2.cloned.1.call-start = ((), (), s32[]{:S(2)}) async-start(), calls=%async_computation.1 | async-start | bytes 131072 | tf_op jit(solution)/shard_map/psum | solution.py:31
  10.1 151.0 %reduce-scatter.2.cloned.1.call-start = ((), (), s32[]{:S(2)}) async-start(), calls=%async_computation.2 | async-start | bytes 327680 | tf_op jit(solution)/shard_map/reduce_scatter | solution.py:24
  203.4 0.7 copy-start.1
Sparse Core Ops, SparseCore 0:
  15.9 120.9 all-reduce.1
Sparse Core Ops, SparseCore 1:
  50.9 20.9 reduce-scatter.1
where the time goes:
time: 212 us; the launch traced here: 211 us
  waiting for transfers between devices  86.2 us (41%)
  blocking collectives  74.1 us (35%)
  other arithmetic  24.4 us (12%)
  between operations  15.5 us (7%)
  matrix products  11 us (5%)
    psum x1, waiting for transfers between devices, per_device(): gram = lax.psum(own_gram, ('row', 'col'))  86.1 us
    psum x1, blocking collectives, per_device(): squares = lax.psum(jnp.sum(solved * solved, axis=0), ('row', 'col'))  40.9 us
    all_gather x1, blocking collectives, per_device(): lax.all_gather(low_factor, 'row', axis=0, tiled=True)  33.2 us
    another operation x3, other arithmetic, per_device(): lower = jnp.linalg.cholesky(gram * time_gram)  12.4 us
    another operation x2, other arithmetic, per_device(): jax.scipy.linalg.cho_solve((lower, True), local.T)  10.5 us
    dot_general x1, matrix products, per_device(): jnp.einsum('kij,jr->kir', tensor, lax.all_gather(low_factor, 'row', axis=...  6.47 us
  transfers between devices with their start and end apart: 2, of which 1 were waited for; matrix products, arithmetic and copies ran while one was open for 15% of the time, Pallas kernels for 0%

commit v1 on v0

v1 whole, which is shorter than its diff:
```python
import functools

import jax
import jax.numpy as jnp
from jax import lax
from jax.experimental import pallas as pl
from jax.experimental.pallas import tpu as pltpu
from jax.sharding import PartitionSpec as P

F32, BF16 = jnp.float32, jnp.bfloat16
VMEM = pl.BlockSpec(memory_space=pltpu.VMEM)
BLOCK = 16


def tdot(a, b):
    return lax.dot_general(a, b, (((0,), (0,)), ((), ())), preferred_element_type=F32)


def split3(x):
    hi = x.astype(BF16)
    rest = x - hi.astype(F32)
    mid = rest.astype(BF16)
    return hi, mid, (rest - mid.astype(F32)).astype(BF16)


def prepare_kernel(factor_ref, out_ref):
    rows, rank = factor_ref.shape
    factor = factor_ref[...]
    low = factor.astype(BF16)
    residual = (factor - low.astype(F32)).astype(BF16)
    cross = tdot(low, residual)
    rest = cross + cross.T + tdot(residual, residual)
    out_ref[:rows, :] = low
    out_ref[rows:, :] = rest.astype(BF16)


def mttkrp_kernel(owners, tensor_ref, time_ref, *refs):
    parts, (keep_ref, send_ref, low_ref) = refs[: len(owners)], refs[len(owners) :]
    snaps, own_rows, own_cols = tensor_ref.shape
    rank = time_ref.shape[1]
    depth = parts[0].shape[0] - rank
    row, col = lax.axis_index("row"), lax.axis_index("col")
    cols = lax.axis_size("col")
    piece = own_rows // cols
    gram = jnp.zeros((rank, rank), F32)
    for owner, part in zip(owners, parts):
        start = pl.multiple_of(lax.bitwise_xor(row, owner) * depth, depth)
        low_ref[pl.ds(start, depth), :] = part[:depth, :]
        gram = gram + part[depth:, :].astype(F32)
    low = low_ref[...]
    gram = gram + tdot(low, low)
    total = [
        jnp.dot(tensor_ref[snap], low, preferred_element_type=F32) for snap in range(snaps)
    ]
    result = sum(total[snap] * time_ref[snap : snap + 1, :] for snap in range(snaps))
    core = lax.rem(col, 2)
    for pair in range(cols // 2):
        even = result[(2 * pair) * piece : (2 * pair + 1) * piece, :]
        odd = result[(2 * pair + 1) * piece : (2 * pair + 2) * piece, :]
        keep_ref[pair * piece : (pair + 1) * piece, :] = jnp.where(core == 0, even, odd)
        send_ref[pair * piece : (pair + 1) * piece, :] = jnp.where(core == 0, odd, even)
    send_ref[(cols // 2) * piece :, :] = gram


def negative_inverse(matrix):
    size = matrix.shape[0]
    lane = lax.broadcasted_iota(jnp.int32, (BLOCK, size), 1)
    sub = lax.broadcasted_iota(jnp.int32, (BLOCK, size), 0)
    at_row = lax.broadcasted_iota(jnp.int32, (size, size), 0)
    at_col = lax.broadcasted_iota(jnp.int32, (size, size), 1)
    for begin in range(0, size, BLOCK):
        end = begin + BLOCK
        panel = matrix[begin:end, :]
        diag = [
            jnp.broadcast_to(panel[:, begin + j : begin + j + 1], (BLOCK, size))
            for j in range(BLOCK)
        ]
        inside = (lane >= begin) & (lane < end)
        work = jnp.where(inside, jnp.where(lane - begin == sub, -1.0, 0.0), panel)
        solved = jnp.zeros((BLOCK, size), F32)
        for k in range(BLOCK):
            scale = lax.rsqrt(jnp.broadcast_to(diag[k][k : k + 1, :], (BLOCK, size)))
            lower = jnp.where(sub > k, diag[k] * scale, 0.0)
            pivot = jnp.broadcast_to(work[k : k + 1, :], (BLOCK, size)) * scale
            solved = jnp.where(sub == k, pivot, solved)
            work = work - lower * pivot
            for j in range(k + 1, BLOCK):
                diag[j] = diag[j] - lower * (
                    jnp.broadcast_to(diag[j][k : k + 1, :], (BLOCK, size)) * scale
                )
        hi, mid, lo = split3(solved)
        update = tdot(
            jnp.concatenate([hi, hi, mid, mid, hi, lo], 0),
            jnp.concatenate([hi, mid, hi, mid, lo, hi], 0),
        )
        swept = (at_row >= begin) & (at_row < end) | (at_col >= begin) & (at_col < end)
        matrix = jnp.where(swept, 0.0, matrix) - update
    return matrix


def solve_kernel(own_ref, got_ref, time_ref, solved_ref, squares_ref):
    piece = solved_ref.shape[0]
    time = time_ref[...]
    time_gram = lax.dot_general(
        time,
        time,
        (((0,), (0,)), ((), ())),
        precision=lax.Precision.HIGHEST,
        preferred_element_type=F32,
    )
    total = own_ref[...] + sum(got_ref[at] for at in range(got_ref.shape[0]))
    inverse = negative_inverse(total[piece:, :] * time_gram)
    solved = -jnp.dot(
        total[:piece, :],
        inverse,
        precision=lax.Precision.HIGHEST,
        preferred_element_type=F32,
    )
    solved_ref[...] = solved
    squares = jnp.sum(solved * solved, axis=0, keepdims=True)
    squares_ref[...] = jnp.broadcast_to(squares, squares_ref.shape)


def normalize_kernel(total_rows, solved_ref, squares_ref, out_ref, scales_ref):
    mean = jnp.sum(squares_ref[...], axis=0, keepdims=True) / total_rows
    scales = jnp.sqrt(mean + 1e-06)
    scales_ref[...] = scales
    out_ref[...] = solved_ref[...] / scales


def shifted(value, axis, offset, groups):
    return lax.ppermute(value, axis, [(at, at ^ offset) for at in range(groups)])


def per_device(tensor, second_factor, time_factor):
    snaps, own_rows, own_cols = tensor.shape
    depth, rank = second_factor.shape
    rows, cols = lax.axis_size("row"), lax.axis_size("col")
    piece = own_rows // cols
    pairs = cols // 2

    message = pl.pallas_call(
        prepare_kernel,
        out_shape=jax.ShapeDtypeStruct((depth + rank, rank), BF16),
        in_specs=[VMEM],
        out_specs=VMEM,
    )(second_factor)
    owners = tuple(range(rows))
    messages = [message] + [shifted(message, "row", at, rows) for at in owners[1:]]
    keep, send = pl.pallas_call(
        functools.partial(mttkrp_kernel, owners),
        out_shape=(
            jax.ShapeDtypeStruct((pairs * piece, rank), F32),
            jax.ShapeDtypeStruct((pairs * piece + rank, rank), F32),
        ),
        in_specs=[VMEM] * (2 + rows),
        out_specs=(VMEM, VMEM),
        scratch_shapes=[pltpu.VMEM((rows * depth, rank), BF16)],
        compiler_params=pltpu.CompilerParams(vmem_limit_bytes=32 * 2**20),
    )(tensor, time_factor, *messages)

    got = shifted(send, "col", 1, cols)
    part = pairs * piece
    sums = keep + got[:part]
    gram = send[part:] + got[part:]
    place = lax.axis_index("col") // 2
    own = jnp.concatenate([lax.dynamic_slice_in_dim(sums, place * piece, piece, 0), gram], 0)
    others = []
    for offset in range(1, pairs):
        there = lax.bitwise_xor(place, offset)
        out = jnp.concatenate([lax.dynamic_slice_in_dim(sums, there * piece, piece, 0), gram], 0)
        others.append(shifted(out, "col", 2 * offset, cols))
    solved, squares = pl.pallas_call(
        solve_kernel,
        out_shape=(
            jax.ShapeDtypeStruct((piece, rank), F32),
            jax.ShapeDtypeStruct((rows * cols, rank), F32),
        ),
        in_specs=[VMEM] * 3,
        out_specs=(VMEM, VMEM),
    )(own, jnp.stack(others), time_factor)
    squares = lax.all_to_all(squares, ("row", "col"), 0, 0, tiled=True)
    first_factor, scales = pl.pallas_call(
        functools.partial(normalize_kernel, own_rows * rows),
        out_shape=(
            jax.ShapeDtypeStruct((piece, rank), F32),
            jax.ShapeDtypeStruct((1, rank), F32),
        ),
        in_specs=[VMEM] * 2,
        out_specs=(VMEM, VMEM),
    )(solved, squares)
    return first_factor, scales.reshape(rank)


def solution(mesh):
    in_specs = (P(None, "row", "col"), P(("col", "row"), None), P())
    out_specs = (P(("row", "col"), None), P())
    return jax.shard_map(
        per_device, mesh=mesh, in_specs=in_specs, out_specs=out_specs, check_vma=False
    )
```

time: 212 us -> 62.6 us (0.30)
  waiting for transfers between devices: 86.2 us -> 16 us
  blocking collectives: 74.1 us -> 13.7 us
  other arithmetic: 24.4 us -> 0.71 us
  between operations: 15.5 us -> 0.7 us
  starting transfers between devices: 0.08 us -> 14 us
  Pallas kernels: 0 us -> 11.6 us
  matrix products: 11 us -> 0 us
  local copies, waits for them, and re-layouts: 0.1 us -> 5.59 us
    psum x1 -> x0, waiting for transfers between devices: 86.1 us -> none  [per_device(): gram = lax.psum(own_gram, ('row', 'col'))]
    psum x1 -> x0, blocking collectives: 40.9 us -> none  [per_device(): squares = lax.psum(jnp.sum(solved * solved, axis=0), ('row', 'col'))]
    all_gather x1 -> x0, blocking collectives: 33.2 us -> none  [per_device(): lax.all_gather(low_factor, 'row', axis=0, tiled=True)]
    another operation x5 -> x0, other arithmetic: 22.9 us -> none  [the longest x3 12.4 us: per_device(): lower = jnp.linalg.cholesky(gram * time_gram)]
    ppermute x0 -> x9, waiting for transfers between devices: none -> 16 us  [shifted(): lax.ppermute(value, axis, [(at, at ^ offset) for at in range(groups)])]
    ppermute x0 -> x9, starting transfers between devices: none -> 14 us  [shifted(): lax.ppermute(value, axis, [(at, at ^ offset) for at in range(groups)])]
    all_to_all x0 -> x1, blocking collectives: none -> 13.7 us  [per_device(): squares = lax.all_to_all(squares, ('row', 'col'), 0, 0, tiled=True)]
    pallas_call x0 -> x4, Pallas kernels: none -> 11.6 us  [the longest x1 5.75 us: per_device(): pl.pallas_call(solve_kernel, out_shape=(jax.ShapeDtypeStruct((piece, rank...]
  transfers between devices with their start and end apart: 2 -> 9, of which waited for: 1 -> 3; matrix products, arithmetic and copies ran while one was open for 15% -> 0% of each run, Pallas kernels for 0% -> 0%
where the time goes in v1:
time: 62.6 us; the launch traced here: 62.2 us
  waiting for transfers between devices  16 us (26%)
  starting transfers between devices  14 us (22%)
  blocking collectives  13.7 us (22%)
  Pallas kernels  11.6 us (19%)
  local copies, waits for them, and re-layouts  5.59 us (9%)
  other arithmetic  0.71 us (1%)
  between operations  0.7 us (1%)
    ppermute x9, waiting for transfers between devices, shifted(): lax.ppermute(value, axis, [(at, at ^ offset) for at in range(groups)])  16 us
    ppermute x9, starting transfers between devices, shifted(): lax.ppermute(value, axis, [(at, at ^ offset) for at in range(groups)])  14 us
    all_to_all x1, blocking collectives, per_device(): squares = lax.all_to_all(squares, ('row', 'col'), 0, 0, tiled=True)  13.7 us
    pallas_call x1, Pallas kernels, per_device(): pl.pallas_call(solve_kernel, out_shape=(jax.ShapeDtypeStruct((piece, rank...  5.75 us
    unnamed x8, local copies, waits for them, and re-layouts  5.59 us
    pallas_call x1, Pallas kernels, per_device(): pl.pallas_call(functools.partial(mttkrp_kernel, owners), out_shape=(jax.S...  2.54 us
    pallas_call x1, Pallas kernels, per_device(): pl.pallas_call(prepare_kernel, out_shape=jax.ShapeDtypeStruct((depth + ra...  1.83 us
    pallas_call x1, Pallas kernels, per_device(): pl.pallas_call(functools.partial(normalize_kernel, own_rows * rows), out_...  1.5 us
  transfers between devices with their start and end apart: 9, of which 3 were waited for; matrix products, arithmetic and copies ran while one was open for 0% of the time, Pallas kernels for 0%

profile of v1, /device:TPU:0, one launch (start us, length us, event | category | flops | bytes accessed | tf_op | source)
XLA Modules:
  0.0 62.2 jit_solution(10748472260899688284)
XLA Ops:
  0.6 1.8 %shard_map.50.refs_0_ = bf16[384,128]{1,0:T(8,128)(2,1)} custom-call(f32[256,128]{1,0:T(8,128)} %factor_ref.1), custom_call_target="tpu_custom_call" | custom-call | tf_op jit(solution)/shard_map/pallas_call | solution.py:142
  2.5 3.0 %collective-permute-start = (bf16[384,128]{1,0:T(8,128)(2,1)}, bf16[384,128]{1,0:T(8,128)(2,1)S(1)}, u32[]{:S(2)}, u32[]{:S(2)}) collective-permute-start(bf16[384,128]{1,0:T(8,128)(2,1)} %shard_map.50.refs_0_), channel_id=1, source_target_pairs={{0,4},{4,0},{8,12},{12,8},{16,20},{20,16},{24,28},{28,24},{1,5},{5... | collective-permute-start | bytes 294920 | tf_op jit(solution)/shard_map/ppermute | solution.py:132
  5.4 1.6 %collective-permute-start.1 = (bf16[384,128]{1,0:T(8,128)(2,1)}, bf16[384,128]{1,0:T(8,128)(2,1)S(1)}, u32[]{:S(2)}, u32[]{:S(2)}) collective-permute-start(bf16[384,128]{1,0:T(8,128)(2,1)} %shard_map.50.refs_0_), channel_id=1, source_target_pairs={{0,8},{4,12},{8,0},{12,4},{16,24},{20,28},{24,16},{28,20},{1,9},{5... | collective-permute-start | bytes 294920 | tf_op jit(solution)/shard_map/ppermute | solution.py:132
  7.0 0.0 collective-permute-start.2
  7.0 3.0 %collective-permute-start.3 = (bf16[384,128]{1,0:T(8,128)(2,1)}, bf16[384,128]{1,0:T(8,128)(2,1)S(1)}, u32[]{:S(2)}, u32[]{:S(2)}) collective-permute-start(bf16[384,128]{1,0:T(8,128)(2,1)} %shard_map.50.refs_0_), channel_id=1, source_target_pairs={{0,16},{4,20},{8,24},{12,28},{16,0},{20,4},{24,8},{28,12},{1,17},{... | collective-permute-start | bytes 294920 | tf_op jit(solution)/shard_map/ppermute | solution.py:132
  10.0 1.3 %collective-permute-start.4 = (bf16[384,128]{1,0:T(8,128)(2,1)}, bf16[384,128]{1,0:T(8,128)(2,1)S(1)}, u32[]{:S(2)}, u32[]{:S(2)}) collective-permute-start(bf16[384,128]{1,0:T(8,128)(2,1)} %shard_map.50.refs_0_), channel_id=1, source_target_pairs={{0,20},{4,16},{8,28},{12,24},{16,4},{20,0},{24,12},{28,8},{1,21},{... | collective-permute-start | bytes 294920 | tf_op jit(solution)/shard_map/ppermute | solution.py:132
  11.3 0.0 collective-permute-done.refs_1_
  11.3 3.6 %collective-permute-start.5 = (bf16[384,128]{1,0:T(8,128)(2,1)}, bf16[384,128]{1,0:T(8,128)(2,1)S(1)}, u32[]{:S(2)}, u32[]{:S(2)}) collective-permute-start(bf16[384,128]{1,0:T(8,128)(2,1)} %shard_map.50.refs_0_), channel_id=1, source_target_pairs={{0,24},{4,28},{8,16},{12,20},{16,8},{20,12},{24,0},{28,4},{1,25},{... | collective-permute-start | bytes 294920 | tf_op jit(solution)/shard_map/ppermute | solution.py:132
  14.9 0.0 collective-permute-done.1.refs_2_
  14.9 0.0 collective-permute-start.6
  14.9 0.0 collective-permute-done.2.refs_3_
  14.9 0.0 collective-permute-done.3.refs_4_
  14.9 10.5 %collective-permute-done.4.refs_5_ = bf16[384,128]{1,0:T(8,128)(2,1)S(1)} collective-permute-done((bf16[384,128]{1,0:T(8,128)(2,1)}, bf16[384,128]{1,0:T(8,128)(2,1)S(1)}, u32[]{:S(2)}, u32[]{:S(2)}) %collective-permute-start.4) | collective-permute-done | bytes 98336 | tf_op jit(solution)/shard_map/ppermute | solution.py:132
  25.4 0.0 collective-permute-done.5.refs_6_
  25.4 0.0 collective-permute-done.6.refs_7_
  25.4 0.0 copy-start
  25.4 3.4 %copy-done = bf16[4,512,2048]{2,1,0:T(8,128)(2,1)S(1)} copy-done((bf16[4,512,2048]{2,1,0:T(8,128)(2,1)S(1)}, bf16[4,512,2048]{2,1,0:T(8,128)(2,1)}, u32[]{:S(2)}) %copy-start) | copy-done | bytes 8388632
  28.8 0.0 copy-start.1
  28.8 0.9 %copy-done.1 = bf16[384,128]{1,0:T(8,128)(2,1)S(1)} copy-done((bf16[384,128]{1,0:T(8,128)(2,1)S(1)}, bf16[384,128]{1,0:T(8,128)(2,1)}, u32[]{:S(2)}) %copy-start.1) | copy-done | bytes 98328
  29.7 0.0 copy-start.2
  29.7 0.7 %copy-done.2 = f32[4,128]{1,0:T(4,128)S(1)} copy-done((f32[4,128]{1,0:T(4,128)S(1)}, f32[4,128]{1,0:T(4,128)}, u32[]{:S(2)}) %copy-start.2) | copy-done | bytes 2072
  30.4 2.5 %shard_map.51 = (f32[256,128]{1,0:T(8,128)S(1)}, f32[384,128]{1,0:T(8,128)S(1)}) custom-call(bf16[4,512,2048]{2,1,0:T(8,128)(2,1)S(1)} %copy-done, f32[4,128]{1,0:T(4,128)S(1)} %copy-done.2, bf16[384,128]{1,0:T(8,128)(2,1)S(1)} %copy-done.1, bf16[384,128]{1,0:T(8,128)(2,1)S(1)} %collective-permute-done.refs_1_, ...), custom_call_target="tpu_custom_call" | custom-call | tf_op jit(solution)/shard_map/pallas_call | solution.py:150
  32.9 0.1 collective-permute-start.7
  33.0 1.4 %collective-permute-done.7 = f32[384,128]{1,0:T(8,128)S(1)} collective-permute-done((f32[384,128]{1,0:T(8,128)S(1)}, f32[384,128]{1,0:T(8,128)S(1)}, u32[]{:S(2)}, u32[]{:S(2)}) %collective-permute-start.7) | collective-permute-done | bytes 196640 | tf_op jit(solution)/shard_map/ppermute | solution.py:132
  34.5 0.7 %pad_maximum_fusion = (f32[256,128]{1,0:T(8,128)S(1)}, f32[256,128]{1,0:T(8,128)}) fusion(f32[128,128]{1,0:T(8,128)S(1)} %get-tuple-element.18, f32[128,128]{1,0:T(8,128)S(1)} %get-tuple-element.14, f32[128,128]{1,0:T(8,128)S(1)} %get-tuple-element.15), kind=kLoop, calls=%fused_computation | loop fusion | flops 65536 | bytes 458752 | tf_op jit(solution)/shard_map/concatenate | solution.py:171
  35.1 1.5 %collective-permute-start.8 = (f32[256,128]{1,0:T(8,128)S(1)}, f32[256,128]{1,0:T(8,128)S(1)}, u32[]{:S(2)}, u32[]{:S(2)}) collective-permute-start(f32[256,128]{1,0:T(8,128)S(1)} %get-tuple-element.16), channel_id=1, source_target_pairs={{0,2},{1,3},{2,0},{3,1},{4,6},{5,7},{6,4},{7,5},{8,10},{9,11},{10,... | collective-permute-start | bytes 393224 | tf_op jit(solution)/shard_map/ppermute | solution.py:132
  36.6 4.0 %collective-permute-done.8 = f32[256,128]{1,0:T(8,128)S(1)} collective-permute-done((f32[256,128]{1,0:T(8,128)S(1)}, f32[256,128]{1,0:T(8,128)S(1)}, u32[]{:S(2)}, u32[]{:S(2)}) %collective-permute-start.8) | collective-permute-done | bytes 131104 | tf_op jit(solution)/shard_map/ppermute | solution.py:132
  40.7 0.0 copy-start.3
  40.7 0.6 %copy-done.3 = f32[256,128]{1,0:T(8,128)} copy-done((f32[256,128]{1,0:T(8,128)}, f32[256,128]{1,0:T(8,128)S(1)}, u32[]{:S(2)}) %copy-start.3) | copy-done | bytes 131096
  41.3 5.8 %shard_map.52 = (f32[128,128]{1,0:T(8,128)}, f32[32,128]{1,0:T(8,128)}) custom-call(f32[256,128]{1,0:T(8,128)} %get-tuple-element.17.own_ref, f32[1,256,128]{2,1,0:T(8,128)} %bitcast.6, f32[4,128]{1,0:T(4,128)} %time_ref.3), custom_call_target="tpu_custom_call" | custom-call | tf_op jit(solution)/shard_map/pallas_call | solution.py:173
  47.1 13.7 %all_to_all.11 = f32[32,1,128]{2,1,0:T(1,128)} all-to-all(f32[32,1,128]{2,1,0:T(1,128)} %bitcast.8), channel_id=1, replica_groups=mesh['row'=8,'col'=4] {'row','col'}, dimensions={0} | all-to-all | bytes 32768 | tf_op jit(solution)/shard_map/all_to_all | solution.py:182
  60.7 1.5 %shard_map.53 = (f32[128,128]{1,0:T(8,128)}, f32[1,128]{1,0:T(1,128)}) custom-call(f32[128,128]{1,0:T(8,128)} %get-tuple-element.10.solved_ref, f32[32,128]{1,0:T(8,128)} %bitcast.7), custom_call_target="tpu_custom_call" | custom-call | tf_op jit(solution)/shard_map/pallas_call | solution.py:183
  (2 shorter events, 0.0 us)
Async XLA Ops:
  2.5 8.8 %collective-permute-start = (bf16[384,128]{1,0:T(8,128)(2,1)}, bf16[384,128]{1,0:T(8,128)(2,1)S(1)}, u32[]{:S(2)}, u32[]{:S(2)}) collective-permute-start(bf16[384,128]{1,0:T(8,128)(2,1)} %shard_map.50.refs_0_), channel_id=1, source_target_pairs={{0,4},{4,0},{8,12},{12,8},{16,20},{20,16},{24,28},{28,24},{1,5},{5... | collective-permute-start | bytes 294920 | tf_op jit(solution)/shard_map/ppermute | solution.py:132
  5.4 9.5 %collective-permute-start.1 = (bf16[384,128]{1,0:T(8,128)(2,1)}, bf16[384,128]{1,0:T(8,128)(2,1)S(1)}, u32[]{:S(2)}, u32[]{:S(2)}) collective-permute-start(bf16[384,128]{1,0:T(8,128)(2,1)} %shard_map.50.refs_0_), channel_id=1, source_target_pairs={{0,8},{4,12},{8,0},{12,4},{16,24},{20,28},{24,16},{28,20},{1,9},{5... | collective-permute-start | bytes 294920 | tf_op jit(solution)/shard_map/ppermute | solution.py:132
  7.0 7.9 %collective-permute-start.2 = (bf16[384,128]{1,0:T(8,128)(2,1)}, bf16[384,128]{1,0:T(8,128)(2,1)S(1)}, u32[]{:S(2)}, u32[]{:S(2)}) collective-permute-start(bf16[384,128]{1,0:T(8,128)(2,1)} %shard_map.50.refs_0_), channel_id=1, source_target_pairs={{0,12},{4,8},{8,4},{12,0},{16,28},{20,24},{24,20},{28,16},{1,13},{... | collective-permute-start | bytes 294920 | tf_op jit(solution)/shard_map/ppermute | solution.py:132
  7.0 7.9 %collective-permute-start.3 = (bf16[384,128]{1,0:T(8,128)(2,1)}, bf16[384,128]{1,0:T(8,128)(2,1)S(1)}, u32[]{:S(2)}, u32[]{:S(2)}) collective-permute-start(bf16[384,128]{1,0:T(8,128)(2,1)} %shard_map.50.refs_0_), channel_id=1, source_target_pairs={{0,16},{4,20},{8,24},{12,28},{16,0},{20,4},{24,8},{28,12},{1,17},{... | collective-permute-start | bytes 294920 | tf_op jit(solution)/shard_map/ppermute | solution.py:132
  10.0 15.4 %collective-permute-start.4 = (bf16[384,128]{1,0:T(8,128)(2,1)}, bf16[384,128]{1,0:T(8,128)(2,1)S(1)}, u32[]{:S(2)}, u32[]{:S(2)}) collective-permute-start(bf16[384,128]{1,0:T(8,128)(2,1)} %shard_map.50.refs_0_), channel_id=1, source_target_pairs={{0,20},{4,16},{8,28},{12,24},{16,4},{20,0},{24,12},{28,8},{1,21},{... | collective-permute-start | bytes 294920 | tf_op jit(solution)/shard_map/ppermute | solution.py:132
  11.3 14.1 %collective-permute-start.5 = (bf16[384,128]{1,0:T(8,128)(2,1)}, bf16[384,128]{1,0:T(8,128)(2,1)S(1)}, u32[]{:S(2)}, u32[]{:S(2)}) collective-permute-start(bf16[384,128]{1,0:T(8,128)(2,1)} %shard_map.50.refs_0_), channel_id=1, source_target_pairs={{0,24},{4,28},{8,16},{12,20},{16,8},{20,12},{24,0},{28,4},{1,25},{... | collective-permute-start | bytes 294920 | tf_op jit(solution)/shard_map/ppermute | solution.py:132
  14.9 10.5 %collective-permute-start.6 = (bf16[384,128]{1,0:T(8,128)(2,1)}, bf16[384,128]{1,0:T(8,128)(2,1)S(1)}, u32[]{:S(2)}, u32[]{:S(2)}) collective-permute-start(bf16[384,128]{1,0:T(8,128)(2,1)} %shard_map.50.refs_0_), channel_id=1, source_target_pairs={{0,28},{4,24},{8,20},{12,16},{16,12},{20,8},{24,4},{28,0},{1,29},{... | collective-permute-start | bytes 294920 | tf_op jit(solution)/shard_map/ppermute | solution.py:132
  25.4 3.4 %copy-start = (bf16[4,512,2048]{2,1,0:T(8,128)(2,1)S(1)}, bf16[4,512,2048]{2,1,0:T(8,128)(2,1)}, u32[]{:S(2)}) copy-start(bf16[4,512,2048]{2,1,0:T(8,128)(2,1)} %tensor_ref.1) | copy-start | bytes 25165828
  28.8 0.9 %copy-start.1 = (bf16[384,128]{1,0:T(8,128)(2,1)S(1)}, bf16[384,128]{1,0:T(8,128)(2,1)}, u32[]{:S(2)}) copy-start(bf16[384,128]{1,0:T(8,128)(2,1)} %shard_map.50.refs_0_) | copy-start | bytes 294916
  29.7 0.7 %copy-start.2 = (f32[4,128]{1,0:T(4,128)S(1)}, f32[4,128]{1,0:T(4,128)}, u32[]{:S(2)}) copy-start(f32[4,128]{1,0:T(4,128)} %time_ref.3) | copy-start | bytes 6148
  32.9 1.5 %collective-permute-start.7 = (f32[384,128]{1,0:T(8,128)S(1)}, f32[384,128]{1,0:T(8,128)S(1)}, u32[]{:S(2)}, u32[]{:S(2)}) collective-permute-start(f32[384,128]{1,0:T(8,128)S(1)} %get-tuple-element.9), channel_id=1, source_target_pairs={{0,1},{1,0},{2,3},{3,2},{4,5},{5,4},{6,7},{7,6},{8,9},{9,8},{10,11... | collective-permute-start | bytes 589832 | tf_op jit(solution)/shard_map/ppermute | solution.py:132
  35.1 5.5 %collective-permute-start.8 = (f32[256,128]{1,0:T(8,128)S(1)}, f32[256,128]{1,0:T(8,128)S(1)}, u32[]{:S(2)}, u32[]{:S(2)}) collective-permute-start(f32[256,128]{1,0:T(8,128)S(1)} %get-tuple-element.16), channel_id=1, source_target_pairs={{0,2},{1,3},{2,0},{3,1},{4,6},{5,7},{6,4},{7,5},{8,10},{9,11},{10,... | collective-permute-start | bytes 393224 | tf_op jit(solution)/shard_map/ppermute | solution.py:132
  40.7 0.6 %copy-start.3 = (f32[256,128]{1,0:T(8,128)}, f32[256,128]{1,0:T(8,128)S(1)}, u32[]{:S(2)}) copy-start(f32[256,128]{1,0:T(8,128)S(1)} %collective-permute-done.8) | copy-start | bytes 393220

commit v2 on v1

v2 whole, which is shorter than its diff:
```python
import functools

import jax
import jax.numpy as jnp
from jax import lax
from jax.experimental import pallas as pl
from jax.experimental.pallas import tpu as pltpu
from jax.sharding import PartitionSpec as P

F32, BF16 = jnp.float32, jnp.bfloat16
HBM = pl.BlockSpec(memory_space=pltpu.HBM)
VMEM = pl.BlockSpec(memory_space=pltpu.VMEM)
BLOCK = 16


def tdot(a, b):
    return lax.dot_general(a, b, (((0,), (0,)), ((), ())), preferred_element_type=F32)


def split3(x):
    hi = x.astype(BF16)
    rest = x - hi.astype(F32)
    mid = rest.astype(BF16)
    return hi, mid, (rest - mid.astype(F32)).astype(BF16)


def prepare_kernel(factor_ref, out_ref):
    rows, rank = factor_ref.shape
    factor = factor_ref[...]
    low = factor.astype(BF16)
    residual = (factor - low.astype(F32)).astype(BF16)
    cross = tdot(low, residual)
    rest = cross + cross.T + tdot(residual, residual)
    out_ref[:rows, :] = low
    out_ref[rows:, :] = rest.astype(BF16)


def load_kernel(owners, depth, tensor_ref, time_ref, gate_ref, slots_ref, time_out_ref, gram_ref, sems):
    del gate_ref
    row = lax.axis_index("row")
    copies = [pltpu.make_async_copy(time_ref, time_out_ref, sems.at[len(owners)])]
    for at, owner in enumerate(owners):
        start = pl.multiple_of(lax.bitwise_xor(row, owner) * depth, depth)
        copies.append(
            pltpu.make_async_copy(
                tensor_ref.at[:, :, pl.ds(start, depth)], slots_ref.at[at], sems.at[at]
            )
        )
    for copy in copies:
        copy.start()
    copies[0].wait()
    time = time_out_ref[...]
    gram_ref[...] = lax.dot_general(
        time,
        time,
        (((0,), (0,)), ((), ())),
        precision=lax.Precision.HIGHEST,
        preferred_element_type=F32,
    )
    for copy in copies[1:]:
        copy.wait()


def multiply(slots, slots_ref, time_ref, parts):
    snaps, own_rows, depth = slots_ref.shape[1:]
    rank = time_ref.shape[1]
    gram = jnp.zeros((rank, rank), F32)
    total = [jnp.zeros((own_rows, rank), F32) for _ in range(snaps)]
    for at, part in zip(slots, parts):
        low = part[:depth, :]
        gram = gram + tdot(low, low) + part[depth:, :].astype(F32)
        for snap in range(snaps):
            total[snap] = total[snap] + jnp.dot(
                slots_ref[at, snap], low, preferred_element_type=F32
            )
    return sum(total[snap] * time_ref[snap : snap + 1, :] for snap in range(snaps)), gram


def first_kernel(slots, slots_ref, time_ref, *refs):
    parts, (result_ref, gram_ref) = refs[:-2], refs[-2:]
    result_ref[...], gram_ref[...] = multiply(slots, slots_ref, time_ref, parts)


def last_kernel(slots, slots_ref, time_ref, result_ref, gram_ref, *refs):
    parts, (keep_ref, send_ref) = refs[:-2], refs[-2:]
    col, cols = lax.axis_index("col"), lax.axis_size("col")
    result, gram = result_ref[...], gram_ref[...]
    if parts:
        more, more_gram = multiply(slots, slots_ref, time_ref, parts)
        result, gram = result + more, gram + more_gram
    piece = result.shape[0] // cols
    core = lax.rem(col, 2)
    for pair in range(cols // 2):
        even = result[(2 * pair) * piece : (2 * pair + 1) * piece, :]
        odd = result[(2 * pair + 1) * piece : (2 * pair + 2) * piece, :]
        keep_ref[pair * piece : (pair + 1) * piece, :] = jnp.where(core == 0, even, odd)
        send_ref[pair * piece : (pair + 1) * piece, :] = jnp.where(core == 0, odd, even)
    send_ref[(cols // 2) * piece :, :] = gram


def chip_kernel(piece, keep_ref, sent_ref, got_ref, own_ref, *out_refs):
    place = lax.div(lax.axis_index("col"), 2)
    held = keep_ref.shape[0]
    gram = sent_ref[held:, :] + got_ref[held:, :]
    for offset, out_ref in enumerate((own_ref,) + out_refs):
        start = pl.multiple_of(lax.bitwise_xor(place, offset) * piece, piece)
        out_ref[:piece, :] = keep_ref[pl.ds(start, piece), :] + got_ref[pl.ds(start, piece), :]
        out_ref[piece:, :] = gram


def negative_inverse(matrix):
    size = matrix.shape[0]
    lane = lax.broadcasted_iota(jnp.int32, (BLOCK, size), 1)
    sub = lax.broadcasted_iota(jnp.int32, (BLOCK, size), 0)
    at_row = lax.broadcasted_iota(jnp.int32, (size, size), 0)
    at_col = lax.broadcasted_iota(jnp.int32, (size, size), 1)
    for begin in range(0, size, BLOCK):
        end = begin + BLOCK
        panel = matrix[begin:end, :]
        diag = [
            jnp.broadcast_to(panel[:, begin + j : begin + j + 1], (BLOCK, size))
            for j in range(BLOCK)
        ]
        inside = (lane >= begin) & (lane < end)
        work = jnp.where(inside, jnp.where(lane - begin == sub, -1.0, 0.0), panel)
        solved = jnp.zeros((BLOCK, size), F32)
        for k in range(BLOCK):
            scale = lax.rsqrt(jnp.broadcast_to(diag[k][k : k + 1, :], (BLOCK, size)))
            lower = jnp.where(sub > k, diag[k] * scale, 0.0)
            pivot = jnp.broadcast_to(work[k : k + 1, :], (BLOCK, size)) * scale
            solved = jnp.where(sub == k, pivot, solved)
            work = work - lower * pivot
            for j in range(k + 1, BLOCK):
                diag[j] = diag[j] - lower * (
                    jnp.broadcast_to(diag[j][k : k + 1, :], (BLOCK, size)) * scale
                )
        hi, mid, lo = split3(solved)
        update = tdot(
            jnp.concatenate([hi, hi, mid, mid, hi, lo], 0),
            jnp.concatenate([hi, mid, hi, mid, lo, hi], 0),
        )
        swept = (at_row >= begin) & (at_row < end) | (at_col >= begin) & (at_col < end)
        matrix = jnp.where(swept, 0.0, matrix) - update
    return matrix


def solve_kernel(time_gram_ref, own_ref, *refs):
    others, (solved_ref, squares_ref) = refs[:-2], refs[-2:]
    piece = solved_ref.shape[0]
    total = own_ref[...] + sum(other[...] for other in others)
    inverse = negative_inverse(total[piece:, :] * time_gram_ref[...])
    solved = -jnp.dot(
        total[:piece, :],
        inverse,
        precision=lax.Precision.HIGHEST,
        preferred_element_type=F32,
    )
    solved_ref[...] = solved
    squares = jnp.sum(solved * solved, axis=0, keepdims=True)
    squares_ref[...] = jnp.broadcast_to(squares, squares_ref.shape)


def shifted(value, axis, offset, groups):
    return lax.ppermute(value, axis, [(at, at ^ offset) for at in range(groups)])


def call(kernel, operands, in_specs, outs, scratch=()):
    return pl.pallas_call(
        kernel,
        out_shape=tuple(jax.ShapeDtypeStruct(shape, dtype) for shape, dtype in outs),
        in_specs=in_specs,
        out_specs=(VMEM,) * len(outs),
        scratch_shapes=scratch,
        compiler_params=pltpu.CompilerParams(vmem_limit_bytes=40 * 2**20),
    )(*operands)


def per_device(tensor, second_factor, time_factor):
    snaps, own_rows, own_cols = tensor.shape
    depth, rank = second_factor.shape
    rows, cols = lax.axis_size("row"), lax.axis_size("col")
    piece = own_rows // cols
    pairs = cols // 2

    (message,) = call(prepare_kernel, (second_factor,), [VMEM], [((depth + rank, rank), BF16)])
    arrived = {0: message}
    forwarded = [at for at in range(rows) if at % 2 == 1 and 2 * (at - 1) >= rows and at > 1]
    for at in range(1, rows):
        if at not in forwarded:
            arrived[at] = shifted(message, "row", at, rows)
    for at in forwarded:
        arrived[at] = shifted(arrived[at - 1], "row", 1, rows)

    early = [at for at in range(rows) if at not in forwarded]
    if depth % 128 == 0:
        owners, width = early + forwarded, depth
        first, last = [arrived[at] for at in early], [arrived[at] for at in forwarded]
    else:
        owners, width = [0], own_cols
        row = lax.axis_index("row")
        by_row = jnp.stack([arrived[at] for at in range(rows)])
        by_row = by_row[jnp.arange(rows) ^ row]
        rest = jnp.sum(by_row[:, depth:, :].astype(F32), axis=0).astype(BF16)
        low = by_row[:, :depth, :].reshape(rows * depth, rank)
        first, last = [jnp.concatenate([low, rest], 0)], []
    slots, time, time_gram = call(
        functools.partial(load_kernel, owners, width),
        (tensor, time_factor, arrived[rows // 2]),
        [HBM, HBM, VMEM],
        [((len(owners), snaps, own_rows, width), BF16), ((snaps, rank), F32), ((rank, rank), F32)],
        [pltpu.SemaphoreType.DMA((len(owners) + 1,))],
    )
    result, gram = call(
        functools.partial(first_kernel, range(len(first))),
        (slots, time, *first),
        [VMEM] * (2 + len(first)),
        [((own_rows, rank), F32), ((rank, rank), F32)],
    )
    keep, send = call(
        functools.partial(last_kernel, range(len(first), len(owners))),
        (slots, time, result, gram, *last),
        [VMEM] * (4 + len(last)),
        [((pairs * piece, rank), F32), ((pairs * piece + rank, rank), F32)],
    )

    own, *outs = call(
        functools.partial(chip_kernel, piece),
        (keep, send, shifted(send, "col", 1, cols)),
        [VMEM] * 3,
        [((piece + rank, rank), F32)] * pairs,
    )
    others = [shifted(out, "col", 2 * (at + 1), cols) for at, out in enumerate(outs)]
    solved, squares = call(
        solve_kernel,
        (time_gram, own, *others),
        [VMEM] * (1 + pairs),
        [((piece, rank), F32), ((rows * cols, rank), F32)],
    )
    squares = lax.all_to_all(squares, ("row", "col"), 0, 0, tiled=True)
    scales = jnp.sqrt(jnp.sum(squares, axis=0) / (own_rows * rows) + 1e-06)
    return solved / scales[None, :], scales


def solution(mesh):
    in_specs = (P(None, "row", "col"), P(("col", "row"), None), P())
    out_specs = (P(("row", "col"), None), P())
    return jax.shard_map(
        per_device, mesh=mesh, in_specs=in_specs, out_specs=out_specs, check_vma=False
    )
```

time: 62.6 us -> 46.9 us (0.75)
  waiting for transfers between devices: 16 us -> 8.27 us
  local copies, waits for them, and re-layouts: 5.59 us -> 1.58 us
  blocking collectives: 13.7 us -> 12.1 us
  starting transfers between devices: 14 us -> 12.8 us
  Pallas kernels: 11.6 us -> 10.5 us
    ppermute x9, waiting for transfers between devices: 16 us -> 8.27 us  [shifted(): lax.ppermute(value, axis, [(at, at ^ offset) for at in range(groups)])]
    unnamed x8 -> x6, local copies, waits for them, and re-layouts: 5.59 us -> 1.58 us
    all_to_all x1, blocking collectives: 13.7 us -> 12.1 us  [per_device(): squares = lax.all_to_all(squares, ('row', 'col'), 0, 0, tiled=True)]
    ppermute x9, starting transfers between devices: 14 us -> 12.8 us  [shifted(): lax.ppermute(value, axis, [(at, at ^ offset) for at in range(groups)])]
    pallas_call x4 -> x6, Pallas kernels: 11.6 us -> 10.5 us  [call(): pl.pallas_call(kernel, out_shape=tuple((jax.ShapeDtypeStruct(shape, dtype...]
    concatenate x1 -> x0, other arithmetic: 0.67 us -> none  [per_device(): jnp.concatenate([lax.dynamic_slice_in_dim(sums, there * piece, piece, 0),...]
    div x0 -> x1, other arithmetic: none -> 0.64 us  [per_device(): return (solved / scales[None, :], scales)]
  transfers between devices with their start and end apart: 9 -> 9, of which waited for: 3 -> 3; matrix products, arithmetic and copies ran while one was open for 0% -> 0% of each run, Pallas kernels for 0% -> 12%
where the time goes in v2:
time: 46.9 us; the launch traced here: 46.7 us
  starting transfers between devices  12.8 us (27%)
  blocking collectives  12.1 us (26%)
  Pallas kernels  10.5 us (22%)
  waiting for transfers between devices  8.27 us (18%)
  local copies, waits for them, and re-layouts  1.58 us (3%)
  between operations  0.73 us (2%)
  other arithmetic  0.7 us (1%)
    ppermute x9, starting transfers between devices, shifted(): lax.ppermute(value, axis, [(at, at ^ offset) for at in range(groups)])  12.8 us
    all_to_all x1, blocking collectives, per_device(): squares = lax.all_to_all(squares, ('row', 'col'), 0, 0, tiled=True)  12.1 us
    pallas_call x6, Pallas kernels, call(): pl.pallas_call(kernel, out_shape=tuple((jax.ShapeDtypeStruct(shape, dtype...  10.5 us
    ppermute x9, waiting for transfers between devices, shifted(): lax.ppermute(value, axis, [(at, at ^ offset) for at in range(groups)])  8.27 us
    unnamed x6, local copies, waits for them, and re-layouts  1.58 us
  transfers between devices with their start and end apart: 9, of which 3 were waited for; matrix products, arithmetic and copies ran while one was open for 0% of the time, Pallas kernels for 12%

profile of v2, /device:TPU:0, one launch (start us, length us, event | category | flops | bytes accessed | tf_op | source)
XLA Modules:
  0.0 46.7 jit_solution(5717613934186108195)
XLA Ops:
  0.6 0.0 copy-start
  0.6 0.9 %copy-done = f32[256,128]{1,0:T(8,128)S(1)} copy-done((f32[256,128]{1,0:T(8,128)S(1)}, f32[256,128]{1,0:T(8,128)}, u32[]{:S(2)}) %copy-start) | copy-done | bytes 131096
  1.5 0.3 shard_map.50.refs_0_
  1.8 4.1 %collective-permute-start = (bf16[384,128]{1,0:T(8,128)(2,1)S(1)}, bf16[384,128]{1,0:T(8,128)(2,1)S(1)}, u32[]{:S(2)}, u32[]{:S(2)}) collective-permute-start(bf16[384,128]{1,0:T(8,128)(2,1)S(1)} %shard_map.50.refs_0_), channel_id=1, source_target_pairs={{0,16},{4,20},{8,24},{12,28},{16,0},{20,4},{24,8},{28,12},{1,17},{... | collective-permute-start | bytes 294920 | tf_op jit(solution)/shard_map/ppermute | solution.py:164
  5.9 1.3 %collective-permute-start.4 = (bf16[384,128]{1,0:T(8,128)(2,1)S(1)}, bf16[384,128]{1,0:T(8,128)(2,1)S(1)}, u32[]{:S(2)}, u32[]{:S(2)}) collective-permute-start(bf16[384,128]{1,0:T(8,128)(2,1)S(1)} %shard_map.50.refs_0_), channel_id=1, source_target_pairs={{0,24},{4,28},{8,16},{12,20},{16,8},{20,12},{24,0},{28,4},{1,25},{... | collective-permute-start | bytes 294920 | tf_op jit(solution)/shard_map/ppermute | solution.py:164
  7.3 1.5 %collective-permute-start.1 = (bf16[384,128]{1,0:T(8,128)(2,1)S(1)}, bf16[384,128]{1,0:T(8,128)(2,1)S(1)}, u32[]{:S(2)}, u32[]{:S(2)}) collective-permute-start(bf16[384,128]{1,0:T(8,128)(2,1)S(1)} %shard_map.50.refs_0_), channel_id=1, source_target_pairs={{0,4},{4,0},{8,12},{12,8},{16,20},{20,16},{24,28},{28,24},{1,5},{5... | collective-permute-start | bytes 294920 | tf_op jit(solution)/shard_map/ppermute | solution.py:164
  8.8 0.2 collective-permute-start.2
  9.0 1.7 %collective-permute-start.3 = (bf16[384,128]{1,0:T(8,128)(2,1)S(1)}, bf16[384,128]{1,0:T(8,128)(2,1)S(1)}, u32[]{:S(2)}, u32[]{:S(2)}) collective-permute-start(bf16[384,128]{1,0:T(8,128)(2,1)S(1)} %shard_map.50.refs_0_), channel_id=1, source_target_pairs={{0,12},{4,8},{8,4},{12,0},{16,28},{20,24},{24,20},{28,16},{1,13},{... | collective-permute-start | bytes 294920 | tf_op jit(solution)/shard_map/ppermute | solution.py:164
  10.8 3.0 %collective-permute-done.gate_ref.refs_4_ = bf16[384,128]{1,0:T(8,128)(2,1)S(1)} collective-permute-done((bf16[384,128]{1,0:T(8,128)(2,1)S(1)}, bf16[384,128]{1,0:T(8,128)(2,1)S(1)}, u32[]{:S(2)}, u32[]{:S(2)}) %collective-permute-start) | collective-permute-done | bytes 98336 | tf_op jit(solution)/shard_map/ppermute | solution.py:164
  13.8 1.8 %collective-permute-start.5 = (bf16[384,128]{1,0:T(8,128)(2,1)S(1)}, bf16[384,128]{1,0:T(8,128)(2,1)S(1)}, u32[]{:S(2)}, u32[]{:S(2)}) collective-permute-start(bf16[384,128]{1,0:T(8,128)(2,1)S(1)} %collective-permute-done.gate_ref.refs_4_), channel_id=1, source_target_pairs={{0,4},{4,0},{8,12},{12,8},{16,20},{20,16},{24,28},{28,24},{1,5},{5... | collective-permute-start | bytes 294920 | tf_op jit(solution)/shard_map/ppermute | solution.py:164
  15.5 0.0 collective-permute-done.4.refs_5_
  15.5 0.3 collective-permute-start.6
  15.8 0.0 copy-start.1
  15.8 0.7 %copy-done.1 = f32[4,128]{1,0:T(4,128)S(1)} copy-done((f32[4,128]{1,0:T(4,128)S(1)}, f32[4,128]{1,0:T(4,128)}, u32[]{:S(2)}) %copy-start.1) | copy-done | bytes 2072
  16.5 3.6 %shard_map.51 = (bf16[8,4,512,256]{3,2,1,0:T(8,128)(2,1)S(1)}, f32[4,128]{1,0:T(4,128)S(1)}, f32[128,128]{1,0:T(8,128)S(1)}) custom-call(bf16[4,512,2048]{2,1,0:T(8,128)(2,1)} %tensor_ref.1, f32[4,128]{1,0:T(4,128)S(1)} %copy-done.1, bf16[384,128]{1,0:T(8,128)(2,1)S(1)} %collective-permute-done.gate_ref.refs_4_), custom_call_target="tpu_custom_call" | custom-call | tf_op jit(solution)/shard_map/pallas_call | solution.py:168
  20.1 0.0 collective-permute-done.1.refs_1_
  20.1 0.0 collective-permute-done.2.refs_2_
  20.1 0.0 collective-permute-done.3.refs_3_
  20.1 1.9 %shard_map.52 = (f32[512,128]{1,0:T(8,128)S(1)}, f32[128,128]{1,0:T(8,128)S(1)}) custom-call(bf16[8,4,512,256]{3,2,1,0:T(8,128)(2,1)S(1)} %get-tuple-element.14.slots_ref, f32[4,128]{1,0:T(4,128)S(1)} %get-tuple-element.15.time_ref, bf16[384,128]{1,0:T(8,128)(2,1)S(1)} %shard_map.50.refs_0_, bf16[384,128]{1,0:T(8,128)(2,1)S(1)} %collective-permute-done.1.refs_1_, ...), custom_call_target="tpu_custom_call" | custom-call | tf_op jit(solution)/shard_map/pallas_call | solution.py:168
  22.0 0.0 collective-permute-done.5.refs_0_
  22.1 0.0 collective-permute-done.6.refs_1_
  22.1 0.8 %shard_map.53 = (f32[256,128]{1,0:T(8,128)S(1)}, f32[384,128]{1,0:T(8,128)S(1)}) custom-call(bf16[8,4,512,256]{3,2,1,0:T(8,128)(2,1)S(1)} %get-tuple-element.14.slots_ref, f32[4,128]{1,0:T(4,128)S(1)} %get-tuple-element.15.time_ref, f32[512,128]{1,0:T(8,128)S(1)} %get-tuple-element.16.result_ref, f32[128,128]{1,0:T(8,128)S(1)} %get-tuple-element.17.gram_ref, ...), custom_call_target="tpu_custom_call" | custom-call | tf_op jit(solution)/shard_map/pallas_call | solution.py:168
  22.9 0.1 collective-permute-start.7
  22.9 1.4 %collective-permute-done.7.got_ref = f32[384,128]{1,0:T(8,128)S(1)} collective-permute-done((f32[384,128]{1,0:T(8,128)S(1)}, f32[384,128]{1,0:T(8,128)S(1)}, u32[]{:S(2)}, u32[]{:S(2)}) %collective-permute-start.7) | collective-permute-done | bytes 196640 | tf_op jit(solution)/shard_map/ppermute | solution.py:164
  24.4 1.8 %collective-permute-start.8 = (f32[256,128]{1,0:T(8,128)S(1)}, f32[256,128]{1,0:T(8,128)S(1)}, u32[]{:S(2)}, u32[]{:S(2)}) collective-permute-start(f32[256,128]{1,0:T(8,128)S(1)} %get-tuple-element.21), channel_id=1, source_target_pairs={{0,2},{1,3},{2,0},{3,1},{4,6},{5,7},{6,4},{7,5},{8,10},{9,11},{10,... | collective-permute-start | bytes 393224 | tf_op jit(solution)/shard_map/ppermute | solution.py:164
  26.2 3.8 %collective-permute-done.8.refs_0_ = f32[256,128]{1,0:T(8,128)S(1)} collective-permute-done((f32[256,128]{1,0:T(8,128)S(1)}, f32[256,128]{1,0:T(8,128)S(1)}, u32[]{:S(2)}, u32[]{:S(2)}) %collective-permute-start.8) | collective-permute-done | bytes 131104 | tf_op jit(solution)/shard_map/ppermute | solution.py:164
  30.0 3.9 %shard_map.55 = (f32[128,128]{1,0:T(8,128)S(1)}, f32[32,128]{1,0:T(8,128)S(1)}) custom-call(f32[128,128]{1,0:T(8,128)S(1)} %get-tuple-element.13.time_gram_ref, f32[256,128]{1,0:T(8,128)S(1)} %get-tuple-element.20.own_ref, f32[256,128]{1,0:T(8,128)S(1)} %collective-permute-done.8.refs_0_), custom_call_target="tpu_custom_call" | custom-call | tf_op jit(solution)/shard_map/pallas_call | solution.py:168
  33.9 12.1 %all_to_all.9 = f32[32,1,128]{2,1,0:T(1,128)S(1)} all-to-all(f32[32,1,128]{2,1,0:T(1,128)S(1)} %bitcast.3), channel_id=1, replica_groups=mesh['row'=8,'col'=4] {'row','col'}, dimensions={0} | all-to-all | bytes 32768 | tf_op jit(solution)/shard_map/all_to_all | solution.py:239
  46.0 0.1 reduce_sum.9
  46.0 0.0 copy-start.2
  46.1 0.6 %broadcast_divide_fusion = f32[128,128]{1,0:T(8,128)} fusion(f32[128,128]{1,0:T(8,128)S(1)} %get-tuple-element.22, f32[128]{0:T(128)S(1)} %add_sqrt_fusion), kind=kLoop, calls=%fused_computation | loop fusion | flops 16384 | bytes 131584 | tf_op jit(solution)/shard_map/div | solution.py:241
  46.7 0.0 copy-done.2
  (2 shorter events, 0.0 us)
Async XLA Ops:
  0.6 0.9 %copy-start = (f32[256,128]{1,0:T(8,128)S(1)}, f32[256,128]{1,0:T(8,128)}, u32[]{:S(2)}) copy-start(f32[256,128]{1,0:T(8,128)} %factor_ref.1) | copy-start | bytes 393220
  1.8 11.9 %collective-permute-start = (bf16[384,128]{1,0:T(8,128)(2,1)S(1)}, bf16[384,128]{1,0:T(8,128)(2,1)S(1)}, u32[]{:S(2)}, u32[]{:S(2)}) collective-permute-start(bf16[384,128]{1,0:T(8,128)(2,1)S(1)} %shard_map.50.refs_0_), channel_id=1, source_target_pairs={{0,16},{4,20},{8,24},{12,28},{16,0},{20,4},{24,8},{28,12},{1,17},{... | collective-permute-start | bytes 294920 | tf_op jit(solution)/shard_map/ppermute | solution.py:164
  5.9 9.6 %collective-permute-start.4 = (bf16[384,128]{1,0:T(8,128)(2,1)S(1)}, bf16[384,128]{1,0:T(8,128)(2,1)S(1)}, u32[]{:S(2)}, u32[]{:S(2)}) collective-permute-start(bf16[384,128]{1,0:T(8,128)(2,1)S(1)} %shard_map.50.refs_0_), channel_id=1, source_target_pairs={{0,24},{4,28},{8,16},{12,20},{16,8},{20,12},{24,0},{28,4},{1,25},{... | collective-permute-start | bytes 294920 | tf_op jit(solution)/shard_map/ppermute | solution.py:164
  7.3 12.8 %collective-permute-start.1 = (bf16[384,128]{1,0:T(8,128)(2,1)S(1)}, bf16[384,128]{1,0:T(8,128)(2,1)S(1)}, u32[]{:S(2)}, u32[]{:S(2)}) collective-permute-start(bf16[384,128]{1,0:T(8,128)(2,1)S(1)} %shard_map.50.refs_0_), channel_id=1, source_target_pairs={{0,4},{4,0},{8,12},{12,8},{16,20},{20,16},{24,28},{28,24},{1,5},{5... | collective-permute-start | bytes 294920 | tf_op jit(solution)/shard_map/ppermute | solution.py:164
  8.8 11.3 %collective-permute-start.2 = (bf16[384,128]{1,0:T(8,128)(2,1)S(1)}, bf16[384,128]{1,0:T(8,128)(2,1)S(1)}, u32[]{:S(2)}, u32[]{:S(2)}) collective-permute-start(bf16[384,128]{1,0:T(8,128)(2,1)S(1)} %shard_map.50.refs_0_), channel_id=1, source_target_pairs={{0,8},{4,12},{8,0},{12,4},{16,24},{20,28},{24,16},{28,20},{1,9},{5... | collective-permute-start | bytes 294920 | tf_op jit(solution)/shard_map/ppermute | solution.py:164
  9.0 11.1 %collective-permute-start.3 = (bf16[384,128]{1,0:T(8,128)(2,1)S(1)}, bf16[384,128]{1,0:T(8,128)(2,1)S(1)}, u32[]{:S(2)}, u32[]{:S(2)}) collective-permute-start(bf16[384,128]{1,0:T(8,128)(2,1)S(1)} %shard_map.50.refs_0_), channel_id=1, source_target_pairs={{0,12},{4,8},{8,4},{12,0},{16,28},{20,24},{24,20},{28,16},{1,13},{... | collective-permute-start | bytes 294920 | tf_op jit(solution)/shard_map/ppermute | solution.py:164
  13.8 8.3 %collective-permute-start.5 = (bf16[384,128]{1,0:T(8,128)(2,1)S(1)}, bf16[384,128]{1,0:T(8,128)(2,1)S(1)}, u32[]{:S(2)}, u32[]{:S(2)}) collective-permute-start(bf16[384,128]{1,0:T(8,128)(2,1)S(1)} %collective-permute-done.gate_ref.refs_4_), channel_id=1, source_target_pairs={{0,4},{4,0},{8,12},{12,8},{16,20},{20,16},{24,28},{28,24},{1,5},{5... | collective-permute-start | bytes 294920 | tf_op jit(solution)/shard_map/ppermute | solution.py:164
  15.5 6.5 %collective-permute-start.6 = (bf16[384,128]{1,0:T(8,128)(2,1)S(1)}, bf16[384,128]{1,0:T(8,128)(2,1)S(1)}, u32[]{:S(2)}, u32[]{:S(2)}) collective-permute-start(bf16[384,128]{1,0:T(8,128)(2,1)S(1)} %collective-permute-done.4.refs_5_), channel_id=1, source_target_pairs={{0,4},{4,0},{8,12},{12,8},{16,20},{20,16},{24,28},{28,24},{1,5},{5... | collective-permute-start | bytes 294920 | tf_op jit(solution)/shard_map/ppermute | solution.py:164
  15.8 0.7 %copy-start.1 = (f32[4,128]{1,0:T(4,128)S(1)}, f32[4,128]{1,0:T(4,128)}, u32[]{:S(2)}) copy-start(f32[4,128]{1,0:T(4,128)} %time_ref.1) | copy-start | bytes 6148
  22.9 1.5 %collective-permute-start.7 = (f32[384,128]{1,0:T(8,128)S(1)}, f32[384,128]{1,0:T(8,128)S(1)}, u32[]{:S(2)}, u32[]{:S(2)}) collective-permute-start(f32[384,128]{1,0:T(8,128)S(1)} %get-tuple-element.19.sent_ref), channel_id=1, source_target_pairs={{0,1},{1,0},{2,3},{3,2},{4,5},{5,4},{6,7},{7,6},{8,9},{9,8},{10,11... | collective-permute-start | bytes 589832 | tf_op jit(solution)/shard_map/ppermute | solution.py:164
  24.4 5.6 %collective-permute-start.8 = (f32[256,128]{1,0:T(8,128)S(1)}, f32[256,128]{1,0:T(8,128)S(1)}, u32[]{:S(2)}, u32[]{:S(2)}) collective-permute-start(f32[256,128]{1,0:T(8,128)S(1)} %get-tuple-element.21), channel_id=1, source_target_pairs={{0,2},{1,3},{2,0},{3,1},{4,6},{5,7},{6,4},{7,5},{8,10},{9,11},{10,... | collective-permute-start | bytes 393224 | tf_op jit(solution)/shard_map/ppermute | solution.py:164
  46.0 0.7 %copy-start.2 = (f32[128]{0:T(128)}, f32[128]{0:T(128)S(1)}, u32[]{:S(2)}) copy-start(f32[128]{0:T(128)S(1)} %add_sqrt_fusion) | copy-start | bytes 1540

commit v3 on v2

v3 whole, which is shorter than its diff:
```python
import functools

import jax
import jax.numpy as jnp
from jax import lax
from jax.experimental import pallas as pl
from jax.experimental.pallas import tpu as pltpu
from jax.sharding import PartitionSpec as P

F32, BF16 = jnp.float32, jnp.bfloat16
HBM = pl.BlockSpec(memory_space=pltpu.HBM)
VMEM = pl.BlockSpec(memory_space=pltpu.VMEM)
TILE, STRIP, BLOCK = 8, 16, 32


def tdot(a, b):
    return lax.dot_general(a, b, (((0,), (0,)), ((), ())), preferred_element_type=F32)


def split3(x):
    hi = x.astype(BF16)
    rest = x - hi.astype(F32)
    mid = rest.astype(BF16)
    return hi, mid, (rest - mid.astype(F32)).astype(BF16)


def prepare_kernel(factor_ref, out_ref, own_ref):
    rows, rank = factor_ref.shape
    factor = factor_ref[...]
    low = factor.astype(BF16)
    residual = (factor - low.astype(F32)).astype(BF16)
    cross = tdot(low, residual)
    rest = cross + cross.T + tdot(residual, residual)
    for ref in (out_ref, own_ref):
        ref[:rows, :] = low
        ref[rows:, :] = rest.astype(BF16)


def load_kernel(owners, depth, tensor_ref, time_ref, slots_ref, time_out_ref, gram_ref, sems):
    row = lax.axis_index("row")
    copies = [pltpu.make_async_copy(time_ref, time_out_ref, sems.at[len(owners)])]
    for at, owner in enumerate(owners):
        start = pl.multiple_of(lax.bitwise_xor(row, owner) * depth, depth)
        copies.append(
            pltpu.make_async_copy(
                tensor_ref.at[:, :, pl.ds(start, depth)], slots_ref.at[at], sems.at[at]
            )
        )
    for copy in copies:
        copy.start()
    copies[0].wait()
    time = time_out_ref[...]
    gram_ref[...] = lax.dot_general(
        time,
        time,
        (((0,), (0,)), ((), ())),
        precision=lax.Precision.HIGHEST,
        preferred_element_type=F32,
    )
    for copy in copies[1:]:
        copy.wait()


def relay_kernel(loaded_ref, *refs):
    del loaded_ref
    parts, out_ref = refs[:-1], refs[-1]
    depth = parts[0].shape[0] - parts[0].shape[1]
    out_ref[:depth, :] = parts[0][:depth, :]
    if len(parts) > 1:
        rest = sum(part[depth:, :].astype(F32) for part in parts)
        out_ref[depth:, :] = rest.astype(BF16)


def gram_of(parts, depth):
    gram = 0.0
    for part in parts:
        low = part[:depth, :]
        gram = gram + tdot(low, low)
        if part.shape[0] > depth:
            gram = gram + part[depth:, :].astype(F32)
    return gram


def multiply(slots, slots_ref, time_ref, parts):
    snaps, own_rows, depth = slots_ref.shape[1:]
    rank = time_ref.shape[1]
    total = [jnp.zeros((own_rows, rank), F32) for _ in range(snaps)]
    for at, part in zip(slots, parts):
        low = part[:depth, :]
        for snap in range(snaps):
            total[snap] = total[snap] + jnp.dot(
                slots_ref[at, snap], low, preferred_element_type=F32
            )
    return sum(total[snap] * time_ref[snap : snap + 1, :] for snap in range(snaps))


def first_kernel(slots, slots_ref, time_ref, *refs):
    parts, (result_ref, gram_ref) = refs[:-2], refs[-2:]
    result_ref[...] = multiply(slots, slots_ref, time_ref, parts)
    gram_ref[...] = gram_of(parts, slots_ref.shape[-1])


def last_kernel(slots, slots_ref, time_ref, result_ref, gram_ref, *refs):
    parts, (keep_ref, send_ref) = refs[:-2], refs[-2:]
    col, cols = lax.axis_index("col"), lax.axis_size("col")
    result = result_ref[...]
    if parts:
        result = result + multiply(slots, slots_ref, time_ref, parts)
    piece = result.shape[0] // cols
    core = lax.rem(col, 2)
    for pair in range(cols // 2):
        even = result[(2 * pair) * piece : (2 * pair + 1) * piece, :]
        odd = result[(2 * pair + 1) * piece : (2 * pair + 2) * piece, :]
        keep_ref[pair * piece : (pair + 1) * piece, :] = jnp.where(core == 0, even, odd)
        send_ref[pair * piece : (pair + 1) * piece, :] = jnp.where(core == 0, odd, even)
    send_ref[(cols // 2) * piece :, :] = gram_ref[...] + gram_of(parts, slots_ref.shape[-1])


def chip_kernel(piece, keep_ref, sent_ref, got_ref, gram_ref, *out_refs):
    held = keep_ref.shape[0]
    gram_ref[...] = sent_ref[held:, :] + got_ref[held:, :]
    place = lax.div(lax.axis_index("col"), 2)
    for offset, out_ref in enumerate(out_refs):
        start = pl.multiple_of(lax.bitwise_xor(place, offset) * piece, piece)
        out_ref[...] = keep_ref[pl.ds(start, piece), :] + got_ref[pl.ds(start, piece), :]


def negative_inverse(matrix):
    size = matrix.shape[0]
    tiles = BLOCK // TILE
    lane = lax.broadcasted_iota(jnp.int32, (TILE, size), 1)
    sub = lax.broadcasted_iota(jnp.int32, (TILE, size), 0)
    at_row = lax.broadcasted_iota(jnp.int32, (size, size), 0)
    at_col = lax.broadcasted_iota(jnp.int32, (size, size), 1)

    def spread(value, row):
        return jnp.broadcast_to(value[row : row + 1, :], (TILE, size))

    for begin in range(0, size, BLOCK):
        end = begin + BLOCK
        work = [matrix[begin + TILE * t : begin + TILE * (t + 1), :] for t in range(tiles)]
        solved = [None] * tiles
        for strip in range(0, BLOCK, STRIP):
            cols = [
                {
                    t: jnp.broadcast_to(work[t][:, at : at + 1], (TILE, size))
                    for t in range(strip // TILE, tiles)
                }
                for at in range(begin + strip, begin + strip + STRIP)
            ]
            for k in range(STRIP):
                tile, row = divmod(strip + k, TILE)
                scale = lax.rsqrt(spread(cols[k][tile], row))
                here = lane == begin + strip + k
                pivot = jnp.where(here, -1.0, spread(work[tile], row)) * scale
                solved[tile] = pivot if row == 0 else jnp.where(sub >= row, pivot, solved[tile])
                lower = {t: cols[k][t] * scale for t in range(tile, tiles)}
                lower[tile] = jnp.where(sub > row, lower[tile], 0.0)
                for j in range(k + 1, STRIP):
                    its_tile, its_row = divmod(strip + j, TILE)
                    if its_tile == tile:
                        factor = spread(cols[j][tile], row) * scale
                    else:
                        factor = spread(lower[its_tile], its_row)
                    for t in range(its_tile, tiles):
                        cols[j][t] = cols[j][t] - lower[t] * factor
                for t in range(tile, tiles):
                    work[t] = jnp.where(here, 0.0, work[t]) - lower[t] * pivot
        row_of = lax.broadcasted_iota(jnp.int32, (BLOCK, size), 0) + begin
        col_of = lax.broadcasted_iota(jnp.int32, (BLOCK, size), 1)
        upper = (col_of > row_of) & (col_of < end)
        hi, mid, lo = split3(jnp.where(upper, 0.0, jnp.concatenate(solved, 0)))
        update = tdot(
            jnp.concatenate([hi, hi, mid, mid, hi, lo], 0),
            jnp.concatenate([hi, mid, hi, mid, lo, hi], 0),
        )
        swept = (at_row >= begin) & (at_row < end) | (at_col >= begin) & (at_col < end)
        matrix = jnp.where(swept, 0.0, matrix) - update
    return matrix


def inverse_kernel(time_gram_ref, *refs):
    grams, inverse_ref = refs[:-1], refs[-1]
    gram = sum(ref[...] for ref in grams)
    inverse_ref[...] = negative_inverse(gram * time_gram_ref[...])


def solve_kernel(inverse_ref, *refs):
    sums, (solved_ref, squares_ref) = refs[:-2], refs[-2:]
    solved = -jnp.dot(
        sum(ref[...] for ref in sums),
        inverse_ref[...],
        precision=lax.Precision.HIGHEST,
        preferred_element_type=F32,
    )
    solved_ref[...] = solved
    squares = jnp.sum(solved * solved, axis=0, keepdims=True)
    squares_ref[...] = jnp.broadcast_to(squares, squares_ref.shape)


def shifted(value, axis, offset, groups):
    return lax.ppermute(value, axis, [(at, at ^ offset) for at in range(groups)])


def call(kernel, operands, in_specs, outs, scratch=()):
    return pl.pallas_call(
        kernel,
        out_shape=tuple(jax.ShapeDtypeStruct(shape, dtype) for shape, dtype in outs),
        in_specs=in_specs,
        out_specs=(VMEM,) * len(outs),
        scratch_shapes=scratch,
        compiler_params=pltpu.CompilerParams(vmem_limit_bytes=40 * 2**20),
    )(*operands)


def per_device(tensor, second_factor, time_factor):
    snaps, own_rows, own_cols = tensor.shape
    depth, rank = second_factor.shape
    rows, cols = lax.axis_size("row"), lax.axis_size("col")
    piece = own_rows // cols
    pairs = cols // 2

    whole = ((depth + rank, rank), BF16)
    message, own = call(prepare_kernel, (second_factor,), [VMEM], [whole, whole])
    passed = list(range(rows // 2 + rows // 2 % 2, rows, 2))
    forwarded = [at + 1 for at in passed]
    early = [at for at in range(rows) if at not in forwarded]
    arrived = {at: shifted(message, "row", at, rows) for at in early[1:]}
    arrived[0] = own
    direct = depth % 128 == 0
    owners, width = (early + forwarded, depth) if direct else ([0], own_cols)
    slots, time, time_gram = call(
        functools.partial(load_kernel, owners, width),
        (tensor, time_factor),
        [HBM, HBM],
        [((len(owners), snaps, own_rows, width), BF16), ((snaps, rank), F32), ((rank, rank), F32)],
        [pltpu.SemaphoreType.DMA((len(owners) + 1,))],
    )
    for at in passed:
        final = at == passed[-1]
        parts = [arrived[at]] + ([arrived[it] for it in passed[:-1]] if final else [])
        shape = whole if final else ((depth, rank), BF16)
        (relayed,) = call(relay_kernel, (time, *parts), [VMEM] * (1 + len(parts)), [shape])
        arrived[at + 1] = shifted(relayed, "row", 1, rows)
    if direct:
        first, last = [arrived[at] for at in early], [arrived[at] for at in forwarded]
    else:
        row = lax.axis_index("row")
        low = jnp.stack([arrived[at][:depth] for at in range(rows)])
        low = low[jnp.arange(rows) ^ row].reshape(rows * depth, rank)
        rests = [arrived[at][depth:].astype(F32) for at in early + forwarded[-1:]]
        first, last = [jnp.concatenate([low, sum(rests).astype(BF16)], 0)], []
    result, gram = call(
        functools.partial(first_kernel, range(len(first))),
        (slots, time, *first),
        [VMEM] * (2 + len(first)),
        [((own_rows, rank), F32), ((rank, rank), F32)],
    )
    keep, send = call(
        functools.partial(last_kernel, range(len(first), len(owners))),
        (slots, time, result, gram, *last),
        [VMEM] * (4 + len(last)),
        [((pairs * piece, rank), F32), ((pairs * piece + rank, rank), F32)],
    )

    chip_gram, own_sum, *outs = call(
        functools.partial(chip_kernel, piece),
        (keep, send, shifted(send, "col", 1, cols)),
        [VMEM] * 3,
        [((rank, rank), F32)] + [((piece, rank), F32)] * pairs,
    )
    grams = [chip_gram] + [shifted(chip_gram, "col", 2 * at, cols) for at in range(1, pairs)]
    sums = [own_sum] + [shifted(out, "col", 2 * (at + 1), cols) for at, out in enumerate(outs)]
    (inverse,) = call(
        inverse_kernel, (time_gram, *grams), [VMEM] * (1 + pairs), [((rank, rank), F32)]
    )
    solved, squares = call(
        solve_kernel,
        (inverse, *sums),
        [VMEM] * (1 + pairs),
        [((piece, rank), F32), ((rows * cols, rank), F32)],
    )
    squares = lax.all_to_all(squares, ("row", "col"), 0, 0, tiled=True)
    scales = jnp.sqrt(jnp.sum(squares, axis=0) / (own_rows * rows) + 1e-06)
    return solved / scales[None, :], scales


def solution(mesh):
    in_specs = (P(None, "row", "col"), P(("col", "row"), None), P())
    out_specs = (P(("row", "col"), None), P())
    return jax.shard_map(
        per_device, mesh=mesh, in_specs=in_specs, out_specs=out_specs, check_vma=False
    )
```

time: 46.9 us -> 44.6 us (0.951)
  waiting for transfers between devices: 8.27 us -> 6.1 us
  Pallas kernels: 10.5 us -> 9.88 us
    ppermute x9 -> x10, waiting for transfers between devices: 8.27 us -> 6.1 us  [shifted(): lax.ppermute(value, axis, [(at, at ^ offset) for at in range(groups)])]
    pallas_call x6 -> x9, Pallas kernels: 10.5 us -> 9.88 us  [call(): pl.pallas_call(kernel, out_shape=tuple((jax.ShapeDtypeStruct(shape, dtype...]
    ppermute x9 -> x10, starting transfers between devices: 12.8 us -> 13.2 us  [shifted(): lax.ppermute(value, axis, [(at, at ^ offset) for at in range(groups)])]
  transfers between devices with their start and end apart: 9 -> 10, of which waited for: 3 -> 4; matrix products, arithmetic and copies ran while one was open for 0% -> 0% of each run, Pallas kernels for 12% -> 19%
where the time goes in v3:
time: 44.6 us; the launch traced here: 44.4 us
  starting transfers between devices  13.2 us (30%)
  blocking collectives  12.2 us (27%)
  Pallas kernels  9.88 us (22%)
  waiting for transfers between devices  6.1 us (14%)
  local copies, waits for them, and re-layouts  1.58 us (4%)
  between operations  0.73 us (2%)
  other arithmetic  0.7 us (2%)
    ppermute x10, starting transfers between devices, shifted(): lax.ppermute(value, axis, [(at, at ^ offset) for at in range(groups)])  13.2 us
    all_to_all x1, blocking collectives, per_device(): squares = lax.all_to_all(squares, ('row', 'col'), 0, 0, tiled=True)  12.2 us
    pallas_call x9, Pallas kernels, call(): pl.pallas_call(kernel, out_shape=tuple((jax.ShapeDtypeStruct(shape, dtype...  9.88 us
    ppermute x10, waiting for transfers between devices, shifted(): lax.ppermute(value, axis, [(at, at ^ offset) for at in range(groups)])  6.1 us
    unnamed x6, local copies, waits for them, and re-layouts  1.58 us
  transfers between devices with their start and end apart: 10, of which 4 were waited for; matrix products, arithmetic and copies ran while one was open for 0% of the time, Pallas kernels for 19%

profile of v3, /device:TPU:0, one launch (start us, length us, event | category | flops | bytes accessed | tf_op | source)
XLA Modules:
  0.0 44.4 jit_solution(13299110604337234097)
XLA Ops:
  0.6 0.9 %copy-done = f32[256,128]{1,0:T(8,128)S(1)} copy-done((f32[256,128]{1,0:T(8,128)S(1)}, f32[256,128]{1,0:T(8,128)}, u32[]{:S(2)}) %copy-start) | copy-done | bytes 131096
  1.5 0.3 shard_map.51
  1.8 4.1 %collective-permute-start.3 = (bf16[384,128]{1,0:T(8,128)(2,1)S(1)}, bf16[384,128]{1,0:T(8,128)(2,1)S(1)}, u32[]{:S(2)}, u32[]{:S(2)}) collective-permute-start(bf16[384,128]{1,0:T(8,128)(2,1)S(1)} %get-tuple-element.20), channel_id=1, source_target_pairs={{0,16},{4,20},{8,24},{12,28},{16,0},{20,4},{24,8},{28,12},{1,17},{... | collective-permute-start | bytes 294920 | tf_op jit(solution)/shard_map/ppermute | solution.py:202
  5.9 1.3 %collective-permute-start.4 = (bf16[384,128]{1,0:T(8,128)(2,1)S(1)}, bf16[384,128]{1,0:T(8,128)(2,1)S(1)}, u32[]{:S(2)}, u32[]{:S(2)}) collective-permute-start(bf16[384,128]{1,0:T(8,128)(2,1)S(1)} %get-tuple-element.20), channel_id=1, source_target_pairs={{0,24},{4,28},{8,16},{12,20},{16,8},{20,12},{24,0},{28,4},{1,25},{... | collective-permute-start | bytes 294920 | tf_op jit(solution)/shard_map/ppermute | solution.py:202
  7.3 1.5 %collective-permute-start = (bf16[384,128]{1,0:T(8,128)(2,1)S(1)}, bf16[384,128]{1,0:T(8,128)(2,1)S(1)}, u32[]{:S(2)}, u32[]{:S(2)}) collective-permute-start(bf16[384,128]{1,0:T(8,128)(2,1)S(1)} %get-tuple-element.20), channel_id=1, source_target_pairs={{0,4},{4,0},{8,12},{12,8},{16,20},{20,16},{24,28},{28,24},{1,5},{5... | collective-permute-start | bytes 294920 | tf_op jit(solution)/shard_map/ppermute | solution.py:202
  8.8 0.2 collective-permute-start.1
  9.0 1.7 %collective-permute-start.2 = (bf16[384,128]{1,0:T(8,128)(2,1)S(1)}, bf16[384,128]{1,0:T(8,128)(2,1)S(1)}, u32[]{:S(2)}, u32[]{:S(2)}) collective-permute-start(bf16[384,128]{1,0:T(8,128)(2,1)S(1)} %get-tuple-element.20), channel_id=1, source_target_pairs={{0,12},{4,8},{8,4},{12,0},{16,28},{20,24},{24,20},{28,16},{1,13},{... | collective-permute-start | bytes 294920 | tf_op jit(solution)/shard_map/ppermute | solution.py:202
  10.8 0.7 %copy-done.1 = f32[4,128]{1,0:T(4,128)S(1)} copy-done((f32[4,128]{1,0:T(4,128)S(1)}, f32[4,128]{1,0:T(4,128)}, u32[]{:S(2)}) %copy-start.1) | copy-done | bytes 2072
  11.4 3.6 %shard_map.50 = (bf16[8,4,512,256]{3,2,1,0:T(8,128)(2,1)S(1)}, f32[4,128]{1,0:T(4,128)S(1)}, f32[128,128]{1,0:T(8,128)S(1)}) custom-call(bf16[4,512,2048]{2,1,0:T(8,128)(2,1)} %tensor_ref.1, f32[4,128]{1,0:T(4,128)S(1)} %copy-done.1), custom_call_target="tpu_custom_call" | custom-call | tf_op jit(solution)/shard_map/pallas_call | solution.py:206
  15.0 0.0 collective-permute-done.3.refs_4_.refs_0_.refs_1_
  15.1 0.0 collective-permute-done.4.refs_5_.refs_0_
  15.1 1.6 %collective-permute-start.6 = (bf16[384,128]{1,0:T(8,128)(2,1)S(1)}, bf16[384,128]{1,0:T(8,128)(2,1)S(1)}, u32[]{:S(2)}, u32[]{:S(2)}) collective-permute-start(bf16[384,128]{1,0:T(8,128)(2,1)S(1)} %shard_map.54), channel_id=1, source_target_pairs={{0,4},{4,0},{8,12},{12,8},{16,20},{20,16},{24,28},{28,24},{1,5},{5... | collective-permute-start | bytes 294920 | tf_op jit(solution)/shard_map/ppermute | solution.py:202
  16.7 0.5 %collective-permute-start.5 = (bf16[256,128]{1,0:T(8,128)(2,1)S(1)}, bf16[256,128]{1,0:T(8,128)(2,1)S(1)}, u32[]{:S(2)}, u32[]{:S(2)}) collective-permute-start(bf16[256,128]{1,0:T(8,128)(2,1)S(1)} %shard_map.53), channel_id=1, source_target_pairs={{0,4},{4,0},{8,12},{12,8},{16,20},{20,16},{24,28},{28,24},{1,5},{5... | collective-permute-start | bytes 196616 | tf_op jit(solution)/shard_map/ppermute | solution.py:202
  17.2 0.0 collective-permute-done.refs_1_
  17.2 0.0 collective-permute-done.1.refs_2_
  17.2 0.6 %collective-permute-done.2.refs_3_ = bf16[384,128]{1,0:T(8,128)(2,1)S(1)} collective-permute-done((bf16[384,128]{1,0:T(8,128)(2,1)S(1)}, bf16[384,128]{1,0:T(8,128)(2,1)S(1)}, u32[]{:S(2)}, u32[]{:S(2)}) %collective-permute-start.2) | collective-permute-done | bytes 98336 | tf_op jit(solution)/shard_map/ppermute | solution.py:202
  17.8 1.9 %shard_map.52 = (f32[512,128]{1,0:T(8,128)S(1)}, f32[128,128]{1,0:T(8,128)S(1)}) custom-call(bf16[8,4,512,256]{3,2,1,0:T(8,128)(2,1)S(1)} %get-tuple-element.17.slots_ref, f32[4,128]{1,0:T(4,128)S(1)} %get-tuple-element.18.time_ref.loaded_ref, bf16[384,128]{1,0:T(8,128)(2,1)S(1)} %get-tuple-element.19.refs_0_, ...), custom_call_target="tpu_custom_call" | custom-call | tf_op jit(solution)/shard_map/pallas_call | solution.py:206
  19.7 1.4 %collective-permute-done.5.refs_0_ = bf16[256,128]{1,0:T(8,128)(2,1)S(1)} collective-permute-done((bf16[256,128]{1,0:T(8,128)(2,1)S(1)}, bf16[256,128]{1,0:T(8,128)(2,1)S(1)}, u32[]{:S(2)}, u32[]{:S(2)}) %collective-permute-start.5) | collective-permute-done | bytes 65568 | tf_op jit(solution)/shard_map/ppermute | solution.py:202
  21.1 0.0 collective-permute-done.6.refs_1_
  21.1 0.7 %shard_map.55 = (f32[256,128]{1,0:T(8,128)S(1)}, f32[384,128]{1,0:T(8,128)S(1)}) custom-call(bf16[8,4,512,256]{3,2,1,0:T(8,128)(2,1)S(1)} %get-tuple-element.17.slots_ref, f32[4,128]{1,0:T(4,128)S(1)} %get-tuple-element.18.time_ref.loaded_ref, f32[512,128]{1,0:T(8,128)S(1)} %get-tuple-element.21.result_ref, f32[128,128]{1,0:T(8,128)S(1)} %get-tuple-element.22.gram_ref, ...), custom_call_target="tpu_custom_call" | custom-call | tf_op jit(solution)/shard_map/pallas_call | solution.py:206
  21.9 0.1 collective-permute-start.7
  21.9 1.4 %collective-permute-done.7.got_ref = f32[384,128]{1,0:T(8,128)S(1)} collective-permute-done((f32[384,128]{1,0:T(8,128)S(1)}, f32[384,128]{1,0:T(8,128)S(1)}, u32[]{:S(2)}, u32[]{:S(2)}) %collective-permute-start.7) | collective-permute-done | bytes 196640 | tf_op jit(solution)/shard_map/ppermute | solution.py:202
  23.4 1.6 %collective-permute-start.8 = (f32[128,128]{1,0:T(8,128)S(1)}, f32[128,128]{1,0:T(8,128)S(1)}, u32[]{:S(2)}, u32[]{:S(2)}) collective-permute-start(f32[128,128]{1,0:T(8,128)S(1)} %get-tuple-element.25.refs_0_), channel_id=1, source_target_pairs={{0,2},{1,3},{2,0},{3,1},{4,6},{5,7},{6,4},{7,5},{8,10},{9,11},{10,... | collective-permute-start | bytes 196616 | tf_op jit(solution)/shard_map/ppermute | solution.py:202
  25.0 0.5 %collective-permute-start.9 = (f32[128,128]{1,0:T(8,128)S(1)}, f32[128,128]{1,0:T(8,128)S(1)}, u32[]{:S(2)}, u32[]{:S(2)}) collective-permute-start(f32[128,128]{1,0:T(8,128)S(1)} %get-tuple-element.27), channel_id=1, source_target_pairs={{0,2},{1,3},{2,0},{3,1},{4,6},{5,7},{6,4},{7,5},{8,10},{9,11},{10,... | collective-permute-start | bytes 196616 | tf_op jit(solution)/shard_map/ppermute | solution.py:202
  25.5 2.6 %collective-permute-done.8.refs_1_ = f32[128,128]{1,0:T(8,128)S(1)} collective-permute-done((f32[128,128]{1,0:T(8,128)S(1)}, f32[128,128]{1,0:T(8,128)S(1)}, u32[]{:S(2)}, u32[]{:S(2)}) %collective-permute-start.8) | collective-permute-done | bytes 65568 | tf_op jit(solution)/shard_map/ppermute | solution.py:202
  28.1 3.1 %shard_map.57.inverse_ref = f32[128,128]{1,0:T(8,128)S(1)} custom-call(f32[128,128]{1,0:T(8,128)S(1)} %get-tuple-element.16.time_gram_ref, f32[128,128]{1,0:T(8,128)S(1)} %get-tuple-element.25.refs_0_, f32[128,128]{1,0:T(8,128)S(1)} %collective-permute-done.8.refs_1_), custom_call_target="tpu_custom_call" | custom-call | tf_op jit(solution)/shard_map/pallas_call | solution.py:206
  31.3 0.0 collective-permute-done.9.refs_1_
  31.3 0.2 shard_map.58
  31.5 12.2 %all_to_all.9 = f32[32,1,128]{2,1,0:T(1,128)S(1)} all-to-all(f32[32,1,128]{2,1,0:T(1,128)S(1)} %bitcast.3), channel_id=1, replica_groups=mesh['row'=8,'col'=4] {'row','col'}, dimensions={0} | all-to-all | bytes 32768 | tf_op jit(solution)/shard_map/all_to_all | solution.py:283
  43.7 0.1 reduce_sum.9
  43.7 0.6 %broadcast_divide_fusion = f32[128,128]{1,0:T(8,128)} fusion(f32[128,128]{1,0:T(8,128)S(1)} %get-tuple-element.28, f32[128]{0:T(128)S(1)} %add_sqrt_fusion), kind=kLoop, calls=%fused_computation | loop fusion | flops 16384 | bytes 131584 | tf_op jit(solution)/shard_map/div | solution.py:285
  44.4 0.0 copy-done.2
  (7 shorter events, 0.1 us)
Async XLA Ops:
  0.6 0.9 %copy-start = (f32[256,128]{1,0:T(8,128)S(1)}, f32[256,128]{1,0:T(8,128)}, u32[]{:S(2)}) copy-start(f32[256,128]{1,0:T(8,128)} %factor_ref.1) | copy-start | bytes 393220
  1.8 13.2 %collective-permute-start.3 = (bf16[384,128]{1,0:T(8,128)(2,1)S(1)}, bf16[384,128]{1,0:T(8,128)(2,1)S(1)}, u32[]{:S(2)}, u32[]{:S(2)}) collective-permute-start(bf16[384,128]{1,0:T(8,128)(2,1)S(1)} %get-tuple-element.20), channel_id=1, source_target_pairs={{0,16},{4,20},{8,24},{12,28},{16,0},{20,4},{24,8},{28,12},{1,17},{... | collective-permute-start | bytes 294920 | tf_op jit(solution)/shard_map/ppermute | solution.py:202
  5.9 9.1 %collective-permute-start.4 = (bf16[384,128]{1,0:T(8,128)(2,1)S(1)}, bf16[384,128]{1,0:T(8,128)(2,1)S(1)}, u32[]{:S(2)}, u32[]{:S(2)}) collective-permute-start(bf16[384,128]{1,0:T(8,128)(2,1)S(1)} %get-tuple-element.20), channel_id=1, source_target_pairs={{0,24},{4,28},{8,16},{12,20},{16,8},{20,12},{24,0},{28,4},{1,25},{... | collective-permute-start | bytes 294920 | tf_op jit(solution)/shard_map/ppermute | solution.py:202
  7.3 9.9 %collective-permute-start = (bf16[384,128]{1,0:T(8,128)(2,1)S(1)}, bf16[384,128]{1,0:T(8,128)(2,1)S(1)}, u32[]{:S(2)}, u32[]{:S(2)}) collective-permute-start(bf16[384,128]{1,0:T(8,128)(2,1)S(1)} %get-tuple-element.20), channel_id=1, source_target_pairs={{0,4},{4,0},{8,12},{12,8},{16,20},{20,16},{24,28},{28,24},{1,5},{5... | collective-permute-start | bytes 294920 | tf_op jit(solution)/shard_map/ppermute | solution.py:202
  8.8 8.4 %collective-permute-start.1 = (bf16[384,128]{1,0:T(8,128)(2,1)S(1)}, bf16[384,128]{1,0:T(8,128)(2,1)S(1)}, u32[]{:S(2)}, u32[]{:S(2)}) collective-permute-start(bf16[384,128]{1,0:T(8,128)(2,1)S(1)} %get-tuple-element.20), channel_id=1, source_target_pairs={{0,8},{4,12},{8,0},{12,4},{16,24},{20,28},{24,16},{28,20},{1,9},{5... | collective-permute-start | bytes 294920 | tf_op jit(solution)/shard_map/ppermute | solution.py:202
  9.0 8.7 %collective-permute-start.2 = (bf16[384,128]{1,0:T(8,128)(2,1)S(1)}, bf16[384,128]{1,0:T(8,128)(2,1)S(1)}, u32[]{:S(2)}, u32[]{:S(2)}) collective-permute-start(bf16[384,128]{1,0:T(8,128)(2,1)S(1)} %get-tuple-element.20), channel_id=1, source_target_pairs={{0,12},{4,8},{8,4},{12,0},{16,28},{20,24},{24,20},{28,16},{1,13},{... | collective-permute-start | bytes 294920 | tf_op jit(solution)/shard_map/ppermute | solution.py:202
  10.8 0.7 %copy-start.1 = (f32[4,128]{1,0:T(4,128)S(1)}, f32[4,128]{1,0:T(4,128)}, u32[]{:S(2)}) copy-start(f32[4,128]{1,0:T(4,128)} %time_ref.1) | copy-start | bytes 6148
  15.1 6.0 %collective-permute-start.6 = (bf16[384,128]{1,0:T(8,128)(2,1)S(1)}, bf16[384,128]{1,0:T(8,128)(2,1)S(1)}, u32[]{:S(2)}, u32[]{:S(2)}) collective-permute-start(bf16[384,128]{1,0:T(8,128)(2,1)S(1)} %shard_map.54), channel_id=1, source_target_pairs={{0,4},{4,0},{8,12},{12,8},{16,20},{20,16},{24,28},{28,24},{1,5},{5... | collective-permute-start | bytes 294920 | tf_op jit(solution)/shard_map/ppermute | solution.py:202
  16.7 4.4 %collective-permute-start.5 = (bf16[256,128]{1,0:T(8,128)(2,1)S(1)}, bf16[256,128]{1,0:T(8,128)(2,1)S(1)}, u32[]{:S(2)}, u32[]{:S(2)}) collective-permute-start(bf16[256,128]{1,0:T(8,128)(2,1)S(1)} %shard_map.53), channel_id=1, source_target_pairs={{0,4},{4,0},{8,12},{12,8},{16,20},{20,16},{24,28},{28,24},{1,5},{5... | collective-permute-start | bytes 196616 | tf_op jit(solution)/shard_map/ppermute | solution.py:202
  21.9 1.5 %collective-permute-start.7 = (f32[384,128]{1,0:T(8,128)S(1)}, f32[384,128]{1,0:T(8,128)S(1)}, u32[]{:S(2)}, u32[]{:S(2)}) collective-permute-start(f32[384,128]{1,0:T(8,128)S(1)} %get-tuple-element.24.sent_ref), channel_id=1, source_target_pairs={{0,1},{1,0},{2,3},{3,2},{4,5},{5,4},{6,7},{7,6},{8,9},{9,8},{10,11... | collective-permute-start | bytes 589832 | tf_op jit(solution)/shard_map/ppermute | solution.py:202
  23.4 4.7 %collective-permute-start.8 = (f32[128,128]{1,0:T(8,128)S(1)}, f32[128,128]{1,0:T(8,128)S(1)}, u32[]{:S(2)}, u32[]{:S(2)}) collective-permute-start(f32[128,128]{1,0:T(8,128)S(1)} %get-tuple-element.25.refs_0_), channel_id=1, source_target_pairs={{0,2},{1,3},{2,0},{3,1},{4,6},{5,7},{6,4},{7,5},{8,10},{9,11},{10,... | collective-permute-start | bytes 196616 | tf_op jit(solution)/shard_map/ppermute | solution.py:202
  25.0 6.3 %collective-permute-start.9 = (f32[128,128]{1,0:T(8,128)S(1)}, f32[128,128]{1,0:T(8,128)S(1)}, u32[]{:S(2)}, u32[]{:S(2)}) collective-permute-start(f32[128,128]{1,0:T(8,128)S(1)} %get-tuple-element.27), channel_id=1, source_target_pairs={{0,2},{1,3},{2,0},{3,1},{4,6},{5,7},{6,4},{7,5},{8,10},{9,11},{10,... | collective-permute-start | bytes 196616 | tf_op jit(solution)/shard_map/ppermute | solution.py:202
  43.7 0.7 %copy-start.2 = (f32[128]{0:T(128)}, f32[128]{0:T(128)S(1)}, u32[]{:S(2)}) copy-start(f32[128]{0:T(128)S(1)} %add_sqrt_fusion) | copy-start | bytes 1540

commit v4 on v3

--- a/solution.py
+++ b/solution.py
@@ -24,32 +24,52 @@
     return hi, mid, (rest - mid.astype(F32)).astype(BF16)
 
 
+def packed(square):
+    size = square.shape[0]
+    q, h = size // 4, size // 8
+    return jnp.concatenate(
+        [
+            jnp.concatenate([square[2 * q : 3 * q, : 3 * q], square[:q, :q]], 1),
+            square[3 * q :, :],
+            jnp.concatenate([square[q : q + h, : 2 * q], square[q + h : 2 * q, : 2 * q]], 1),
+        ],
+        0,
+    )
+
+
+def unpacked(pack):
+    size = pack.shape[1]
+    q, h = size // 4, size // 8
+    second = jnp.concatenate([pack[2 * q :, : 2 * q], pack[2 * q :, 2 * q :]], 0)
+    lower = jnp.concatenate(
+        [
+            jnp.concatenate([pack[:q, 3 * q :], jnp.zeros((q, 3 * q), F32)], 1),
+            jnp.concatenate([second, jnp.zeros((q, 2 * q), F32)], 1),
+            jnp.concatenate([pack[:q, : 3 * q], jnp.zeros((q, q), F32)], 1),
+            pack[q : 2 * q, :],
+        ],
+        0,
+    )
+    row = lax.broadcasted_iota(jnp.int32, (size, size), 0)
+    col = lax.broadcasted_iota(jnp.int32, (size, size), 1)
+    return jnp.where(col >= row, lower.T, lower)
+
+
 def prepare_kernel(factor_ref, out_ref, own_ref):
     rows, rank = factor_ref.shape
     factor = factor_ref[...]
     low = factor.astype(BF16)
     residual = (factor - low.astype(F32)).astype(BF16)
     cross = tdot(low, residual)
-    rest = cross + cross.T + tdot(residual, residual)
+    rest = packed((cross + cross.T + tdot(residual, residual)).astype(BF16))
     for ref in (out_ref, own_ref):
         ref[:rows, :] = low
-        ref[rows:, :] = rest.astype(BF16)
-
-
-def load_kernel(owners, depth, tensor_ref, time_ref, slots_ref, time_out_ref, gram_ref, sems):
-    row = lax.axis_index("row")
-    copies = [pltpu.make_async_copy(time_ref, time_out_ref, sems.at[len(owners)])]
-    for at, owner in enumerate(owners):
-        start = pl.multiple_of(lax.bitwise_xor(row, owner) * depth, depth)
-        copies.append(
-            pltpu.make_async_copy(
-                tensor_ref.at[:, :, pl.ds(start, depth)], slots_ref.at[at], sems.at[at]
-            )
-        )
-    for copy in copies:
-        copy.start()
-    copies[0].wait()
-    time = time_out_ref[...]
+        ref[rows:, :] = rest
+
+
+def time_kernel(time_ref, out_ref, gram_ref):
+    time = time_ref[...]
+    out_ref[...] = time
     gram_ref[...] = lax.dot_general(
         time,
         time,
@@ -57,55 +77,63 @@
         precision=lax.Precision.HIGHEST,
         preferred_element_type=F32,
     )
-    for copy in copies[1:]:
-        copy.wait()
-
-
-def relay_kernel(loaded_ref, *refs):
-    del loaded_ref
-    parts, out_ref = refs[:-1], refs[-1]
-    depth = parts[0].shape[0] - parts[0].shape[1]
-    out_ref[:depth, :] = parts[0][:depth, :]
-    if len(parts) > 1:
-        rest = sum(part[depth:, :].astype(F32) for part in parts)
-        out_ref[depth:, :] = rest.astype(BF16)
+
+
+def relay_kernel(ready_ref, part_ref, out_ref):
+    del ready_ref
+    out_ref[...] = part_ref[...]
 
 
 def gram_of(parts, depth):
-    gram = 0.0
+    gram, rest = 0.0, 0.0
     for part in parts:
         low = part[:depth, :]
         gram = gram + tdot(low, low)
-        if part.shape[0] > depth:
-            gram = gram + part[depth:, :].astype(F32)
-    return gram
-
-
-def multiply(slots, slots_ref, time_ref, parts):
-    snaps, own_rows, depth = slots_ref.shape[1:]
-    rank = time_ref.shape[1]
-    total = [jnp.zeros((own_rows, rank), F32) for _ in range(snaps)]
-    for at, part in zip(slots, parts):
+        rest = rest + part[depth:, :].astype(F32)
+    return gram, rest
+
+
+def multiply(blocks, time_ref, parts, depth):
+    snaps = time_ref.shape[0]
+    total = [0.0] * snaps
+    for (block, arrival), part in zip(blocks, parts):
+        if arrival is not None:
+            arrival.wait()
         low = part[:depth, :]
         for snap in range(snaps):
             total[snap] = total[snap] + jnp.dot(
-                slots_ref[at, snap], low, preferred_element_type=F32
+                block[snap], low, preferred_element_type=F32
             )
     return sum(total[snap] * time_ref[snap : snap + 1, :] for snap in range(snaps))
 
 
-def first_kernel(slots, slots_ref, time_ref, *refs):
-    parts, (result_ref, gram_ref) = refs[:-2], refs[-2:]
-    result_ref[...] = multiply(slots, slots_ref, time_ref, parts)
-    gram_ref[...] = gram_of(parts, slots_ref.shape[-1])
-
-
-def last_kernel(slots, slots_ref, time_ref, result_ref, gram_ref, *refs):
-    parts, (keep_ref, send_ref) = refs[:-2], refs[-2:]
+def first_kernel(owners, depth, tensor_ref, time_ref, *refs):
+    count = len(refs) - 6
+    parts, (result_ref, gram_ref, rest_ref, later_ref, slots, sems) = refs[:count], refs[count:]
+    row = lax.axis_index("row")
+    blocks = []
+    for at, owner in enumerate(owners):
+        block = slots.at[at] if at < count else later_ref.at[at - count]
+        start = pl.multiple_of(lax.bitwise_xor(row, owner) * depth, depth)
+        arrival = pltpu.make_async_copy(
+            tensor_ref.at[:, :, pl.ds(start, depth)], block, sems.at[at]
+        )
+        arrival.start()
+        blocks.append((block, arrival))
+    gram_ref[...], rest_ref[...] = gram_of(parts, depth)
+    result_ref[...] = multiply(blocks[:count], time_ref, parts, depth)
+    for _, arrival in blocks[count:]:
+        arrival.wait()
+
+
+def last_kernel(depth, time_ref, result_ref, gram_ref, rest_ref, *refs):
+    parts, (later_ref, keep_ref, send_ref) = refs[:-3], refs[-3:]
     col, cols = lax.axis_index("col"), lax.axis_size("col")
     result = result_ref[...]
+    gram, rest = gram_of(parts, depth)
     if parts:
-        result = result + multiply(slots, slots_ref, time_ref, parts)
+        blocks = [(later_ref.at[at], None) for at in range(len(parts))]
+        result = result + multiply(blocks, time_ref, parts, depth)
     piece = result.shape[0] // cols
     core = lax.rem(col, 2)
     for pair in range(cols // 2):
@@ -113,7 +141,7 @@
         odd = result[(2 * pair + 1) * piece : (2 * pair + 2) * piece, :]
         keep_ref[pair * piece : (pair + 1) * piece, :] = jnp.where(core == 0, even, odd)
         send_ref[pair * piece : (pair + 1) * piece, :] = jnp.where(core == 0, odd, even)
-    send_ref[(cols // 2) * piece :, :] = gram_ref[...] + gram_of(parts, slots_ref.shape[-1])
+    send_ref[(cols // 2) * piece :, :] = gram_ref[...] + gram + unpacked(rest_ref[...] + rest)
 
 
 def chip_kernel(piece, keep_ref, sent_ref, got_ref, gram_ref, *out_refs):
@@ -202,14 +230,14 @@
     return lax.ppermute(value, axis, [(at, at ^ offset) for at in range(groups)])
 
 
-def call(kernel, operands, in_specs, outs, scratch=()):
+def call(kernel, operands, in_specs, outs, scratch=(), room=40):
     return pl.pallas_call(
         kernel,
         out_shape=tuple(jax.ShapeDtypeStruct(shape, dtype) for shape, dtype in outs),
         in_specs=in_specs,
         out_specs=(VMEM,) * len(outs),
         scratch_shapes=scratch,
-        compiler_params=pltpu.CompilerParams(vmem_limit_bytes=40 * 2**20),
+        compiler_params=pltpu.CompilerParams(vmem_limit_bytes=room * 2**20),
     )(*operands)
 
 
@@ -220,46 +248,46 @@
     piece = own_rows // cols
     pairs = cols // 2
 
-    whole = ((depth + rank, rank), BF16)
+    pack = rank * 5 // 8
+    whole = ((depth + pack, rank), BF16)
     message, own = call(prepare_kernel, (second_factor,), [VMEM], [whole, whole])
-    passed = list(range(rows // 2 + rows // 2 % 2, rows, 2))
-    forwarded = [at + 1 for at in passed]
-    early = [at for at in range(rows) if at not in forwarded]
-    arrived = {at: shifted(message, "row", at, rows) for at in early[1:]}
-    arrived[0] = own
-    direct = depth % 128 == 0
-    owners, width = (early + forwarded, depth) if direct else ([0], own_cols)
-    slots, time, time_gram = call(
-        functools.partial(load_kernel, owners, width),
-        (tensor, time_factor),
-        [HBM, HBM],
-        [((len(owners), snaps, own_rows, width), BF16), ((snaps, rank), F32), ((rank, rank), F32)],
-        [pltpu.SemaphoreType.DMA((len(owners) + 1,))],
-    )
-    for at in passed:
-        final = at == passed[-1]
-        parts = [arrived[at]] + ([arrived[it] for it in passed[:-1]] if final else [])
-        shape = whole if final else ((depth, rank), BF16)
-        (relayed,) = call(relay_kernel, (time, *parts), [VMEM] * (1 + len(parts)), [shape])
-        arrived[at + 1] = shifted(relayed, "row", 1, rows)
-    if direct:
-        first, last = [arrived[at] for at in early], [arrived[at] for at in forwarded]
+    half = rows // 2
+    near = range(1, half)
+    opposite = shifted(message, "row", half, rows)
+    arrived = {at: shifted(message, "row", at, rows) for at in near}
+    time, time_gram = call(
+        time_kernel, (time_factor,), [VMEM], [((snaps, rank), F32), ((rank, rank), F32)]
+    )
+    (opposite,) = call(relay_kernel, (time, opposite), [VMEM] * 2, [whole])
+    arrived[0], arrived[half] = own, opposite
+    for at in near:
+        arrived[half + at] = shifted(opposite, "row", at, rows)
+
+    if depth % 128 == 0:
+        owners, width, split = list(range(rows)), depth, half + 1
+        parts = [arrived[at] for at in range(rows)]
     else:
+        owners, width, split = [0], own_cols, 1
         row = lax.axis_index("row")
         low = jnp.stack([arrived[at][:depth] for at in range(rows)])
         low = low[jnp.arange(rows) ^ row].reshape(rows * depth, rank)
-        rests = [arrived[at][depth:].astype(F32) for at in early + forwarded[-1:]]
-        first, last = [jnp.concatenate([low, sum(rests).astype(BF16)], 0)], []
-    result, gram = call(
-        functools.partial(first_kernel, range(len(first))),
-        (slots, time, *first),
-        [VMEM] * (2 + len(first)),
-        [((own_rows, rank), F32), ((rank, rank), F32)],
+        rest = sum(arrived[at][depth:].astype(F32) for at in range(rows)).astype(BF16)
+        parts = [jnp.concatenate([low, rest], 0)]
+    square = ((rank, rank), F32)
+    block = (snaps, own_rows, width)
+    later = max(len(owners) - split, 1)
+    result, gram, rest, tensor_later = call(
+        functools.partial(first_kernel, owners, width),
+        (tensor, time, *parts[:split]),
+        [HBM] + [VMEM] * (1 + split),
+        [((own_rows, rank), F32), square, ((pack, rank), F32), ((later, *block), BF16)],
+        [pltpu.VMEM((split, *block), BF16), pltpu.SemaphoreType.DMA((len(owners),))],
+        room=48,
     )
     keep, send = call(
-        functools.partial(last_kernel, range(len(first), len(owners))),
-        (slots, time, result, gram, *last),
-        [VMEM] * (4 + len(last)),
+        functools.partial(last_kernel, width),
+        (time, result, gram, rest, *parts[split:], tensor_later),
+        [VMEM] * (5 + len(parts) - split),
         [((pairs * piece, rank), F32), ((pairs * piece + rank, rank), F32)],
     )
 

time: 44.6 us -> 42.3 us (0.948)
  Pallas kernels: 9.88 us -> 8.69 us
  waiting for transfers between devices: 6.1 us -> 5.4 us
  blocking collectives: 12.2 us -> 11.7 us
    pallas_call x9 -> x8, Pallas kernels: 9.88 us -> 8.69 us  [call(): pl.pallas_call(kernel, out_shape=tuple((jax.ShapeDtypeStruct(shape, dtype...]
    ppermute x10, waiting for transfers between devices: 6.1 us -> 5.4 us  [shifted(): lax.ppermute(value, axis, [(at, at ^ offset) for at in range(groups)])]
    all_to_all x1, blocking collectives: 12.2 us -> 11.7 us  [per_device(): squares = lax.all_to_all(squares, ('row', 'col'), 0, 0, tiled=True)]
  transfers between devices with their start and end apart: 10 -> 10, of which waited for: 4 -> 4; matrix products, arithmetic and copies ran while one was open for 0% -> 0% of each run, Pallas kernels for 19% -> 17%
where the time goes in v4:
time: 42.3 us; the launch traced here: 42.1 us
  starting transfers between devices  13.3 us (31%)
  blocking collectives  11.7 us (28%)
  Pallas kernels  8.69 us (21%)
  waiting for transfers between devices  5.4 us (13%)
  local copies, waits for them, and re-layouts  1.58 us (4%)
  between operations  0.73 us (2%)
  other arithmetic  0.7 us (2%)
    ppermute x10, starting transfers between devices, shifted(): lax.ppermute(value, axis, [(at, at ^ offset) for at in range(groups)])  13.3 us
    all_to_all x1, blocking collectives, per_device(): squares = lax.all_to_all(squares, ('row', 'col'), 0, 0, tiled=True)  11.7 us
    pallas_call x8, Pallas kernels, call(): pl.pallas_call(kernel, out_shape=tuple((jax.ShapeDtypeStruct(shape, dtype...  8.69 us
    ppermute x10, waiting for transfers between devices, shifted(): lax.ppermute(value, axis, [(at, at ^ offset) for at in range(groups)])  5.4 us
    unnamed x6, local copies, waits for them, and re-layouts  1.58 us
  transfers between devices with their start and end apart: 10, of which 4 were waited for; matrix products, arithmetic and copies ran while one was open for 0% of the time, Pallas kernels for 17%

profile of v4, /device:TPU:0, one launch (start us, length us, event | category | flops | bytes accessed | tf_op | source)
XLA Modules:
  0.0 42.1 jit_solution(8969156211598771792)
XLA Ops:
  0.6 0.0 copy-start
  0.6 0.9 %copy-done = f32[256,128]{1,0:T(8,128)S(1)} copy-done((f32[256,128]{1,0:T(8,128)S(1)}, f32[256,128]{1,0:T(8,128)}, u32[]{:S(2)}) %copy-start) | copy-done | bytes 131096
  1.5 0.3 shard_map.51
  1.9 4.1 %collective-permute-start.3 = (bf16[336,128]{1,0:T(8,128)(2,1)S(1)}, bf16[336,128]{1,0:T(8,128)(2,1)S(1)}, u32[]{:S(2)}, u32[]{:S(2)}) collective-permute-start(bf16[336,128]{1,0:T(8,128)(2,1)S(1)} %get-tuple-element.20), channel_id=1, source_target_pairs={{0,16},{4,20},{8,24},{12,28},{16,0},{20,4},{24,8},{28,12},{1,17},{... | collective-permute-start | bytes 258056 | tf_op jit(solution)/shard_map/ppermute | solution.py:230
  5.9 1.5 %collective-permute-start = (bf16[336,128]{1,0:T(8,128)(2,1)S(1)}, bf16[336,128]{1,0:T(8,128)(2,1)S(1)}, u32[]{:S(2)}, u32[]{:S(2)}) collective-permute-start(bf16[336,128]{1,0:T(8,128)(2,1)S(1)} %get-tuple-element.20), channel_id=1, source_target_pairs={{0,4},{4,0},{8,12},{12,8},{16,20},{20,16},{24,28},{28,24},{1,5},{5... | collective-permute-start | bytes 258056 | tf_op jit(solution)/shard_map/ppermute | solution.py:230
  7.5 1.6 %collective-permute-start.1 = (bf16[336,128]{1,0:T(8,128)(2,1)S(1)}, bf16[336,128]{1,0:T(8,128)(2,1)S(1)}, u32[]{:S(2)}, u32[]{:S(2)}) collective-permute-start(bf16[336,128]{1,0:T(8,128)(2,1)S(1)} %get-tuple-element.20), channel_id=1, source_target_pairs={{0,8},{4,12},{8,0},{12,4},{16,24},{20,28},{24,16},{28,20},{1,9},{5... | collective-permute-start | bytes 258056 | tf_op jit(solution)/shard_map/ppermute | solution.py:230
  9.0 0.4 collective-permute-start.2
  9.4 0.7 %copy-done.1 = f32[4,128]{1,0:T(4,128)S(1)} copy-done((f32[4,128]{1,0:T(4,128)S(1)}, f32[4,128]{1,0:T(4,128)}, u32[]{:S(2)}) %copy-start.1) | copy-done | bytes 2072
  10.1 0.3 shard_map.50
  10.4 0.0 collective-permute-done.3.part_ref
  10.4 1.6 %collective-permute-start.4 = (bf16[336,128]{1,0:T(8,128)(2,1)S(1)}, bf16[336,128]{1,0:T(8,128)(2,1)S(1)}, u32[]{:S(2)}, u32[]{:S(2)}) collective-permute-start(bf16[336,128]{1,0:T(8,128)(2,1)S(1)} %shard_map.52.refs_4_), channel_id=1, source_target_pairs={{0,4},{4,0},{8,12},{12,8},{16,20},{20,16},{24,28},{28,24},{1,5},{5... | collective-permute-start | bytes 258056 | tf_op jit(solution)/shard_map/ppermute | solution.py:230
  12.0 1.6 %collective-permute-start.5 = (bf16[336,128]{1,0:T(8,128)(2,1)S(1)}, bf16[336,128]{1,0:T(8,128)(2,1)S(1)}, u32[]{:S(2)}, u32[]{:S(2)}) collective-permute-start(bf16[336,128]{1,0:T(8,128)(2,1)S(1)} %shard_map.52.refs_4_), channel_id=1, source_target_pairs={{0,8},{4,12},{8,0},{12,4},{16,24},{20,28},{24,16},{28,20},{1,9},{5... | collective-permute-start | bytes 258056 | tf_op jit(solution)/shard_map/ppermute | solution.py:230
  13.6 0.0 collective-permute-done.refs_1_
  13.6 0.4 collective-permute-start.6
  14.0 0.0 collective-permute-done.1.refs_2_
  14.0 1.0 %collective-permute-done.2.refs_3_ = bf16[336,128]{1,0:T(8,128)(2,1)S(1)} collective-permute-done((bf16[336,128]{1,0:T(8,128)(2,1)S(1)}, bf16[336,128]{1,0:T(8,128)(2,1)S(1)}, u32[]{:S(2)}, u32[]{:S(2)}) %collective-permute-start.2) | collective-permute-done | bytes 86048 | tf_op jit(solution)/shard_map/ppermute | solution.py:230
  15.0 3.7 %shard_map.53 = (f32[512,128]{1,0:T(8,128)S(1)}, f32[128,128]{1,0:T(8,128)S(1)}, f32[80,128]{1,0:T(8,128)S(1)}, bf16[3,4,512,256]{3,2,1,0:T(8,128)(2,1)S(1)}) custom-call(bf16[4,512,2048]{2,1,0:T(8,128)(2,1)} %tensor_ref.1, f32[4,128]{1,0:T(4,128)S(1)} %get-tuple-element.18.ready_ref.time_ref, bf16[336,128]{1,0:T(8,128)(2,1)S(1)} %get-tuple-element.19.refs_0_, ...), custom_call_target="tpu_custom_call" | custom-call | tf_op jit(solution)/shard_map/pallas_call | solution.py:234
  18.6 0.0 collective-permute-done.4.refs_0_
  18.6 0.0 collective-permute-done.5.refs_1_
  18.7 0.3 collective-permute-done.6.refs_2_
  18.9 1.1 %shard_map.54 = (f32[256,128]{1,0:T(8,128)S(1)}, f32[384,128]{1,0:T(8,128)S(1)}) custom-call(f32[4,128]{1,0:T(4,128)S(1)} %get-tuple-element.18.ready_ref.time_ref, f32[512,128]{1,0:T(8,128)S(1)} %get-tuple-element.21.result_ref, f32[128,128]{1,0:T(8,128)S(1)} %get-tuple-element.22.gram_ref, f32[80,128]{1,0:T(8,128)S(1)} %get-tuple-element.23.rest_ref, ...), custom_call_target="tpu_custom_call" | custom-call | tf_op jit(solution)/shard_map/pallas_call | solution.py:234
  20.0 0.1 collective-permute-start.7
  20.1 1.4 %collective-permute-done.7.got_ref = f32[384,128]{1,0:T(8,128)S(1)} collective-permute-done((f32[384,128]{1,0:T(8,128)S(1)}, f32[384,128]{1,0:T(8,128)S(1)}, u32[]{:S(2)}, u32[]{:S(2)}) %collective-permute-start.7) | collective-permute-done | bytes 196640 | tf_op jit(solution)/shard_map/ppermute | solution.py:230
  21.6 1.6 %collective-permute-start.8 = (f32[128,128]{1,0:T(8,128)S(1)}, f32[128,128]{1,0:T(8,128)S(1)}, u32[]{:S(2)}, u32[]{:S(2)}) collective-permute-start(f32[128,128]{1,0:T(8,128)S(1)} %get-tuple-element.27.refs_0_), channel_id=1, source_target_pairs={{0,2},{1,3},{2,0},{3,1},{4,6},{5,7},{6,4},{7,5},{8,10},{9,11},{10,... | collective-permute-start | bytes 196616 | tf_op jit(solution)/shard_map/ppermute | solution.py:230
  23.1 0.5 %collective-permute-start.9 = (f32[128,128]{1,0:T(8,128)S(1)}, f32[128,128]{1,0:T(8,128)S(1)}, u32[]{:S(2)}, u32[]{:S(2)}) collective-permute-start(f32[128,128]{1,0:T(8,128)S(1)} %get-tuple-element.29), channel_id=1, source_target_pairs={{0,2},{1,3},{2,0},{3,1},{4,6},{5,7},{6,4},{7,5},{8,10},{9,11},{10,... | collective-permute-start | bytes 196616 | tf_op jit(solution)/shard_map/ppermute | solution.py:230
  23.7 2.6 %collective-permute-done.8.refs_1_ = f32[128,128]{1,0:T(8,128)S(1)} collective-permute-done((f32[128,128]{1,0:T(8,128)S(1)}, f32[128,128]{1,0:T(8,128)S(1)}, u32[]{:S(2)}, u32[]{:S(2)}) %collective-permute-start.8) | collective-permute-done | bytes 65568 | tf_op jit(solution)/shard_map/ppermute | solution.py:230
  26.3 3.1 %shard_map.56.inverse_ref = f32[128,128]{1,0:T(8,128)S(1)} custom-call(f32[128,128]{1,0:T(8,128)S(1)} %get-tuple-element.17.time_gram_ref, f32[128,128]{1,0:T(8,128)S(1)} %get-tuple-element.27.refs_0_, f32[128,128]{1,0:T(8,128)S(1)} %collective-permute-done.8.refs_1_), custom_call_target="tpu_custom_call" | custom-call | tf_op jit(solution)/shard_map/pallas_call | solution.py:234
  29.4 0.0 collective-permute-done.9.refs_1_
  29.5 0.2 shard_map.57
  29.7 11.7 %all_to_all.9 = f32[32,1,128]{2,1,0:T(1,128)S(1)} all-to-all(f32[32,1,128]{2,1,0:T(1,128)S(1)} %bitcast.3), channel_id=1, replica_groups=mesh['row'=8,'col'=4] {'row','col'}, dimensions={0} | all-to-all | bytes 32768 | tf_op jit(solution)/shard_map/all_to_all | solution.py:311
  41.4 0.1 reduce_sum.9
  41.4 0.6 %broadcast_divide_fusion = f32[128,128]{1,0:T(8,128)} fusion(f32[128,128]{1,0:T(8,128)S(1)} %get-tuple-element.30, f32[128]{0:T(128)S(1)} %add_sqrt_fusion), kind=kLoop, calls=%fused_computation | loop fusion | flops 16384 | bytes 131584 | tf_op jit(solution)/shard_map/div | solution.py:313
  (6 shorter events, 0.1 us)
Async XLA Ops:
  0.6 0.9 %copy-start = (f32[256,128]{1,0:T(8,128)S(1)}, f32[256,128]{1,0:T(8,128)}, u32[]{:S(2)}) copy-start(f32[256,128]{1,0:T(8,128)} %factor_ref.1) | copy-start | bytes 393220
  1.9 8.5 %collective-permute-start.3 = (bf16[336,128]{1,0:T(8,128)(2,1)S(1)}, bf16[336,128]{1,0:T(8,128)(2,1)S(1)}, u32[]{:S(2)}, u32[]{:S(2)}) collective-permute-start(bf16[336,128]{1,0:T(8,128)(2,1)S(1)} %get-tuple-element.20), channel_id=1, source_target_pairs={{0,16},{4,20},{8,24},{12,28},{16,0},{20,4},{24,8},{28,12},{1,17},{... | collective-permute-start | bytes 258056 | tf_op jit(solution)/shard_map/ppermute | solution.py:230
  5.9 7.6 %collective-permute-start = (bf16[336,128]{1,0:T(8,128)(2,1)S(1)}, bf16[336,128]{1,0:T(8,128)(2,1)S(1)}, u32[]{:S(2)}, u32[]{:S(2)}) collective-permute-start(bf16[336,128]{1,0:T(8,128)(2,1)S(1)} %get-tuple-element.20), channel_id=1, source_target_pairs={{0,4},{4,0},{8,12},{12,8},{16,20},{20,16},{24,28},{28,24},{1,5},{5... | collective-permute-start | bytes 258056 | tf_op jit(solution)/shard_map/ppermute | solution.py:230
  7.5 6.5 %collective-permute-start.1 = (bf16[336,128]{1,0:T(8,128)(2,1)S(1)}, bf16[336,128]{1,0:T(8,128)(2,1)S(1)}, u32[]{:S(2)}, u32[]{:S(2)}) collective-permute-start(bf16[336,128]{1,0:T(8,128)(2,1)S(1)} %get-tuple-element.20), channel_id=1, source_target_pairs={{0,8},{4,12},{8,0},{12,4},{16,24},{20,28},{24,16},{28,20},{1,9},{5... | collective-permute-start | bytes 258056 | tf_op jit(solution)/shard_map/ppermute | solution.py:230
  9.0 5.9 %collective-permute-start.2 = (bf16[336,128]{1,0:T(8,128)(2,1)S(1)}, bf16[336,128]{1,0:T(8,128)(2,1)S(1)}, u32[]{:S(2)}, u32[]{:S(2)}) collective-permute-start(bf16[336,128]{1,0:T(8,128)(2,1)S(1)} %get-tuple-element.20), channel_id=1, source_target_pairs={{0,12},{4,8},{8,4},{12,0},{16,28},{20,24},{24,20},{28,16},{1,13},{... | collective-permute-start | bytes 258056 | tf_op jit(solution)/shard_map/ppermute | solution.py:230
  9.4 0.7 %copy-start.1 = (f32[4,128]{1,0:T(4,128)S(1)}, f32[4,128]{1,0:T(4,128)}, u32[]{:S(2)}) copy-start(f32[4,128]{1,0:T(4,128)} %time_ref.1) | copy-start | bytes 6148
  10.4 8.2 %collective-permute-start.4 = (bf16[336,128]{1,0:T(8,128)(2,1)S(1)}, bf16[336,128]{1,0:T(8,128)(2,1)S(1)}, u32[]{:S(2)}, u32[]{:S(2)}) collective-permute-start(bf16[336,128]{1,0:T(8,128)(2,1)S(1)} %shard_map.52.refs_4_), channel_id=1, source_target_pairs={{0,4},{4,0},{8,12},{12,8},{16,20},{20,16},{24,28},{28,24},{1,5},{5... | collective-permute-start | bytes 258056 | tf_op jit(solution)/shard_map/ppermute | solution.py:230
  12.0 6.7 %collective-permute-start.5 = (bf16[336,128]{1,0:T(8,128)(2,1)S(1)}, bf16[336,128]{1,0:T(8,128)(2,1)S(1)}, u32[]{:S(2)}, u32[]{:S(2)}) collective-permute-start(bf16[336,128]{1,0:T(8,128)(2,1)S(1)} %shard_map.52.refs_4_), channel_id=1, source_target_pairs={{0,8},{4,12},{8,0},{12,4},{16,24},{20,28},{24,16},{28,20},{1,9},{5... | collective-permute-start | bytes 258056 | tf_op jit(solution)/shard_map/ppermute | solution.py:230
  13.6 5.4 %collective-permute-start.6 = (bf16[336,128]{1,0:T(8,128)(2,1)S(1)}, bf16[336,128]{1,0:T(8,128)(2,1)S(1)}, u32[]{:S(2)}, u32[]{:S(2)}) collective-permute-start(bf16[336,128]{1,0:T(8,128)(2,1)S(1)} %shard_map.52.refs_4_), channel_id=1, source_target_pairs={{0,12},{4,8},{8,4},{12,0},{16,28},{20,24},{24,20},{28,16},{1,13},{... | collective-permute-start | bytes 258056 | tf_op jit(solution)/shard_map/ppermute | solution.py:230
  20.0 1.5 %collective-permute-start.7 = (f32[384,128]{1,0:T(8,128)S(1)}, f32[384,128]{1,0:T(8,128)S(1)}, u32[]{:S(2)}, u32[]{:S(2)}) collective-permute-start(f32[384,128]{1,0:T(8,128)S(1)} %get-tuple-element.26.sent_ref), channel_id=1, source_target_pairs={{0,1},{1,0},{2,3},{3,2},{4,5},{5,4},{6,7},{7,6},{8,9},{9,8},{10,11... | collective-permute-start | bytes 589832 | tf_op jit(solution)/shard_map/ppermute | solution.py:230
  21.6 4.7 %collective-permute-start.8 = (f32[128,128]{1,0:T(8,128)S(1)}, f32[128,128]{1,0:T(8,128)S(1)}, u32[]{:S(2)}, u32[]{:S(2)}) collective-permute-start(f32[128,128]{1,0:T(8,128)S(1)} %get-tuple-element.27.refs_0_), channel_id=1, source_target_pairs={{0,2},{1,3},{2,0},{3,1},{4,6},{5,7},{6,4},{7,5},{8,10},{9,11},{10,... | collective-permute-start | bytes 196616 | tf_op jit(solution)/shard_map/ppermute | solution.py:230
  23.1 6.3 %collective-permute-start.9 = (f32[128,128]{1,0:T(8,128)S(1)}, f32[128,128]{1,0:T(8,128)S(1)}, u32[]{:S(2)}, u32[]{:S(2)}) collective-permute-start(f32[128,128]{1,0:T(8,128)S(1)} %get-tuple-element.29), channel_id=1, source_target_pairs={{0,2},{1,3},{2,0},{3,1},{4,6},{5,7},{6,4},{7,5},{8,10},{9,11},{10,... | collective-permute-start | bytes 196616 | tf_op jit(solution)/shard_map/ppermute | solution.py:230
  41.4 0.7 %copy-start.2 = (f32[128]{0:T(128)}, f32[128]{0:T(128)S(1)}, u32[]{:S(2)}) copy-start(f32[128]{0:T(128)S(1)} %add_sqrt_fusion) | copy-start | bytes 1540

commit v5 on v4

--- a/solution.py
+++ b/solution.py
@@ -67,7 +67,23 @@
         ref[rows:, :] = rest
 
 
-def time_kernel(time_ref, out_ref, gram_ref):
+def start_loads(owners, depth, tensor_ref, slots_ref, sems):
+    row = lax.axis_index("row")
+    arrivals = []
+    for at, owner in enumerate(owners):
+        start = pl.multiple_of(lax.bitwise_xor(row, owner) * depth, depth)
+        arrivals.append(
+            pltpu.make_async_copy(
+                tensor_ref.at[:, :, pl.ds(start, depth)], slots_ref.at[at], sems.at[at]
+            )
+        )
+    for arrival in arrivals:
+        arrival.start()
+    return arrivals
+
+
+def load_kernel(owners, depth, tensor_ref, time_ref, out_ref, gram_ref, slots_ref, sems):
+    arrivals = start_loads(owners, depth, tensor_ref, slots_ref, sems)
     time = time_ref[...]
     out_ref[...] = time
     gram_ref[...] = lax.dot_general(
@@ -77,6 +93,8 @@
         precision=lax.Precision.HIGHEST,
         preferred_element_type=F32,
     )
+    for arrival in arrivals:
+        arrival.wait()
 
 
 def relay_kernel(ready_ref, part_ref, out_ref):
@@ -90,50 +108,57 @@
         low = part[:depth, :]
         gram = gram + tdot(low, low)
         rest = rest + part[depth:, :].astype(F32)
-    return gram, rest
+    return packed(gram) + rest
 
 
 def multiply(blocks, time_ref, parts, depth):
     snaps = time_ref.shape[0]
     total = [0.0] * snaps
-    for (block, arrival), part in zip(blocks, parts):
-        if arrival is not None:
-            arrival.wait()
-        low = part[:depth, :]
+    for block, part in zip(blocks, parts):
         for snap in range(snaps):
             total[snap] = total[snap] + jnp.dot(
-                block[snap], low, preferred_element_type=F32
+                block[snap], part[:depth, :], preferred_element_type=F32
             )
     return sum(total[snap] * time_ref[snap : snap + 1, :] for snap in range(snaps))
 
 
-def first_kernel(owners, depth, tensor_ref, time_ref, *refs):
-    count = len(refs) - 6
-    parts, (result_ref, gram_ref, rest_ref, later_ref, slots, sems) = refs[:count], refs[count:]
-    row = lax.axis_index("row")
-    blocks = []
-    for at, owner in enumerate(owners):
-        block = slots.at[at] if at < count else later_ref.at[at - count]
-        start = pl.multiple_of(lax.bitwise_xor(row, owner) * depth, depth)
-        arrival = pltpu.make_async_copy(
-            tensor_ref.at[:, :, pl.ds(start, depth)], block, sems.at[at]
-        )
-        arrival.start()
-        blocks.append((block, arrival))
-    gram_ref[...], rest_ref[...] = gram_of(parts, depth)
-    result_ref[...] = multiply(blocks[:count], time_ref, parts, depth)
-    for _, arrival in blocks[count:]:
+def first_kernel(owners, depth, tensor_ref, time_ref, early_ref, *refs):
+    parts, (result_ref, gram_ref, later_ref, sems) = refs[:-4], refs[-4:]
+    arrivals = start_loads(owners, depth, tensor_ref, later_ref, sems)
+    begin = early_ref.shape[0]
+    result_ref[...] = jnp.zeros(result_ref.shape, F32)
+
+    @pl.loop(0, time_ref.shape[0])
+    def _(snap):
+        total = 0.0
+        for at in range(begin):
+            total = total + jnp.dot(
+                early_ref[at, snap], parts[at][:depth, :], preferred_element_type=F32
+            )
+        result_ref[...] += total * time_ref[pl.ds(snap, 1), :]
+
+    gram_ref[...] = gram_of(parts, depth)
+    for at, arrival in enumerate(arrivals):
         arrival.wait()
-
-
-def last_kernel(depth, time_ref, result_ref, gram_ref, rest_ref, *refs):
-    parts, (later_ref, keep_ref, send_ref) = refs[:-3], refs[-3:]
+        if begin + at < len(parts):
+            result_ref[...] += multiply([later_ref.at[at]], time_ref, [parts[begin + at]], depth)
+
+
+def middle_kernel(depth, places, time_ref, later_ref, result_ref, gram_ref, *refs):
+    parts, (result_out_ref, gram_out_ref) = refs[:-2], refs[-2:]
+    blocks = [later_ref.at[at] for at in places]
+    result_out_ref[...] = result_ref[...] + multiply(blocks, time_ref, parts, depth)
+    gram_out_ref[...] = gram_ref[...] + gram_of(parts, depth)
+
+
+def last_kernel(depth, places, time_ref, later_ref, result_ref, gram_ref, *refs):
+    parts, (keep_ref, send_ref) = refs[:-2], refs[-2:]
     col, cols = lax.axis_index("col"), lax.axis_size("col")
-    result = result_ref[...]
-    gram, rest = gram_of(parts, depth)
+    result, gram = result_ref[...], gram_ref[...]
     if parts:
-        blocks = [(later_ref.at[at], None) for at in range(len(parts))]
+        blocks = [later_ref.at[at] for at in places]
         result = result + multiply(blocks, time_ref, parts, depth)
+        gram = gram + gram_of(parts, depth)
     piece = result.shape[0] // cols
     core = lax.rem(col, 2)
     for pair in range(cols // 2):
@@ -141,16 +166,17 @@
         odd = result[(2 * pair + 1) * piece : (2 * pair + 2) * piece, :]
         keep_ref[pair * piece : (pair + 1) * piece, :] = jnp.where(core == 0, even, odd)
         send_ref[pair * piece : (pair + 1) * piece, :] = jnp.where(core == 0, odd, even)
-    send_ref[(cols // 2) * piece :, :] = gram_ref[...] + gram + unpacked(rest_ref[...] + rest)
-
-
-def chip_kernel(piece, keep_ref, sent_ref, got_ref, gram_ref, *out_refs):
+    send_ref[(cols // 2) * piece :, :] = gram
+
+
+def chip_kernel(piece, keep_ref, sent_ref, got_ref, *out_refs):
+    place = lax.div(lax.axis_index("col"), 2)
     held = keep_ref.shape[0]
-    gram_ref[...] = sent_ref[held:, :] + got_ref[held:, :]
-    place = lax.div(lax.axis_index("col"), 2)
+    gram = sent_ref[held:, :] + got_ref[held:, :]
     for offset, out_ref in enumerate(out_refs):
         start = pl.multiple_of(lax.bitwise_xor(place, offset) * piece, piece)
-        out_ref[...] = keep_ref[pl.ds(start, piece), :] + got_ref[pl.ds(start, piece), :]
+        out_ref[:piece, :] = keep_ref[pl.ds(start, piece), :] + got_ref[pl.ds(start, piece), :]
+        out_ref[piece:, :] = gram
 
 
 def negative_inverse(matrix):
@@ -207,17 +233,14 @@
     return matrix
 
 
-def inverse_kernel(time_gram_ref, *refs):
-    grams, inverse_ref = refs[:-1], refs[-1]
-    gram = sum(ref[...] for ref in grams)
-    inverse_ref[...] = negative_inverse(gram * time_gram_ref[...])
-
-
-def solve_kernel(inverse_ref, *refs):
+def solve_kernel(time_gram_ref, *refs):
     sums, (solved_ref, squares_ref) = refs[:-2], refs[-2:]
+    piece = solved_ref.shape[0]
+    total = sum(ref[...] for ref in sums)
+    inverse = negative_inverse(unpacked(total[piece:, :]) * time_gram_ref[...])
     solved = -jnp.dot(
-        sum(ref[...] for ref in sums),
-        inverse_ref[...],
+        total[:piece, :],
+        inverse,
         precision=lax.Precision.HIGHEST,
         preferred_element_type=F32,
     )
@@ -230,7 +253,7 @@
     return lax.ppermute(value, axis, [(at, at ^ offset) for at in range(groups)])
 
 
-def call(kernel, operands, in_specs, outs, scratch=(), room=40):
+def call(kernel, operands, in_specs, outs, scratch=(), room=24):
     return pl.pallas_call(
         kernel,
         out_shape=tuple(jax.ShapeDtypeStruct(shape, dtype) for shape, dtype in outs),
@@ -255,56 +278,66 @@
     near = range(1, half)
     opposite = shifted(message, "row", half, rows)
     arrived = {at: shifted(message, "row", at, rows) for at in near}
-    time, time_gram = call(
-        time_kernel, (time_factor,), [VMEM], [((snaps, rank), F32), ((rank, rank), F32)]
+    in_hbm = pltpu.with_memory_space_constraint(tensor, pltpu.HBM)
+    direct = depth % 128 == 0
+    owners, width = (list(range(rows)), depth) if direct else ([0], own_cols)
+    block = (snaps, own_rows, width)
+    begin, split = (half, half + 1) if direct else (1, 1)
+    time, time_gram, early = call(
+        functools.partial(load_kernel, owners[:begin], width),
+        (in_hbm, time_factor),
+        [HBM, VMEM],
+        [((snaps, rank), F32), ((rank, rank), F32), ((begin, *block), BF16)],
+        [pltpu.SemaphoreType.DMA((begin,))],
     )
     (opposite,) = call(relay_kernel, (time, opposite), [VMEM] * 2, [whole])
     arrived[0], arrived[half] = own, opposite
     for at in near:
         arrived[half + at] = shifted(opposite, "row", at, rows)
 
-    if depth % 128 == 0:
-        owners, width, split = list(range(rows)), depth, half + 1
+    if direct:
         parts = [arrived[at] for at in range(rows)]
     else:
-        owners, width, split = [0], own_cols, 1
         row = lax.axis_index("row")
         low = jnp.stack([arrived[at][:depth] for at in range(rows)])
         low = low[jnp.arange(rows) ^ row].reshape(rows * depth, rank)
         rest = sum(arrived[at][depth:].astype(F32) for at in range(rows)).astype(BF16)
         parts = [jnp.concatenate([low, rest], 0)]
-    square = ((rank, rank), F32)
-    block = (snaps, own_rows, width)
-    later = max(len(owners) - split, 1)
-    result, gram, rest, tensor_later = call(
-        functools.partial(first_kernel, owners, width),
-        (tensor, time, *parts[:split]),
-        [HBM] + [VMEM] * (1 + split),
-        [((own_rows, rank), F32), square, ((pack, rank), F32), ((later, *block), BF16)],
-        [pltpu.VMEM((split, *block), BF16), pltpu.SemaphoreType.DMA((len(owners),))],
-        room=48,
-    )
+    later = max(len(owners) - begin, 1)
+    sums = [((own_rows, rank), F32), ((pack, rank), F32)]
+    result, gram, tensor_later = call(
+        functools.partial(first_kernel, owners[begin:], width),
+        (in_hbm, time, early, *parts[:split]),
+        [HBM] + [VMEM] * (2 + split),
+        sums + [((later, *block), BF16)],
+        [pltpu.SemaphoreType.DMA((later,))],
+    )
+    if len(parts) > split + 1:
+        middle = parts[split:-1]
+        result, gram = call(
+            functools.partial(middle_kernel, width, range(split - begin, later - 1)),
+            (time, tensor_later, result, gram, *middle),
+            [VMEM] * (4 + len(middle)),
+            sums,
+        )
+    last = parts[split:][-1:]
     keep, send = call(
-        functools.partial(last_kernel, width),
-        (time, result, gram, rest, *parts[split:], tensor_later),
-        [VMEM] * (5 + len(parts) - split),
-        [((pairs * piece, rank), F32), ((pairs * piece + rank, rank), F32)],
-    )
-
-    chip_gram, own_sum, *outs = call(
+        functools.partial(last_kernel, width, [later - 1]),
+        (time, tensor_later, result, gram, *last),
+        [VMEM] * (4 + len(last)),
+        [((pairs * piece, rank), F32), ((pairs * piece + pack, rank), F32)],
+    )
+
+    total, *outs = call(
         functools.partial(chip_kernel, piece),
         (keep, send, shifted(send, "col", 1, cols)),
         [VMEM] * 3,
-        [((rank, rank), F32)] + [((piece, rank), F32)] * pairs,
-    )
-    grams = [chip_gram] + [shifted(chip_gram, "col", 2 * at, cols) for at in range(1, pairs)]
-    sums = [own_sum] + [shifted(out, "col", 2 * (at + 1), cols) for at, out in enumerate(outs)]
-    (inverse,) = call(
-        inverse_kernel, (time_gram, *grams), [VMEM] * (1 + pairs), [((rank, rank), F32)]
-    )
+        [((piece + pack, rank), F32)] * pairs,
+    )
+    totals = [total] + [shifted(out, "col", 2 * (at + 1), cols) for at, out in enumerate(outs)]
     solved, squares = call(
         solve_kernel,
-        (inverse, *sums),
+        (time_gram, *totals),
         [VMEM] * (1 + pairs),
         [((piece, rank), F32), ((rows * cols, rank), F32)],
     )

time: 42.3 us -> 42 us (level)
  blocking collectives: 11.7 us -> 9.53 us
  Pallas kernels: 8.69 us -> 10.1 us
  waiting for transfers between devices: 5.4 us -> 6.44 us
  starting transfers between devices: 13.3 us -> 12.7 us
    all_to_all x1, blocking collectives: 11.7 us -> 9.53 us  [per_device(): squares = lax.all_to_all(squares, ('row', 'col'), 0, 0, tiled=True)]
    pallas_call x8, Pallas kernels: 8.69 us -> 10.1 us  [call(): pl.pallas_call(kernel, out_shape=tuple((jax.ShapeDtypeStruct(shape, dtype...]
    ppermute x10 -> x9, waiting for transfers between devices: 5.4 us -> 6.44 us  [shifted(): lax.ppermute(value, axis, [(at, at ^ offset) for at in range(groups)])]
    ppermute x10 -> x9, starting transfers between devices: 13.3 us -> 12.7 us  [shifted(): lax.ppermute(value, axis, [(at, at ^ offset) for at in range(groups)])]
  transfers between devices with their start and end apart: 10 -> 9, of which waited for: 4 -> 3; matrix products, arithmetic and copies ran while one was open for 0% -> 0% of each run, Pallas kernels for 17% -> 14%
where the time goes in v5:
time: 42 us; the launch traced here: 41.8 us
  starting transfers between devices  12.7 us (30%)
  Pallas kernels  10.1 us (24%)
  blocking collectives  9.53 us (23%)
  waiting for transfers between devices  6.44 us (15%)
  local copies, waits for them, and re-layouts  1.58 us (4%)
  between operations  0.72 us (2%)
  other arithmetic  0.7 us (2%)
    ppermute x9, starting transfers between devices, shifted(): lax.ppermute(value, axis, [(at, at ^ offset) for at in range(groups)])  12.7 us
    pallas_call x8, Pallas kernels, call(): pl.pallas_call(kernel, out_shape=tuple((jax.ShapeDtypeStruct(shape, dtype...  10.1 us
    all_to_all x1, blocking collectives, per_device(): squares = lax.all_to_all(squares, ('row', 'col'), 0, 0, tiled=True)  9.53 us
    ppermute x9, waiting for transfers between devices, shifted(): lax.ppermute(value, axis, [(at, at ^ offset) for at in range(groups)])  6.44 us
    unnamed x6, local copies, waits for them, and re-layouts  1.58 us
  transfers between devices with their start and end apart: 9, of which 3 were waited for; matrix products, arithmetic and copies ran while one was open for 0% of the time, Pallas kernels for 14%

profile of v5, /device:TPU:0, one launch (start us, length us, event | category | flops | bytes accessed | tf_op | source)
XLA Modules:
  0.0 41.8 jit_solution(10568704754290820572)
XLA Ops:
  0.6 0.0 copy-start
  0.6 0.9 %copy-done = f32[256,128]{1,0:T(8,128)S(1)} copy-done((f32[256,128]{1,0:T(8,128)S(1)}, f32[256,128]{1,0:T(8,128)}, u32[]{:S(2)}) %copy-start) | copy-done | bytes 131096
  1.5 0.3 shard_map.51
  1.9 4.1 %collective-permute-start.3 = (bf16[336,128]{1,0:T(8,128)(2,1)S(1)}, bf16[336,128]{1,0:T(8,128)(2,1)S(1)}, u32[]{:S(2)}, u32[]{:S(2)}) collective-permute-start(bf16[336,128]{1,0:T(8,128)(2,1)S(1)} %get-tuple-element.22), channel_id=1, source_target_pairs={{0,16},{4,20},{8,24},{12,28},{16,0},{20,4},{24,8},{28,12},{1,17},{... | collective-permute-start | bytes 258056 | tf_op jit(solution)/shard_map/ppermute | solution.py:253
  5.9 1.5 %collective-permute-start = (bf16[336,128]{1,0:T(8,128)(2,1)S(1)}, bf16[336,128]{1,0:T(8,128)(2,1)S(1)}, u32[]{:S(2)}, u32[]{:S(2)}) collective-permute-start(bf16[336,128]{1,0:T(8,128)(2,1)S(1)} %get-tuple-element.22), channel_id=1, source_target_pairs={{0,4},{4,0},{8,12},{12,8},{16,20},{20,16},{24,28},{28,24},{1,5},{5... | collective-permute-start | bytes 258056 | tf_op jit(solution)/shard_map/ppermute | solution.py:253
  7.5 1.6 %collective-permute-start.1 = (bf16[336,128]{1,0:T(8,128)(2,1)S(1)}, bf16[336,128]{1,0:T(8,128)(2,1)S(1)}, u32[]{:S(2)}, u32[]{:S(2)}) collective-permute-start(bf16[336,128]{1,0:T(8,128)(2,1)S(1)} %get-tuple-element.22), channel_id=1, source_target_pairs={{0,8},{4,12},{8,0},{12,4},{16,24},{20,28},{24,16},{28,20},{1,9},{5... | collective-permute-start | bytes 258056 | tf_op jit(solution)/shard_map/ppermute | solution.py:253
  9.0 0.4 collective-permute-start.2
  9.4 0.0 copy-start.1
  9.4 0.7 %copy-done.1 = f32[4,128]{1,0:T(4,128)S(1)} copy-done((f32[4,128]{1,0:T(4,128)S(1)}, f32[4,128]{1,0:T(4,128)}, u32[]{:S(2)}) %copy-start.1) | copy-done | bytes 2072
  10.1 2.3 %shard_map.50 = (f32[4,128]{1,0:T(4,128)S(1)}, f32[128,128]{1,0:T(8,128)S(1)}, bf16[4,4,512,256]{3,2,1,0:T(8,128)(2,1)S(1)}) custom-call(bf16[4,512,2048]{2,1,0:T(8,128)(2,1)} %tensor_ref.3, f32[4,128]{1,0:T(4,128)S(1)} %copy-done.1), custom_call_target="tpu_custom_call" | custom-call | tf_op jit(solution)/shard_map/pallas_call | solution.py:257
  12.4 0.0 collective-permute-done.3.part_ref
  12.4 1.6 %collective-permute-start.4 = (bf16[336,128]{1,0:T(8,128)(2,1)S(1)}, bf16[336,128]{1,0:T(8,128)(2,1)S(1)}, u32[]{:S(2)}, u32[]{:S(2)}) collective-permute-start(bf16[336,128]{1,0:T(8,128)(2,1)S(1)} %shard_map.52.refs_4_), channel_id=1, source_target_pairs={{0,4},{4,0},{8,12},{12,8},{16,20},{20,16},{24,28},{28,24},{1,5},{5... | collective-permute-start | bytes 258056 | tf_op jit(solution)/shard_map/ppermute | solution.py:253
  14.0 1.6 %collective-permute-start.5 = (bf16[336,128]{1,0:T(8,128)(2,1)S(1)}, bf16[336,128]{1,0:T(8,128)(2,1)S(1)}, u32[]{:S(2)}, u32[]{:S(2)}) collective-permute-start(bf16[336,128]{1,0:T(8,128)(2,1)S(1)} %shard_map.52.refs_4_), channel_id=1, source_target_pairs={{0,8},{4,12},{8,0},{12,4},{16,24},{20,28},{24,16},{28,20},{1,9},{5... | collective-permute-start | bytes 258056 | tf_op jit(solution)/shard_map/ppermute | solution.py:253
  15.6 0.0 collective-permute-done.refs_1_
  15.6 0.4 collective-permute-start.6
  16.0 0.0 collective-permute-done.1.refs_2_
  16.0 0.0 collective-permute-done.2.refs_3_
  16.0 2.6 %shard_map.53 = (f32[512,128]{1,0:T(8,128)S(1)}, f32[80,128]{1,0:T(8,128)S(1)}, bf16[4,4,512,256]{3,2,1,0:T(8,128)(2,1)S(1)}) custom-call(bf16[4,512,2048]{2,1,0:T(8,128)(2,1)} %tensor_ref.3, f32[4,128]{1,0:T(4,128)S(1)} %get-tuple-element.19.ready_ref.time_ref, bf16[4,4,512,256]{3,2,1,0:T(8,128)(2,1)S(1)} %get-tuple-element.20.early_ref, ...), custom_call_target="tpu_custom_call" | custom-call | tf_op jit(solution)/shard_map/pallas_call | solution.py:257
  18.6 0.0 collective-permute-done.4.refs_0_
  18.6 0.0 collective-permute-done.5.refs_1_
  18.6 0.8 %shard_map.54 = (f32[512,128]{1,0:T(8,128)S(1)}, f32[80,128]{1,0:T(8,128)S(1)}) custom-call(f32[4,128]{1,0:T(4,128)S(1)} %get-tuple-element.19.ready_ref.time_ref, bf16[4,4,512,256]{3,2,1,0:T(8,128)(2,1)S(1)} %get-tuple-element.23.later_ref, f32[512,128]{1,0:T(8,128)S(1)} %get-tuple-element.24.result_ref, f32[80,128]{1,0:T(8,128)S(1)} %get-tuple-element.25.gram_ref, ...), custom_call_target="tpu_custom_call" | custom-call | tf_op jit(solution)/shard_map/pallas_call | solution.py:257
  19.4 1.5 %collective-permute-done.6.refs_0_ = bf16[336,128]{1,0:T(8,128)(2,1)S(1)} collective-permute-done((bf16[336,128]{1,0:T(8,128)(2,1)S(1)}, bf16[336,128]{1,0:T(8,128)(2,1)S(1)}, u32[]{:S(2)}, u32[]{:S(2)}) %collective-permute-start.6) | collective-permute-done | bytes 86048 | tf_op jit(solution)/shard_map/ppermute | solution.py:253
  21.0 0.5 %shard_map.55 = (f32[256,128]{1,0:T(8,128)S(1)}, f32[336,128]{1,0:T(8,128)S(1)}) custom-call(f32[4,128]{1,0:T(4,128)S(1)} %get-tuple-element.19.ready_ref.time_ref, bf16[4,4,512,256]{3,2,1,0:T(8,128)(2,1)S(1)} %get-tuple-element.23.later_ref, f32[512,128]{1,0:T(8,128)S(1)} %get-tuple-element.26.result_ref, f32[80,128]{1,0:T(8,128)S(1)} %get-tuple-element.27.gram_ref, ...), custom_call_target="tpu_custom_call" | custom-call | tf_op jit(solution)/shard_map/pallas_call | solution.py:257
  21.5 0.1 collective-permute-start.7
  21.6 1.4 %collective-permute-done.7.got_ref = f32[336,128]{1,0:T(8,128)S(1)} collective-permute-done((f32[336,128]{1,0:T(8,128)S(1)}, f32[336,128]{1,0:T(8,128)S(1)}, u32[]{:S(2)}, u32[]{:S(2)}) %collective-permute-start.7) | collective-permute-done | bytes 172064 | tf_op jit(solution)/shard_map/ppermute | solution.py:253
  23.0 1.6 %collective-permute-start.8 = (f32[208,128]{1,0:T(8,128)S(1)}, f32[208,128]{1,0:T(8,128)S(1)}, u32[]{:S(2)}, u32[]{:S(2)}) collective-permute-start(f32[208,128]{1,0:T(8,128)S(1)} %get-tuple-element.31), channel_id=1, source_target_pairs={{0,2},{1,3},{2,0},{3,1},{4,6},{5,7},{6,4},{7,5},{8,10},{9,11},{10,... | collective-permute-start | bytes 319496 | tf_op jit(solution)/shard_map/ppermute | solution.py:253
  24.5 3.5 %collective-permute-done.8.refs_1_ = f32[208,128]{1,0:T(8,128)S(1)} collective-permute-done((f32[208,128]{1,0:T(8,128)S(1)}, f32[208,128]{1,0:T(8,128)S(1)}, u32[]{:S(2)}, u32[]{:S(2)}) %collective-permute-start.8) | collective-permute-done | bytes 106528 | tf_op jit(solution)/shard_map/ppermute | solution.py:253
  28.1 3.5 %shard_map.57 = (f32[128,128]{1,0:T(8,128)S(1)}, f32[32,128]{1,0:T(8,128)S(1)}) custom-call(f32[128,128]{1,0:T(8,128)S(1)} %get-tuple-element.18.time_gram_ref, f32[208,128]{1,0:T(8,128)S(1)} %get-tuple-element.30.refs_0_, f32[208,128]{1,0:T(8,128)S(1)} %collective-permute-done.8.refs_1_), custom_call_target="tpu_custom_call" | custom-call | tf_op jit(solution)/shard_map/pallas_call | solution.py:257
  31.6 9.5 %all_to_all.9 = f32[32,1,128]{2,1,0:T(1,128)S(1)} all-to-all(f32[32,1,128]{2,1,0:T(1,128)S(1)} %bitcast.3), channel_id=1, replica_groups=mesh['row'=8,'col'=4] {'row','col'}, dimensions={0} | all-to-all | bytes 32768 | tf_op jit(solution)/shard_map/all_to_all | solution.py:344
  41.1 0.1 reduce_sum.9
  41.1 0.6 %broadcast_divide_fusion = f32[128,128]{1,0:T(8,128)} fusion(f32[128,128]{1,0:T(8,128)S(1)} %get-tuple-element.32, f32[128]{0:T(128)S(1)} %add_sqrt_fusion), kind=kLoop, calls=%fused_computation | loop fusion | flops 16384 | bytes 131584 | tf_op jit(solution)/shard_map/div | solution.py:346
  41.8 0.0 copy-done.2
  (4 shorter events, 0.0 us)
Async XLA Ops:
  0.6 0.9 %copy-start = (f32[256,128]{1,0:T(8,128)S(1)}, f32[256,128]{1,0:T(8,128)}, u32[]{:S(2)}) copy-start(f32[256,128]{1,0:T(8,128)} %factor_ref.1) | copy-start | bytes 393220
  1.9 10.5 %collective-permute-start.3 = (bf16[336,128]{1,0:T(8,128)(2,1)S(1)}, bf16[336,128]{1,0:T(8,128)(2,1)S(1)}, u32[]{:S(2)}, u32[]{:S(2)}) collective-permute-start(bf16[336,128]{1,0:T(8,128)(2,1)S(1)} %get-tuple-element.22), channel_id=1, source_target_pairs={{0,16},{4,20},{8,24},{12,28},{16,0},{20,4},{24,8},{28,12},{1,17},{... | collective-permute-start | bytes 258056 | tf_op jit(solution)/shard_map/ppermute | solution.py:253
  5.9 9.6 %collective-permute-start = (bf16[336,128]{1,0:T(8,128)(2,1)S(1)}, bf16[336,128]{1,0:T(8,128)(2,1)S(1)}, u32[]{:S(2)}, u32[]{:S(2)}) collective-permute-start(bf16[336,128]{1,0:T(8,128)(2,1)S(1)} %get-tuple-element.22), channel_id=1, source_target_pairs={{0,4},{4,0},{8,12},{12,8},{16,20},{20,16},{24,28},{28,24},{1,5},{5... | collective-permute-start | bytes 258056 | tf_op jit(solution)/shard_map/ppermute | solution.py:253
  7.5 8.5 %collective-permute-start.1 = (bf16[336,128]{1,0:T(8,128)(2,1)S(1)}, bf16[336,128]{1,0:T(8,128)(2,1)S(1)}, u32[]{:S(2)}, u32[]{:S(2)}) collective-permute-start(bf16[336,128]{1,0:T(8,128)(2,1)S(1)} %get-tuple-element.22), channel_id=1, source_target_pairs={{0,8},{4,12},{8,0},{12,4},{16,24},{20,28},{24,16},{28,20},{1,9},{5... | collective-permute-start | bytes 258056 | tf_op jit(solution)/shard_map/ppermute | solution.py:253
  9.0 6.9 %collective-permute-start.2 = (bf16[336,128]{1,0:T(8,128)(2,1)S(1)}, bf16[336,128]{1,0:T(8,128)(2,1)S(1)}, u32[]{:S(2)}, u32[]{:S(2)}) collective-permute-start(bf16[336,128]{1,0:T(8,128)(2,1)S(1)} %get-tuple-element.22), channel_id=1, source_target_pairs={{0,12},{4,8},{8,4},{12,0},{16,28},{20,24},{24,20},{28,16},{1,13},{... | collective-permute-start | bytes 258056 | tf_op jit(solution)/shard_map/ppermute | solution.py:253
  9.4 0.7 %copy-start.1 = (f32[4,128]{1,0:T(4,128)S(1)}, f32[4,128]{1,0:T(4,128)}, u32[]{:S(2)}) copy-start(f32[4,128]{1,0:T(4,128)} %time_ref.1) | copy-start | bytes 6148
  12.4 6.2 %collective-permute-start.4 = (bf16[336,128]{1,0:T(8,128)(2,1)S(1)}, bf16[336,128]{1,0:T(8,128)(2,1)S(1)}, u32[]{:S(2)}, u32[]{:S(2)}) collective-permute-start(bf16[336,128]{1,0:T(8,128)(2,1)S(1)} %shard_map.52.refs_4_), channel_id=1, source_target_pairs={{0,4},{4,0},{8,12},{12,8},{16,20},{20,16},{24,28},{28,24},{1,5},{5... | collective-permute-start | bytes 258056 | tf_op jit(solution)/shard_map/ppermute | solution.py:253
  14.0 4.6 %collective-permute-start.5 = (bf16[336,128]{1,0:T(8,128)(2,1)S(1)}, bf16[336,128]{1,0:T(8,128)(2,1)S(1)}, u32[]{:S(2)}, u32[]{:S(2)}) collective-permute-start(bf16[336,128]{1,0:T(8,128)(2,1)S(1)} %shard_map.52.refs_4_), channel_id=1, source_target_pairs={{0,8},{4,12},{8,0},{12,4},{16,24},{20,28},{24,16},{28,20},{1,9},{5... | collective-permute-start | bytes 258056 | tf_op jit(solution)/shard_map/ppermute | solution.py:253
  15.6 5.4 %collective-permute-start.6 = (bf16[336,128]{1,0:T(8,128)(2,1)S(1)}, bf16[336,128]{1,0:T(8,128)(2,1)S(1)}, u32[]{:S(2)}, u32[]{:S(2)}) collective-permute-start(bf16[336,128]{1,0:T(8,128)(2,1)S(1)} %shard_map.52.refs_4_), channel_id=1, source_target_pairs={{0,12},{4,8},{8,4},{12,0},{16,28},{20,24},{24,20},{28,16},{1,13},{... | collective-permute-start | bytes 258056 | tf_op jit(solution)/shard_map/ppermute | solution.py:253
  21.5 1.5 %collective-permute-start.7 = (f32[336,128]{1,0:T(8,128)S(1)}, f32[336,128]{1,0:T(8,128)S(1)}, u32[]{:S(2)}, u32[]{:S(2)}) collective-permute-start(f32[336,128]{1,0:T(8,128)S(1)} %get-tuple-element.29.sent_ref), channel_id=1, source_target_pairs={{0,1},{1,0},{2,3},{3,2},{4,5},{5,4},{6,7},{7,6},{8,9},{9,8},{10,11... | collective-permute-start | bytes 516104 | tf_op jit(solution)/shard_map/ppermute | solution.py:253
  23.0 5.1 %collective-permute-start.8 = (f32[208,128]{1,0:T(8,128)S(1)}, f32[208,128]{1,0:T(8,128)S(1)}, u32[]{:S(2)}, u32[]{:S(2)}) collective-permute-start(f32[208,128]{1,0:T(8,128)S(1)} %get-tuple-element.31), channel_id=1, source_target_pairs={{0,2},{1,3},{2,0},{3,1},{4,6},{5,7},{6,4},{7,5},{8,10},{9,11},{10,... | collective-permute-start | bytes 319496 | tf_op jit(solution)/shard_map/ppermute | solution.py:253
  41.1 0.7 %copy-start.2 = (f32[128]{0:T(128)}, f32[128]{0:T(128)S(1)}, u32[]{:S(2)}) copy-start(f32[128]{0:T(128)S(1)} %add_sqrt_fusion) | copy-start | bytes 1540

commit v6 on v5

--- a/solution.py
+++ b/solution.py
@@ -83,9 +83,11 @@
 
 
 def load_kernel(owners, depth, tensor_ref, time_ref, out_ref, gram_ref, slots_ref, sems):
+    time_arrival = pltpu.make_async_copy(time_ref, out_ref, sems.at[len(owners)])
+    time_arrival.start()
     arrivals = start_loads(owners, depth, tensor_ref, slots_ref, sems)
-    time = time_ref[...]
-    out_ref[...] = time
+    time_arrival.wait()
+    time = out_ref[...]
     gram_ref[...] = lax.dot_general(
         time,
         time,
@@ -125,38 +127,30 @@
 def first_kernel(owners, depth, tensor_ref, time_ref, early_ref, *refs):
     parts, (result_ref, gram_ref, later_ref, sems) = refs[:-4], refs[-4:]
     arrivals = start_loads(owners, depth, tensor_ref, later_ref, sems)
-    begin = early_ref.shape[0]
     result_ref[...] = jnp.zeros(result_ref.shape, F32)
 
     @pl.loop(0, time_ref.shape[0])
     def _(snap):
         total = 0.0
-        for at in range(begin):
+        for at, part in enumerate(parts):
             total = total + jnp.dot(
-                early_ref[at, snap], parts[at][:depth, :], preferred_element_type=F32
+                early_ref[at, snap], part[:depth, :], preferred_element_type=F32
             )
         result_ref[...] += total * time_ref[pl.ds(snap, 1), :]
 
     gram_ref[...] = gram_of(parts, depth)
-    for at, arrival in enumerate(arrivals):
+    for arrival in arrivals:
         arrival.wait()
-        if begin + at < len(parts):
-            result_ref[...] += multiply([later_ref.at[at]], time_ref, [parts[begin + at]], depth)
-
-
-def middle_kernel(depth, places, time_ref, later_ref, result_ref, gram_ref, *refs):
-    parts, (result_out_ref, gram_out_ref) = refs[:-2], refs[-2:]
-    blocks = [later_ref.at[at] for at in places]
-    result_out_ref[...] = result_ref[...] + multiply(blocks, time_ref, parts, depth)
-    gram_out_ref[...] = gram_ref[...] + gram_of(parts, depth)
-
-
-def last_kernel(depth, places, time_ref, later_ref, result_ref, gram_ref, *refs):
+
+
+def last_kernel(depth, time_ref, early_ref, later_ref, result_ref, gram_ref, *refs):
     parts, (keep_ref, send_ref) = refs[:-2], refs[-2:]
     col, cols = lax.axis_index("col"), lax.axis_size("col")
     result, gram = result_ref[...], gram_ref[...]
     if parts:
-        blocks = [later_ref.at[at] for at in places]
+        begin, later = early_ref.shape[0], later_ref.shape[0]
+        blocks = [early_ref.at[at] for at in range(begin)]
+        blocks = (blocks + [later_ref.at[at] for at in range(later)])[-len(parts) :]
         result = result + multiply(blocks, time_ref, parts, depth)
         gram = gram + gram_of(parts, depth)
     piece = result.shape[0] // cols
@@ -169,14 +163,13 @@
     send_ref[(cols // 2) * piece :, :] = gram
 
 
-def chip_kernel(piece, keep_ref, sent_ref, got_ref, *out_refs):
+def chip_kernel(piece, keep_ref, sent_ref, got_ref, gram_ref, *out_refs):
     place = lax.div(lax.axis_index("col"), 2)
     held = keep_ref.shape[0]
-    gram = sent_ref[held:, :] + got_ref[held:, :]
+    gram_ref[...] = sent_ref[held:, :] + got_ref[held:, :]
     for offset, out_ref in enumerate(out_refs):
         start = pl.multiple_of(lax.bitwise_xor(place, offset) * piece, piece)
-        out_ref[:piece, :] = keep_ref[pl.ds(start, piece), :] + got_ref[pl.ds(start, piece), :]
-        out_ref[piece:, :] = gram
+        out_ref[...] = keep_ref[pl.ds(start, piece), :] + got_ref[pl.ds(start, piece), :]
 
 
 def negative_inverse(matrix):
@@ -233,14 +226,17 @@
     return matrix
 
 
-def solve_kernel(time_gram_ref, *refs):
+def inverse_kernel(time_gram_ref, *refs):
+    grams, inverse_ref = refs[:-1], refs[-1]
+    gram = unpacked(sum(ref[...] for ref in grams))
+    inverse_ref[...] = negative_inverse(gram * time_gram_ref[...])
+
+
+def solve_kernel(inverse_ref, *refs):
     sums, (solved_ref, squares_ref) = refs[:-2], refs[-2:]
-    piece = solved_ref.shape[0]
-    total = sum(ref[...] for ref in sums)
-    inverse = negative_inverse(unpacked(total[piece:, :]) * time_gram_ref[...])
     solved = -jnp.dot(
-        total[:piece, :],
-        inverse,
+        sum(ref[...] for ref in sums),
+        inverse_ref[...],
         precision=lax.Precision.HIGHEST,
         preferred_element_type=F32,
     )
@@ -253,13 +249,14 @@
     return lax.ppermute(value, axis, [(at, at ^ offset) for at in range(groups)])
 
 
-def call(kernel, operands, in_specs, outs, scratch=(), room=24):
+def call(kernel, operands, in_specs, outs, scratch=(), room=24, flops=0):
     return pl.pallas_call(
         kernel,
         out_shape=tuple(jax.ShapeDtypeStruct(shape, dtype) for shape, dtype in outs),
         in_specs=in_specs,
         out_specs=(VMEM,) * len(outs),
         scratch_shapes=scratch,
+        cost_estimate=pl.CostEstimate(flops=flops, bytes_accessed=0, transcendentals=0) if flops else None,
         compiler_params=pltpu.CompilerParams(vmem_limit_bytes=room * 2**20),
     )(*operands)
 
@@ -275,20 +272,20 @@
     whole = ((depth + pack, rank), BF16)
     message, own = call(prepare_kernel, (second_factor,), [VMEM], [whole, whole])
     half = rows // 2
-    near = range(1, half)
+    near = sorted(range(1, half), key=lambda at: (bin(at).count("0") - len(bin(at)), at))
     opposite = shifted(message, "row", half, rows)
     arrived = {at: shifted(message, "row", at, rows) for at in near}
     in_hbm = pltpu.with_memory_space_constraint(tensor, pltpu.HBM)
     direct = depth % 128 == 0
-    owners, width = (list(range(rows)), depth) if direct else ([0], own_cols)
+    owners, width = ([0, *near, half, *(half + at for at in near)], depth) if direct else ([0], own_cols)
     block = (snaps, own_rows, width)
-    begin, split = (half, half + 1) if direct else (1, 1)
+    begin, split = (half + 1, half + 1) if direct else (1, 1)
     time, time_gram, early = call(
         functools.partial(load_kernel, owners[:begin], width),
-        (in_hbm, time_factor),
-        [HBM, VMEM],
+        (in_hbm, pltpu.with_memory_space_constraint(time_factor, pltpu.HBM)),
+        [HBM, HBM],
         [((snaps, rank), F32), ((rank, rank), F32), ((begin, *block), BF16)],
-        [pltpu.SemaphoreType.DMA((begin,))],
+        [pltpu.SemaphoreType.DMA((begin + 1,))],
     )
     (opposite,) = call(relay_kernel, (time, opposite), [VMEM] * 2, [whole])
     arrived[0], arrived[half] = own, opposite
@@ -296,7 +293,7 @@
         arrived[half + at] = shifted(opposite, "row", at, rows)
 
     if direct:
-        parts = [arrived[at] for at in range(rows)]
+        parts = [arrived[at] for at in owners]
     else:
         row = lax.axis_index("row")
         low = jnp.stack([arrived[at][:depth] for at in range(rows)])
@@ -312,32 +309,28 @@
         sums + [((later, *block), BF16)],
         [pltpu.SemaphoreType.DMA((later,))],
     )
-    if len(parts) > split + 1:
-        middle = parts[split:-1]
-        result, gram = call(
-            functools.partial(middle_kernel, width, range(split - begin, later - 1)),
-            (time, tensor_later, result, gram, *middle),
-            [VMEM] * (4 + len(middle)),
-            sums,
-        )
-    last = parts[split:][-1:]
+    last = parts[split:]
     keep, send = call(
-        functools.partial(last_kernel, width, [later - 1]),
-        (time, tensor_later, result, gram, *last),
-        [VMEM] * (4 + len(last)),
+        functools.partial(last_kernel, width),
+        (time, early, tensor_later, result, gram, *last),
+        [VMEM] * (5 + len(last)),
         [((pairs * piece, rank), F32), ((pairs * piece + pack, rank), F32)],
     )
 
-    total, *outs = call(
+    chip_gram, own_sum, *outs = call(
         functools.partial(chip_kernel, piece),
         (keep, send, shifted(send, "col", 1, cols)),
         [VMEM] * 3,
-        [((piece + pack, rank), F32)] * pairs,
-    )
-    totals = [total] + [shifted(out, "col", 2 * (at + 1), cols) for at, out in enumerate(outs)]
+        [((pack, rank), F32)] + [((piece, rank), F32)] * pairs,
+    )
+    grams = [chip_gram] + [shifted(chip_gram, "col", 2 * at, cols) for at in range(1, pairs)]
+    pieces = [own_sum] + [shifted(out, "col", 2 * (at + 1), cols) for at, out in enumerate(outs)]
+    (inverse,) = call(
+        inverse_kernel, (time_gram, *grams), [VMEM] * (1 + pairs), [((rank, rank), F32)], flops=2 * 10**9
+    )
     solved, squares = call(
         solve_kernel,
-        (time_gram, *totals),
+        (inverse, *pieces),
         [VMEM] * (1 + pairs),
         [((piece, rank), F32), ((rows * cols, rank), F32)],
     )

time: 42 us -> 41 us (0.976)
  waiting for transfers between devices: 6.44 us -> 5.11 us
  local copies, waits for them, and re-layouts: 1.58 us -> 0.9 us
  starting transfers between devices: 12.7 us -> 13.3 us
  blocking collectives: 9.53 us -> 10.1 us
    ppermute x9 -> x10, waiting for transfers between devices: 6.44 us -> 5.11 us  [shifted(): lax.ppermute(value, axis, [(at, at ^ offset) for at in range(groups)])]
    unnamed x6 -> x4, local copies, waits for them, and re-layouts: 1.58 us -> 0.9 us
    all_to_all x1, blocking collectives: 9.53 us -> 10.1 us  [per_device(): squares = lax.all_to_all(squares, ('row', 'col'), 0, 0, tiled=True)]
    ppermute x9 -> x10, starting transfers between devices: 12.7 us -> 13.3 us  [shifted(): lax.ppermute(value, axis, [(at, at ^ offset) for at in range(groups)])]
  transfers between devices with their start and end apart: 9 -> 10, of which waited for: 3 -> 5; matrix products, arithmetic and copies ran while one was open for 0% -> 0% of each run, Pallas kernels for 14% -> 20%
where the time goes in v6:
time: 41 us; the launch traced here: 40.8 us
  starting transfers between devices  13.3 us (32%)
  blocking collectives  10.1 us (25%)
  Pallas kernels  9.97 us (24%)
  waiting for transfers between devices  5.11 us (12%)
  local copies, waits for them, and re-layouts  0.9 us (2%)
  between operations  0.71 us (2%)
  other arithmetic  0.7 us (2%)
    ppermute x10, starting transfers between devices, shifted(): lax.ppermute(value, axis, [(at, at ^ offset) for at in range(groups)])  13.3 us
    all_to_all x1, blocking collectives, per_device(): squares = lax.all_to_all(squares, ('row', 'col'), 0, 0, tiled=True)  10.1 us
    pallas_call x8, Pallas kernels, call(): pl.pallas_call(kernel, out_shape=tuple((jax.ShapeDtypeStruct(shape, dtype...  9.97 us
    ppermute x10, waiting for transfers between devices, shifted(): lax.ppermute(value, axis, [(at, at ^ offset) for at in range(groups)])  5.11 us
    unnamed x4, local copies, waits for them, and re-layouts  0.9 us
  transfers between devices with their start and end apart: 10, of which 5 were waited for; matrix products, arithmetic and copies ran while one was open for 0% of the time, Pallas kernels for 20%

profile of v6, /device:TPU:0, one launch (start us, length us, event | category | flops | bytes accessed | tf_op | source)
XLA Modules:
  0.0 40.8 jit_solution(12469241090738093560)
XLA Ops:
  0.6 0.0 copy-start
  0.6 0.9 %copy-done = f32[256,128]{1,0:T(8,128)S(1)} copy-done((f32[256,128]{1,0:T(8,128)S(1)}, f32[256,128]{1,0:T(8,128)}, u32[]{:S(2)}) %copy-start) | copy-done | bytes 131096
  1.5 0.3 shard_map.51
  1.9 4.1 %collective-permute-start.3 = (bf16[336,128]{1,0:T(8,128)(2,1)S(1)}, bf16[336,128]{1,0:T(8,128)(2,1)S(1)}, u32[]{:S(2)}, u32[]{:S(2)}) collective-permute-start(bf16[336,128]{1,0:T(8,128)(2,1)S(1)} %get-tuple-element.21), channel_id=1, source_target_pairs={{0,16},{4,20},{8,24},{12,28},{16,0},{20,4},{24,8},{28,12},{1,17},{... | collective-permute-start | bytes 258056 | tf_op jit(solution)/shard_map/ppermute | solution.py:249
  5.9 2.5 %collective-permute-start = (bf16[336,128]{1,0:T(8,128)(2,1)S(1)}, bf16[336,128]{1,0:T(8,128)(2,1)S(1)}, u32[]{:S(2)}, u32[]{:S(2)}) collective-permute-start(bf16[336,128]{1,0:T(8,128)(2,1)S(1)} %get-tuple-element.21), channel_id=1, source_target_pairs={{0,12},{4,8},{8,4},{12,0},{16,28},{20,24},{24,20},{28,16},{1,13},{... | collective-permute-start | bytes 258056 | tf_op jit(solution)/shard_map/ppermute | solution.py:249
  8.5 0.5 %collective-permute-start.1 = (bf16[336,128]{1,0:T(8,128)(2,1)S(1)}, bf16[336,128]{1,0:T(8,128)(2,1)S(1)}, u32[]{:S(2)}, u32[]{:S(2)}) collective-permute-start(bf16[336,128]{1,0:T(8,128)(2,1)S(1)} %get-tuple-element.21), channel_id=1, source_target_pairs={{0,4},{4,0},{8,12},{12,8},{16,20},{20,16},{24,28},{28,24},{1,5},{5... | collective-permute-start | bytes 258056 | tf_op jit(solution)/shard_map/ppermute | solution.py:249
  9.0 0.4 %collective-permute-start.2 = (bf16[336,128]{1,0:T(8,128)(2,1)S(1)}, bf16[336,128]{1,0:T(8,128)(2,1)S(1)}, u32[]{:S(2)}, u32[]{:S(2)}) collective-permute-start(bf16[336,128]{1,0:T(8,128)(2,1)S(1)} %get-tuple-element.21), channel_id=1, source_target_pairs={{0,8},{4,12},{8,0},{12,4},{16,24},{20,28},{24,16},{28,20},{1,9},{5... | collective-permute-start | bytes 258056 | tf_op jit(solution)/shard_map/ppermute | solution.py:249
  9.4 2.6 %shard_map.50 = (f32[4,128]{1,0:T(4,128)S(1)}, f32[128,128]{1,0:T(8,128)S(1)}, bf16[5,4,512,256]{3,2,1,0:T(8,128)(2,1)S(1)}) custom-call(bf16[4,512,2048]{2,1,0:T(8,128)(2,1)} %tensor_ref.3, f32[4,128]{1,0:T(4,128)} %time_ref.1), custom_call_target="tpu_custom_call" | custom-call | tf_op jit(solution)/shard_map/pallas_call | solution.py:253
  12.1 0.0 collective-permute-done.3.part_ref
  12.1 2.6 %collective-permute-start.4 = (bf16[336,128]{1,0:T(8,128)(2,1)S(1)}, bf16[336,128]{1,0:T(8,128)(2,1)S(1)}, u32[]{:S(2)}, u32[]{:S(2)}) collective-permute-start(bf16[336,128]{1,0:T(8,128)(2,1)S(1)} %shard_map.52.refs_4_), channel_id=1, source_target_pairs={{0,12},{4,8},{8,4},{12,0},{16,28},{20,24},{24,20},{28,16},{1,13},{... | collective-permute-start | bytes 258056 | tf_op jit(solution)/shard_map/ppermute | solution.py:249
  14.7 0.5 %collective-permute-start.5 = (bf16[336,128]{1,0:T(8,128)(2,1)S(1)}, bf16[336,128]{1,0:T(8,128)(2,1)S(1)}, u32[]{:S(2)}, u32[]{:S(2)}) collective-permute-start(bf16[336,128]{1,0:T(8,128)(2,1)S(1)} %shard_map.52.refs_4_), channel_id=1, source_target_pairs={{0,4},{4,0},{8,12},{12,8},{16,20},{20,16},{24,28},{28,24},{1,5},{5... | collective-permute-start | bytes 258056 | tf_op jit(solution)/shard_map/ppermute | solution.py:249
  15.2 0.0 collective-permute-done.refs_1_
  15.2 0.5 %collective-permute-start.6 = (bf16[336,128]{1,0:T(8,128)(2,1)S(1)}, bf16[336,128]{1,0:T(8,128)(2,1)S(1)}, u32[]{:S(2)}, u32[]{:S(2)}) collective-permute-start(bf16[336,128]{1,0:T(8,128)(2,1)S(1)} %shard_map.52.refs_4_), channel_id=1, source_target_pairs={{0,8},{4,12},{8,0},{12,4},{16,24},{20,28},{24,16},{28,20},{1,9},{5... | collective-permute-start | bytes 258056 | tf_op jit(solution)/shard_map/ppermute | solution.py:249
  15.6 0.0 collective-permute-done.1.refs_2_
  15.6 0.0 collective-permute-done.2.refs_3_
  15.6 2.4 %shard_map.53 = (f32[512,128]{1,0:T(8,128)S(1)}, f32[80,128]{1,0:T(8,128)S(1)}, bf16[3,4,512,256]{3,2,1,0:T(8,128)(2,1)S(1)}) custom-call(bf16[4,512,2048]{2,1,0:T(8,128)(2,1)} %tensor_ref.3, f32[4,128]{1,0:T(4,128)S(1)} %get-tuple-element.18.ready_ref.time_ref, bf16[5,4,512,256]{3,2,1,0:T(8,128)(2,1)S(1)} %get-tuple-element.19.early_ref, ...), custom_call_target="tpu_custom_call" | custom-call | tf_op jit(solution)/shard_map/pallas_call | solution.py:253
  18.1 0.1 collective-permute-done.4.refs_0_
  18.2 1.0 %collective-permute-done.5.refs_1_ = bf16[336,128]{1,0:T(8,128)(2,1)S(1)} collective-permute-done((bf16[336,128]{1,0:T(8,128)(2,1)S(1)}, bf16[336,128]{1,0:T(8,128)(2,1)S(1)}, u32[]{:S(2)}, u32[]{:S(2)}) %collective-permute-start.5) | collective-permute-done | bytes 86048 | tf_op jit(solution)/shard_map/ppermute | solution.py:249
  19.2 0.5 %collective-permute-done.6.refs_2_ = bf16[336,128]{1,0:T(8,128)(2,1)S(1)} collective-permute-done((bf16[336,128]{1,0:T(8,128)(2,1)S(1)}, bf16[336,128]{1,0:T(8,128)(2,1)S(1)}, u32[]{:S(2)}, u32[]{:S(2)}) %collective-permute-start.6) | collective-permute-done | bytes 86048 | tf_op jit(solution)/shard_map/ppermute | solution.py:249
  19.7 1.1 %shard_map.54 = (f32[256,128]{1,0:T(8,128)S(1)}, f32[336,128]{1,0:T(8,128)S(1)}) custom-call(f32[4,128]{1,0:T(4,128)S(1)} %get-tuple-element.18.ready_ref.time_ref, bf16[5,4,512,256]{3,2,1,0:T(8,128)(2,1)S(1)} %get-tuple-element.19.early_ref, bf16[3,4,512,256]{3,2,1,0:T(8,128)(2,1)S(1)} %get-tuple-element.22.later_ref, ...), custom_call_target="tpu_custom_call" | custom-call | tf_op jit(solution)/shard_map/pallas_call | solution.py:253
  20.8 0.1 collective-permute-start.7
  20.8 1.4 %collective-permute-done.7.got_ref = f32[336,128]{1,0:T(8,128)S(1)} collective-permute-done((f32[336,128]{1,0:T(8,128)S(1)}, f32[336,128]{1,0:T(8,128)S(1)}, u32[]{:S(2)}, u32[]{:S(2)}) %collective-permute-start.7) | collective-permute-done | bytes 172064 | tf_op jit(solution)/shard_map/ppermute | solution.py:249
  22.3 1.6 %collective-permute-start.8 = (f32[80,128]{1,0:T(8,128)S(1)}, f32[80,128]{1,0:T(8,128)S(1)}, u32[]{:S(2)}, u32[]{:S(2)}) collective-permute-start(f32[80,128]{1,0:T(8,128)S(1)} %get-tuple-element.27.refs_0_), channel_id=1, source_target_pairs={{0,2},{1,3},{2,0},{3,1},{4,6},{5,7},{6,4},{7,5},{8,10},{9,11},{10,... | collective-permute-start | bytes 122888 | tf_op jit(solution)/shard_map/ppermute | solution.py:249
  23.8 0.5 %collective-permute-start.9 = (f32[128,128]{1,0:T(8,128)S(1)}, f32[128,128]{1,0:T(8,128)S(1)}, u32[]{:S(2)}, u32[]{:S(2)}) collective-permute-start(f32[128,128]{1,0:T(8,128)S(1)} %get-tuple-element.29), channel_id=1, source_target_pairs={{0,2},{1,3},{2,0},{3,1},{4,6},{5,7},{6,4},{7,5},{8,10},{9,11},{10,... | collective-permute-start | bytes 196616 | tf_op jit(solution)/shard_map/ppermute | solution.py:249
  24.4 2.1 %collective-permute-done.8.refs_1_ = f32[80,128]{1,0:T(8,128)S(1)} collective-permute-done((f32[80,128]{1,0:T(8,128)S(1)}, f32[80,128]{1,0:T(8,128)S(1)}, u32[]{:S(2)}, u32[]{:S(2)}) %collective-permute-start.8) | collective-permute-done | bytes 40992 | tf_op jit(solution)/shard_map/ppermute | solution.py:249
  26.5 3.3 %shard_map.56.inverse_ref = f32[128,128]{1,0:T(8,128)S(1)} custom-call(f32[128,128]{1,0:T(8,128)S(1)} %get-tuple-element.17.time_gram_ref, f32[80,128]{1,0:T(8,128)S(1)} %get-tuple-element.27.refs_0_, f32[80,128]{1,0:T(8,128)S(1)} %collective-permute-done.8.refs_1_), custom_call_target="tpu_custom_call" | custom-call | flops 2000000000 | tf_op jit(solution)/shard_map/pallas_call | solution.py:253
  29.7 0.0 collective-permute-done.9.refs_1_
  29.7 0.2 shard_map.57
  30.0 10.1 %all_to_all.9 = f32[32,1,128]{2,1,0:T(1,128)S(1)} all-to-all(f32[32,1,128]{2,1,0:T(1,128)S(1)} %bitcast.3), channel_id=1, replica_groups=mesh['row'=8,'col'=4] {'row','col'}, dimensions={0} | all-to-all | bytes 32768 | tf_op jit(solution)/shard_map/all_to_all | solution.py:337
  40.1 0.1 reduce_sum.9
  40.2 0.6 %broadcast_divide_fusion = f32[128,128]{1,0:T(8,128)} fusion(f32[128,128]{1,0:T(8,128)S(1)} %get-tuple-element.30, f32[128]{0:T(128)S(1)} %add_sqrt_fusion), kind=kLoop, calls=%fused_computation | loop fusion | flops 16384 | bytes 131584 | tf_op jit(solution)/shard_map/div | solution.py:339
  40.8 0.0 copy-done.1
  (4 shorter events, 0.0 us)
Async XLA Ops:
  0.6 0.9 %copy-start = (f32[256,128]{1,0:T(8,128)S(1)}, f32[256,128]{1,0:T(8,128)}, u32[]{:S(2)}) copy-start(f32[256,128]{1,0:T(8,128)} %factor_ref.1) | copy-start | bytes 393220
  1.9 10.2 %collective-permute-start.3 = (bf16[336,128]{1,0:T(8,128)(2,1)S(1)}, bf16[336,128]{1,0:T(8,128)(2,1)S(1)}, u32[]{:S(2)}, u32[]{:S(2)}) collective-permute-start(bf16[336,128]{1,0:T(8,128)(2,1)S(1)} %get-tuple-element.21), channel_id=1, source_target_pairs={{0,16},{4,20},{8,24},{12,28},{16,0},{20,4},{24,8},{28,12},{1,17},{... | collective-permute-start | bytes 258056 | tf_op jit(solution)/shard_map/ppermute | solution.py:249
  5.9 9.3 %collective-permute-start = (bf16[336,128]{1,0:T(8,128)(2,1)S(1)}, bf16[336,128]{1,0:T(8,128)(2,1)S(1)}, u32[]{:S(2)}, u32[]{:S(2)}) collective-permute-start(bf16[336,128]{1,0:T(8,128)(2,1)S(1)} %get-tuple-element.21), channel_id=1, source_target_pairs={{0,12},{4,8},{8,4},{12,0},{16,28},{20,24},{24,20},{28,16},{1,13},{... | collective-permute-start | bytes 258056 | tf_op jit(solution)/shard_map/ppermute | solution.py:249
  8.5 7.2 %collective-permute-start.1 = (bf16[336,128]{1,0:T(8,128)(2,1)S(1)}, bf16[336,128]{1,0:T(8,128)(2,1)S(1)}, u32[]{:S(2)}, u32[]{:S(2)}) collective-permute-start(bf16[336,128]{1,0:T(8,128)(2,1)S(1)} %get-tuple-element.21), channel_id=1, source_target_pairs={{0,4},{4,0},{8,12},{12,8},{16,20},{20,16},{24,28},{28,24},{1,5},{5... | collective-permute-start | bytes 258056 | tf_op jit(solution)/shard_map/ppermute | solution.py:249
  9.0 6.7 %collective-permute-start.2 = (bf16[336,128]{1,0:T(8,128)(2,1)S(1)}, bf16[336,128]{1,0:T(8,128)(2,1)S(1)}, u32[]{:S(2)}, u32[]{:S(2)}) collective-permute-start(bf16[336,128]{1,0:T(8,128)(2,1)S(1)} %get-tuple-element.21), channel_id=1, source_target_pairs={{0,8},{4,12},{8,0},{12,4},{16,24},{20,28},{24,16},{28,20},{1,9},{5... | collective-permute-start | bytes 258056 | tf_op jit(solution)/shard_map/ppermute | solution.py:249
  12.1 6.1 %collective-permute-start.4 = (bf16[336,128]{1,0:T(8,128)(2,1)S(1)}, bf16[336,128]{1,0:T(8,128)(2,1)S(1)}, u32[]{:S(2)}, u32[]{:S(2)}) collective-permute-start(bf16[336,128]{1,0:T(8,128)(2,1)S(1)} %shard_map.52.refs_4_), channel_id=1, source_target_pairs={{0,12},{4,8},{8,4},{12,0},{16,28},{20,24},{24,20},{28,16},{1,13},{... | collective-permute-start | bytes 258056 | tf_op jit(solution)/shard_map/ppermute | solution.py:249
  14.7 4.5 %collective-permute-start.5 = (bf16[336,128]{1,0:T(8,128)(2,1)S(1)}, bf16[336,128]{1,0:T(8,128)(2,1)S(1)}, u32[]{:S(2)}, u32[]{:S(2)}) collective-permute-start(bf16[336,128]{1,0:T(8,128)(2,1)S(1)} %shard_map.52.refs_4_), channel_id=1, source_target_pairs={{0,4},{4,0},{8,12},{12,8},{16,20},{20,16},{24,28},{28,24},{1,5},{5... | collective-permute-start | bytes 258056 | tf_op jit(solution)/shard_map/ppermute | solution.py:249
  15.2 4.5 %collective-permute-start.6 = (bf16[336,128]{1,0:T(8,128)(2,1)S(1)}, bf16[336,128]{1,0:T(8,128)(2,1)S(1)}, u32[]{:S(2)}, u32[]{:S(2)}) collective-permute-start(bf16[336,128]{1,0:T(8,128)(2,1)S(1)} %shard_map.52.refs_4_), channel_id=1, source_target_pairs={{0,8},{4,12},{8,0},{12,4},{16,24},{20,28},{24,16},{28,20},{1,9},{5... | collective-permute-start | bytes 258056 | tf_op jit(solution)/shard_map/ppermute | solution.py:249
  20.8 1.5 %collective-permute-start.7 = (f32[336,128]{1,0:T(8,128)S(1)}, f32[336,128]{1,0:T(8,128)S(1)}, u32[]{:S(2)}, u32[]{:S(2)}) collective-permute-start(f32[336,128]{1,0:T(8,128)S(1)} %get-tuple-element.26.sent_ref), channel_id=1, source_target_pairs={{0,1},{1,0},{2,3},{3,2},{4,5},{5,4},{6,7},{7,6},{8,9},{9,8},{10,11... | collective-permute-start | bytes 516104 | tf_op jit(solution)/shard_map/ppermute | solution.py:249
  22.3 4.2 %collective-permute-start.8 = (f32[80,128]{1,0:T(8,128)S(1)}, f32[80,128]{1,0:T(8,128)S(1)}, u32[]{:S(2)}, u32[]{:S(2)}) collective-permute-start(f32[80,128]{1,0:T(8,128)S(1)} %get-tuple-element.27.refs_0_), channel_id=1, source_target_pairs={{0,2},{1,3},{2,0},{3,1},{4,6},{5,7},{6,4},{7,5},{8,10},{9,11},{10,... | collective-permute-start | bytes 122888 | tf_op jit(solution)/shard_map/ppermute | solution.py:249
  23.8 5.9 %collective-permute-start.9 = (f32[128,128]{1,0:T(8,128)S(1)}, f32[128,128]{1,0:T(8,128)S(1)}, u32[]{:S(2)}, u32[]{:S(2)}) collective-permute-start(f32[128,128]{1,0:T(8,128)S(1)} %get-tuple-element.29), channel_id=1, source_target_pairs={{0,2},{1,3},{2,0},{3,1},{4,6},{5,7},{6,4},{7,5},{8,10},{9,11},{10,... | collective-permute-start | bytes 196616 | tf_op jit(solution)/shard_map/ppermute | solution.py:249
  40.2 0.7 %copy-start.1 = (f32[128]{0:T(128)}, f32[128]{0:T(128)S(1)}, u32[]{:S(2)}) copy-start(f32[128]{0:T(128)S(1)} %add_sqrt_fusion) | copy-start | bytes 1540

commit v7 on v6

--- a/solution.py
+++ b/solution.py
@@ -113,17 +113,6 @@
     return packed(gram) + rest
 
 
-def multiply(blocks, time_ref, parts, depth):
-    snaps = time_ref.shape[0]
-    total = [0.0] * snaps
-    for block, part in zip(blocks, parts):
-        for snap in range(snaps):
-            total[snap] = total[snap] + jnp.dot(
-                block[snap], part[:depth, :], preferred_element_type=F32
-            )
-    return sum(total[snap] * time_ref[snap : snap + 1, :] for snap in range(snaps))
-
-
 def first_kernel(owners, depth, tensor_ref, time_ref, early_ref, *refs):
     parts, (result_ref, gram_ref, later_ref, sems) = refs[:-4], refs[-4:]
     arrivals = start_loads(owners, depth, tensor_ref, later_ref, sems)
@@ -143,24 +132,29 @@
         arrival.wait()
 
 
-def last_kernel(depth, time_ref, early_ref, later_ref, result_ref, gram_ref, *refs):
-    parts, (keep_ref, send_ref) = refs[:-2], refs[-2:]
+def last_kernel(depth, other, time_ref, early_ref, later_ref, result_ref, gram_ref, *refs):
+    parts, out_ref = refs[:-1], refs[-1]
     col, cols = lax.axis_index("col"), lax.axis_size("col")
-    result, gram = result_ref[...], gram_ref[...]
-    if parts:
-        begin, later = early_ref.shape[0], later_ref.shape[0]
-        blocks = [early_ref.at[at] for at in range(begin)]
-        blocks = (blocks + [later_ref.at[at] for at in range(later)])[-len(parts) :]
-        result = result + multiply(blocks, time_ref, parts, depth)
-        gram = gram + gram_of(parts, depth)
-    piece = result.shape[0] // cols
-    core = lax.rem(col, 2)
+    piece = result_ref.shape[0] // cols
+    side = lax.rem(col + other, 2)
+    begin, later = early_ref.shape[0], later_ref.shape[0]
+    blocks = [early_ref.at[at] for at in range(begin)]
+    blocks = (blocks + [later_ref.at[at] for at in range(later)])[begin + later - len(parts) :]
     for pair in range(cols // 2):
-        even = result[(2 * pair) * piece : (2 * pair + 1) * piece, :]
-        odd = result[(2 * pair + 1) * piece : (2 * pair + 2) * piece, :]
-        keep_ref[pair * piece : (pair + 1) * piece, :] = jnp.where(core == 0, even, odd)
-        send_ref[pair * piece : (pair + 1) * piece, :] = jnp.where(core == 0, odd, even)
-    send_ref[(cols // 2) * piece :, :] = gram
+        rows = pl.ds(pl.multiple_of((2 * pair + side) * piece, piece), piece)
+        total = result_ref[rows, :]
+        for snap in range(time_ref.shape[0] if parts else 0):
+            product = sum(
+                jnp.dot(block[snap, rows, :], part[:depth, :], preferred_element_type=F32)
+                for block, part in zip(blocks, parts)
+            )
+            total = total + product * time_ref[snap : snap + 1, :]
+        out_ref[pair * piece : (pair + 1) * piece, :] = total
+    if other:
+        gram = gram_ref[...]
+        if parts:
+            gram = gram + gram_of(parts, depth)
+        out_ref[(cols // 2) * piece :, :] = gram
 
 
 def chip_kernel(piece, keep_ref, sent_ref, got_ref, gram_ref, *out_refs):
@@ -310,12 +304,12 @@
         [pltpu.SemaphoreType.DMA((later,))],
     )
     last = parts[split:]
-    keep, send = call(
-        functools.partial(last_kernel, width),
-        (time, early, tensor_later, result, gram, *last),
-        [VMEM] * (5 + len(last)),
-        [((pairs * piece, rank), F32), ((pairs * piece + pack, rank), F32)],
-    )
+    held = pairs * piece
+    operands = (time, early, tensor_later, result, gram, *last)
+    specs = [VMEM] * len(operands)
+    other, own = functools.partial(last_kernel, width, 1), functools.partial(last_kernel, width, 0)
+    (send,) = call(other, operands, specs, [((held + pack, rank), F32)])
+    (keep,) = call(own, operands, specs, [((held, rank), F32)], flops=10**9)
 
     chip_gram, own_sum, *outs = call(
         functools.partial(chip_kernel, piece),

time: 41 us -> 40.6 us (level)
  waiting for transfers between devices: 5.11 us -> 4.52 us
    ppermute x10, waiting for transfers between devices: 5.11 us -> 4.52 us  [shifted(): lax.ppermute(value, axis, [(at, at ^ offset) for at in range(groups)])]
    pallas_call x8 -> x9, Pallas kernels: 9.97 us -> 10.1 us  [call(): pl.pallas_call(kernel, out_shape=tuple((jax.ShapeDtypeStruct(shape, dtype...]
  transfers between devices with their start and end apart: 10 -> 10, of which waited for: 5 -> 5; matrix products, arithmetic and copies ran while one was open for 0% -> 0% of each run, Pallas kernels for 20% -> 22%
where the time goes in v7:
time: 40.6 us; the launch traced here: 40.4 us
  starting transfers between devices  13.3 us (33%)
  Pallas kernels  10.1 us (25%)
  blocking collectives  10.1 us (25%)
  waiting for transfers between devices  4.52 us (11%)
  local copies, waits for them, and re-layouts  0.9 us (2%)
  between operations  0.72 us (2%)
  other arithmetic  0.7 us (2%)
    ppermute x10, starting transfers between devices, shifted(): lax.ppermute(value, axis, [(at, at ^ offset) for at in range(groups)])  13.3 us
    pallas_call x9, Pallas kernels, call(): pl.pallas_call(kernel, out_shape=tuple((jax.ShapeDtypeStruct(shape, dtype...  10.1 us
    all_to_all x1, blocking collectives, per_device(): squares = lax.all_to_all(squares, ('row', 'col'), 0, 0, tiled=True)  10.1 us
    ppermute x10, waiting for transfers between devices, shifted(): lax.ppermute(value, axis, [(at, at ^ offset) for at in range(groups)])  4.52 us
    unnamed x4, local copies, waits for them, and re-layouts  0.9 us
  transfers between devices with their start and end apart: 10, of which 5 were waited for; matrix products, arithmetic and copies ran while one was open for 0% of the time, Pallas kernels for 22%

profile of v7, /device:TPU:0, one launch (start us, length us, event | category | flops | bytes accessed | tf_op | source)
XLA Modules:
  0.0 40.4 jit_solution(12674052456418988906)
XLA Ops:
  0.6 0.9 %copy-done = f32[256,128]{1,0:T(8,128)S(1)} copy-done((f32[256,128]{1,0:T(8,128)S(1)}, f32[256,128]{1,0:T(8,128)}, u32[]{:S(2)}) %copy-start) | copy-done | bytes 131096
  1.5 0.3 shard_map.51
  1.9 4.1 %collective-permute-start.3 = (bf16[336,128]{1,0:T(8,128)(2,1)S(1)}, bf16[336,128]{1,0:T(8,128)(2,1)S(1)}, u32[]{:S(2)}, u32[]{:S(2)}) collective-permute-start(bf16[336,128]{1,0:T(8,128)(2,1)S(1)} %get-tuple-element.19), channel_id=1, source_target_pairs={{0,16},{4,20},{8,24},{12,28},{16,0},{20,4},{24,8},{28,12},{1,17},{... | collective-permute-start | bytes 258056 | tf_op jit(solution)/shard_map/ppermute | solution.py:243
  5.9 2.5 %collective-permute-start = (bf16[336,128]{1,0:T(8,128)(2,1)S(1)}, bf16[336,128]{1,0:T(8,128)(2,1)S(1)}, u32[]{:S(2)}, u32[]{:S(2)}) collective-permute-start(bf16[336,128]{1,0:T(8,128)(2,1)S(1)} %get-tuple-element.19), channel_id=1, source_target_pairs={{0,12},{4,8},{8,4},{12,0},{16,28},{20,24},{24,20},{28,16},{1,13},{... | collective-permute-start | bytes 258056 | tf_op jit(solution)/shard_map/ppermute | solution.py:243
  8.5 0.5 %collective-permute-start.1 = (bf16[336,128]{1,0:T(8,128)(2,1)S(1)}, bf16[336,128]{1,0:T(8,128)(2,1)S(1)}, u32[]{:S(2)}, u32[]{:S(2)}) collective-permute-start(bf16[336,128]{1,0:T(8,128)(2,1)S(1)} %get-tuple-element.19), channel_id=1, source_target_pairs={{0,4},{4,0},{8,12},{12,8},{16,20},{20,16},{24,28},{28,24},{1,5},{5... | collective-permute-start | bytes 258056 | tf_op jit(solution)/shard_map/ppermute | solution.py:243
  9.0 0.4 %collective-permute-start.2 = (bf16[336,128]{1,0:T(8,128)(2,1)S(1)}, bf16[336,128]{1,0:T(8,128)(2,1)S(1)}, u32[]{:S(2)}, u32[]{:S(2)}) collective-permute-start(bf16[336,128]{1,0:T(8,128)(2,1)S(1)} %get-tuple-element.19), channel_id=1, source_target_pairs={{0,8},{4,12},{8,0},{12,4},{16,24},{20,28},{24,16},{28,20},{1,9},{5... | collective-permute-start | bytes 258056 | tf_op jit(solution)/shard_map/ppermute | solution.py:243
  9.4 2.6 %shard_map.50 = (f32[4,128]{1,0:T(4,128)S(1)}, f32[128,128]{1,0:T(8,128)S(1)}, bf16[5,4,512,256]{3,2,1,0:T(8,128)(2,1)S(1)}) custom-call(bf16[4,512,2048]{2,1,0:T(8,128)(2,1)} %tensor_ref.3, f32[4,128]{1,0:T(4,128)} %time_ref.1), custom_call_target="tpu_custom_call" | custom-call | tf_op jit(solution)/shard_map/pallas_call | solution.py:247
  12.1 0.0 collective-permute-done.3.part_ref
  12.1 2.6 %collective-permute-start.4 = (bf16[336,128]{1,0:T(8,128)(2,1)S(1)}, bf16[336,128]{1,0:T(8,128)(2,1)S(1)}, u32[]{:S(2)}, u32[]{:S(2)}) collective-permute-start(bf16[336,128]{1,0:T(8,128)(2,1)S(1)} %shard_map.52.refs_4_), channel_id=1, source_target_pairs={{0,12},{4,8},{8,4},{12,0},{16,28},{20,24},{24,20},{28,16},{1,13},{... | collective-permute-start | bytes 258056 | tf_op jit(solution)/shard_map/ppermute | solution.py:243
  14.7 0.5 %collective-permute-start.5 = (bf16[336,128]{1,0:T(8,128)(2,1)S(1)}, bf16[336,128]{1,0:T(8,128)(2,1)S(1)}, u32[]{:S(2)}, u32[]{:S(2)}) collective-permute-start(bf16[336,128]{1,0:T(8,128)(2,1)S(1)} %shard_map.52.refs_4_), channel_id=1, source_target_pairs={{0,4},{4,0},{8,12},{12,8},{16,20},{20,16},{24,28},{28,24},{1,5},{5... | collective-permute-start | bytes 258056 | tf_op jit(solution)/shard_map/ppermute | solution.py:243
  15.2 0.0 collective-permute-done.refs_1_
  15.2 0.5 %collective-permute-start.6 = (bf16[336,128]{1,0:T(8,128)(2,1)S(1)}, bf16[336,128]{1,0:T(8,128)(2,1)S(1)}, u32[]{:S(2)}, u32[]{:S(2)}) collective-permute-start(bf16[336,128]{1,0:T(8,128)(2,1)S(1)} %shard_map.52.refs_4_), channel_id=1, source_target_pairs={{0,8},{4,12},{8,0},{12,4},{16,24},{20,28},{24,16},{28,20},{1,9},{5... | collective-permute-start | bytes 258056 | tf_op jit(solution)/shard_map/ppermute | solution.py:243
  15.6 0.0 collective-permute-done.1.refs_2_
  15.6 0.0 collective-permute-done.2.refs_3_
  15.6 2.4 %shard_map.53 = (f32[512,128]{1,0:T(8,128)S(1)}, f32[80,128]{1,0:T(8,128)S(1)}, bf16[3,4,512,256]{3,2,1,0:T(8,128)(2,1)S(1)}) custom-call(bf16[4,512,2048]{2,1,0:T(8,128)(2,1)} %tensor_ref.3, f32[4,128]{1,0:T(4,128)S(1)} %get-tuple-element.16.ready_ref.time_ref, bf16[5,4,512,256]{3,2,1,0:T(8,128)(2,1)S(1)} %get-tuple-element.17.early_ref, ...), custom_call_target="tpu_custom_call" | custom-call | tf_op jit(solution)/shard_map/pallas_call | solution.py:247
  18.1 0.1 collective-permute-done.4.refs_0_
  18.2 1.0 %collective-permute-done.5.refs_1_ = bf16[336,128]{1,0:T(8,128)(2,1)S(1)} collective-permute-done((bf16[336,128]{1,0:T(8,128)(2,1)S(1)}, bf16[336,128]{1,0:T(8,128)(2,1)S(1)}, u32[]{:S(2)}, u32[]{:S(2)}) %collective-permute-start.5) | collective-permute-done | bytes 86048 | tf_op jit(solution)/shard_map/ppermute | solution.py:243
  19.2 0.5 %collective-permute-done.6.refs_2_ = bf16[336,128]{1,0:T(8,128)(2,1)S(1)} collective-permute-done((bf16[336,128]{1,0:T(8,128)(2,1)S(1)}, bf16[336,128]{1,0:T(8,128)(2,1)S(1)}, u32[]{:S(2)}, u32[]{:S(2)}) %collective-permute-start.6) | collective-permute-done | bytes 86048 | tf_op jit(solution)/shard_map/ppermute | solution.py:243
  19.7 0.7 %shard_map.55.sent_ref = f32[336,128]{1,0:T(8,128)S(1)} custom-call(f32[4,128]{1,0:T(4,128)S(1)} %get-tuple-element.16.ready_ref.time_ref, bf16[5,4,512,256]{3,2,1,0:T(8,128)(2,1)S(1)} %get-tuple-element.17.early_ref, bf16[3,4,512,256]{3,2,1,0:T(8,128)(2,1)S(1)} %get-tuple-element.20.later_ref, f32[512,128]{1,0:T(8,128)S(1)} %get-tuple-element.21.result_ref, ...), custom_call_target="tpu_custom_call" | custom-call | tf_op jit(solution)/shard_map/pallas_call | solution.py:247
  20.4 0.1 collective-permute-start.7
  20.4 0.6 %shard_map.54.keep_ref = f32[256,128]{1,0:T(8,128)S(1)} custom-call(f32[4,128]{1,0:T(4,128)S(1)} %get-tuple-element.16.ready_ref.time_ref, bf16[5,4,512,256]{3,2,1,0:T(8,128)(2,1)S(1)} %get-tuple-element.17.early_ref, bf16[3,4,512,256]{3,2,1,0:T(8,128)(2,1)S(1)} %get-tuple-element.20.later_ref, f32[512,128]{1,0:T(8,128)S(1)} %get-tuple-element.21.result_ref, ...), custom_call_target="tpu_custom_call" | custom-call | flops 1000000000 | tf_op jit(solution)/shard_map/pallas_call | solution.py:247
  21.0 0.8 %collective-permute-done.7.got_ref = f32[336,128]{1,0:T(8,128)S(1)} collective-permute-done((f32[336,128]{1,0:T(8,128)S(1)}, f32[336,128]{1,0:T(8,128)S(1)}, u32[]{:S(2)}, u32[]{:S(2)}) %collective-permute-start.7) | collective-permute-done | bytes 172064 | tf_op jit(solution)/shard_map/ppermute | solution.py:243
  21.9 1.6 %collective-permute-start.8 = (f32[80,128]{1,0:T(8,128)S(1)}, f32[80,128]{1,0:T(8,128)S(1)}, u32[]{:S(2)}, u32[]{:S(2)}) collective-permute-start(f32[80,128]{1,0:T(8,128)S(1)} %get-tuple-element.23.refs_0_), channel_id=1, source_target_pairs={{0,2},{1,3},{2,0},{3,1},{4,6},{5,7},{6,4},{7,5},{8,10},{9,11},{10,... | collective-permute-start | bytes 122888 | tf_op jit(solution)/shard_map/ppermute | solution.py:243
  23.4 0.5 %collective-permute-start.9 = (f32[128,128]{1,0:T(8,128)S(1)}, f32[128,128]{1,0:T(8,128)S(1)}, u32[]{:S(2)}, u32[]{:S(2)}) collective-permute-start(f32[128,128]{1,0:T(8,128)S(1)} %get-tuple-element.25), channel_id=1, source_target_pairs={{0,2},{1,3},{2,0},{3,1},{4,6},{5,7},{6,4},{7,5},{8,10},{9,11},{10,... | collective-permute-start | bytes 196616 | tf_op jit(solution)/shard_map/ppermute | solution.py:243
  24.0 2.1 %collective-permute-done.8.refs_1_ = f32[80,128]{1,0:T(8,128)S(1)} collective-permute-done((f32[80,128]{1,0:T(8,128)S(1)}, f32[80,128]{1,0:T(8,128)S(1)}, u32[]{:S(2)}, u32[]{:S(2)}) %collective-permute-start.8) | collective-permute-done | bytes 40992 | tf_op jit(solution)/shard_map/ppermute | solution.py:243
  26.1 3.3 %shard_map.57.inverse_ref = f32[128,128]{1,0:T(8,128)S(1)} custom-call(f32[128,128]{1,0:T(8,128)S(1)} %get-tuple-element.15.time_gram_ref, f32[80,128]{1,0:T(8,128)S(1)} %get-tuple-element.23.refs_0_, f32[80,128]{1,0:T(8,128)S(1)} %collective-permute-done.8.refs_1_), custom_call_target="tpu_custom_call" | custom-call | flops 2000000000 | tf_op jit(solution)/shard_map/pallas_call | solution.py:247
  29.3 0.0 collective-permute-done.9.refs_1_
  29.3 0.2 shard_map.58
  29.6 10.1 %all_to_all.9 = f32[32,1,128]{2,1,0:T(1,128)S(1)} all-to-all(f32[32,1,128]{2,1,0:T(1,128)S(1)} %bitcast.3), channel_id=1, replica_groups=mesh['row'=8,'col'=4] {'row','col'}, dimensions={0} | all-to-all | bytes 32768 | tf_op jit(solution)/shard_map/all_to_all | solution.py:331
  39.7 0.1 reduce_sum.9
  39.8 0.6 %broadcast_divide_fusion = f32[128,128]{1,0:T(8,128)} fusion(f32[128,128]{1,0:T(8,128)S(1)} %get-tuple-element.26, f32[128]{0:T(128)S(1)} %add_sqrt_fusion), kind=kLoop, calls=%fused_computation | loop fusion | flops 16384 | bytes 131584 | tf_op jit(solution)/shard_map/div | solution.py:333
  40.4 0.0 copy-done.1
  (5 shorter events, 0.0 us)
Async XLA Ops:
  0.6 0.9 %copy-start = (f32[256,128]{1,0:T(8,128)S(1)}, f32[256,128]{1,0:T(8,128)}, u32[]{:S(2)}) copy-start(f32[256,128]{1,0:T(8,128)} %factor_ref.1) | copy-start | bytes 393220
  1.9 10.2 %collective-permute-start.3 = (bf16[336,128]{1,0:T(8,128)(2,1)S(1)}, bf16[336,128]{1,0:T(8,128)(2,1)S(1)}, u32[]{:S(2)}, u32[]{:S(2)}) collective-permute-start(bf16[336,128]{1,0:T(8,128)(2,1)S(1)} %get-tuple-element.19), channel_id=1, source_target_pairs={{0,16},{4,20},{8,24},{12,28},{16,0},{20,4},{24,8},{28,12},{1,17},{... | collective-permute-start | bytes 258056 | tf_op jit(solution)/shard_map/ppermute | solution.py:243
  5.9 9.3 %collective-permute-start = (bf16[336,128]{1,0:T(8,128)(2,1)S(1)}, bf16[336,128]{1,0:T(8,128)(2,1)S(1)}, u32[]{:S(2)}, u32[]{:S(2)}) collective-permute-start(bf16[336,128]{1,0:T(8,128)(2,1)S(1)} %get-tuple-element.19), channel_id=1, source_target_pairs={{0,12},{4,8},{8,4},{12,0},{16,28},{20,24},{24,20},{28,16},{1,13},{... | collective-permute-start | bytes 258056 | tf_op jit(solution)/shard_map/ppermute | solution.py:243
  8.5 7.2 %collective-permute-start.1 = (bf16[336,128]{1,0:T(8,128)(2,1)S(1)}, bf16[336,128]{1,0:T(8,128)(2,1)S(1)}, u32[]{:S(2)}, u32[]{:S(2)}) collective-permute-start(bf16[336,128]{1,0:T(8,128)(2,1)S(1)} %get-tuple-element.19), channel_id=1, source_target_pairs={{0,4},{4,0},{8,12},{12,8},{16,20},{20,16},{24,28},{28,24},{1,5},{5... | collective-permute-start | bytes 258056 | tf_op jit(solution)/shard_map/ppermute | solution.py:243
  9.0 6.7 %collective-permute-start.2 = (bf16[336,128]{1,0:T(8,128)(2,1)S(1)}, bf16[336,128]{1,0:T(8,128)(2,1)S(1)}, u32[]{:S(2)}, u32[]{:S(2)}) collective-permute-start(bf16[336,128]{1,0:T(8,128)(2,1)S(1)} %get-tuple-element.19), channel_id=1, source_target_pairs={{0,8},{4,12},{8,0},{12,4},{16,24},{20,28},{24,16},{28,20},{1,9},{5... | collective-permute-start | bytes 258056 | tf_op jit(solution)/shard_map/ppermute | solution.py:243
  12.1 6.1 %collective-permute-start.4 = (bf16[336,128]{1,0:T(8,128)(2,1)S(1)}, bf16[336,128]{1,0:T(8,128)(2,1)S(1)}, u32[]{:S(2)}, u32[]{:S(2)}) collective-permute-start(bf16[336,128]{1,0:T(8,128)(2,1)S(1)} %shard_map.52.refs_4_), channel_id=1, source_target_pairs={{0,12},{4,8},{8,4},{12,0},{16,28},{20,24},{24,20},{28,16},{1,13},{... | collective-permute-start | bytes 258056 | tf_op jit(solution)/shard_map/ppermute | solution.py:243
  14.7 4.5 %collective-permute-start.5 = (bf16[336,128]{1,0:T(8,128)(2,1)S(1)}, bf16[336,128]{1,0:T(8,128)(2,1)S(1)}, u32[]{:S(2)}, u32[]{:S(2)}) collective-permute-start(bf16[336,128]{1,0:T(8,128)(2,1)S(1)} %shard_map.52.refs_4_), channel_id=1, source_target_pairs={{0,4},{4,0},{8,12},{12,8},{16,20},{20,16},{24,28},{28,24},{1,5},{5... | collective-permute-start | bytes 258056 | tf_op jit(solution)/shard_map/ppermute | solution.py:243
  15.2 4.5 %collective-permute-start.6 = (bf16[336,128]{1,0:T(8,128)(2,1)S(1)}, bf16[336,128]{1,0:T(8,128)(2,1)S(1)}, u32[]{:S(2)}, u32[]{:S(2)}) collective-permute-start(bf16[336,128]{1,0:T(8,128)(2,1)S(1)} %shard_map.52.refs_4_), channel_id=1, source_target_pairs={{0,8},{4,12},{8,0},{12,4},{16,24},{20,28},{24,16},{28,20},{1,9},{5... | collective-permute-start | bytes 258056 | tf_op jit(solution)/shard_map/ppermute | solution.py:243
  20.4 1.5 %collective-permute-start.7 = (f32[336,128]{1,0:T(8,128)S(1)}, f32[336,128]{1,0:T(8,128)S(1)}, u32[]{:S(2)}, u32[]{:S(2)}) collective-permute-start(f32[336,128]{1,0:T(8,128)S(1)} %shard_map.55.sent_ref), channel_id=1, source_target_pairs={{0,1},{1,0},{2,3},{3,2},{4,5},{5,4},{6,7},{7,6},{8,9},{9,8},{10,11... | collective-permute-start | bytes 516104 | tf_op jit(solution)/shard_map/ppermute | solution.py:243
  21.9 4.2 %collective-permute-start.8 = (f32[80,128]{1,0:T(8,128)S(1)}, f32[80,128]{1,0:T(8,128)S(1)}, u32[]{:S(2)}, u32[]{:S(2)}) collective-permute-start(f32[80,128]{1,0:T(8,128)S(1)} %get-tuple-element.23.refs_0_), channel_id=1, source_target_pairs={{0,2},{1,3},{2,0},{3,1},{4,6},{5,7},{6,4},{7,5},{8,10},{9,11},{10,... | collective-permute-start | bytes 122888 | tf_op jit(solution)/shard_map/ppermute | solution.py:243
  23.4 5.9 %collective-permute-start.9 = (f32[128,128]{1,0:T(8,128)S(1)}, f32[128,128]{1,0:T(8,128)S(1)}, u32[]{:S(2)}, u32[]{:S(2)}) collective-permute-start(f32[128,128]{1,0:T(8,128)S(1)} %get-tuple-element.25), channel_id=1, source_target_pairs={{0,2},{1,3},{2,0},{3,1},{4,6},{5,7},{6,4},{7,5},{8,10},{9,11},{10,... | collective-permute-start | bytes 196616 | tf_op jit(solution)/shard_map/ppermute | solution.py:243
  39.8 0.7 %copy-start.1 = (f32[128]{0:T(128)}, f32[128]{0:T(128)S(1)}, u32[]{:S(2)}) copy-start(f32[128]{0:T(128)S(1)} %add_sqrt_fusion) | copy-start | bytes 1540

commit v8 on v7

--- a/solution.py
+++ b/solution.py
@@ -71,7 +71,9 @@
     row = lax.axis_index("row")
     arrivals = []
     for at, owner in enumerate(owners):
-        start = pl.multiple_of(lax.bitwise_xor(row, owner) * depth, depth)
+        start = 0
+        if depth < tensor_ref.shape[2]:
+            start = pl.multiple_of(lax.bitwise_xor(row, owner) * depth, depth)
         arrivals.append(
             pltpu.make_async_copy(
                 tensor_ref.at[:, :, pl.ds(start, depth)], slots_ref.at[at], sems.at[at]

time: 40.6 us -> 40.6 us (level)
  no operation moved by 1% of the time
where the time goes in v8:
time: 40.6 us; the launch traced here: 40.4 us
  starting transfers between devices  13.3 us (33%)
  Pallas kernels  10.1 us (25%)
  blocking collectives  10.1 us (25%)
  waiting for transfers between devices  4.52 us (11%)
  local copies, waits for them, and re-layouts  0.9 us (2%)
  between operations  0.72 us (2%)
  other arithmetic  0.7 us (2%)
    ppermute x10, starting transfers between devices, shifted(): lax.ppermute(value, axis, [(at, at ^ offset) for at in range(groups)])  13.3 us
    pallas_call x9, Pallas kernels, call(): pl.pallas_call(kernel, out_shape=tuple((jax.ShapeDtypeStruct(shape, dtype...  10.1 us
    all_to_all x1, blocking collectives, per_device(): squares = lax.all_to_all(squares, ('row', 'col'), 0, 0, tiled=True)  10.1 us
    ppermute x10, waiting for transfers between devices, shifted(): lax.ppermute(value, axis, [(at, at ^ offset) for at in range(groups)])  4.52 us
    unnamed x4, local copies, waits for them, and re-layouts  0.9 us
  transfers between devices with their start and end apart: 10, of which 5 were waited for; matrix products, arithmetic and copies ran while one was open for 0% of the time, Pallas kernels for 22%

profile of v8, /device:TPU:0, one launch (start us, length us, event | category | flops | bytes accessed | tf_op | source)
XLA Modules:
  0.0 40.4 jit_solution(12674052456418988906)
XLA Ops:
  0.6 0.9 %copy-done = f32[256,128]{1,0:T(8,128)S(1)} copy-done((f32[256,128]{1,0:T(8,128)S(1)}, f32[256,128]{1,0:T(8,128)}, u32[]{:S(2)}) %copy-start) | copy-done | bytes 131096
  1.5 0.3 shard_map.51
  1.9 4.1 %collective-permute-start.3 = (bf16[336,128]{1,0:T(8,128)(2,1)S(1)}, bf16[336,128]{1,0:T(8,128)(2,1)S(1)}, u32[]{:S(2)}, u32[]{:S(2)}) collective-permute-start(bf16[336,128]{1,0:T(8,128)(2,1)S(1)} %get-tuple-element.19), channel_id=1, source_target_pairs={{0,16},{4,20},{8,24},{12,28},{16,0},{20,4},{24,8},{28,12},{1,17},{... | collective-permute-start | bytes 258056 | tf_op jit(solution)/shard_map/ppermute | solution.py:245
  5.9 2.5 %collective-permute-start = (bf16[336,128]{1,0:T(8,128)(2,1)S(1)}, bf16[336,128]{1,0:T(8,128)(2,1)S(1)}, u32[]{:S(2)}, u32[]{:S(2)}) collective-permute-start(bf16[336,128]{1,0:T(8,128)(2,1)S(1)} %get-tuple-element.19), channel_id=1, source_target_pairs={{0,12},{4,8},{8,4},{12,0},{16,28},{20,24},{24,20},{28,16},{1,13},{... | collective-permute-start | bytes 258056 | tf_op jit(solution)/shard_map/ppermute | solution.py:245
  8.5 0.5 %collective-permute-start.1 = (bf16[336,128]{1,0:T(8,128)(2,1)S(1)}, bf16[336,128]{1,0:T(8,128)(2,1)S(1)}, u32[]{:S(2)}, u32[]{:S(2)}) collective-permute-start(bf16[336,128]{1,0:T(8,128)(2,1)S(1)} %get-tuple-element.19), channel_id=1, source_target_pairs={{0,4},{4,0},{8,12},{12,8},{16,20},{20,16},{24,28},{28,24},{1,5},{5... | collective-permute-start | bytes 258056 | tf_op jit(solution)/shard_map/ppermute | solution.py:245
  9.0 0.4 %collective-permute-start.2 = (bf16[336,128]{1,0:T(8,128)(2,1)S(1)}, bf16[336,128]{1,0:T(8,128)(2,1)S(1)}, u32[]{:S(2)}, u32[]{:S(2)}) collective-permute-start(bf16[336,128]{1,0:T(8,128)(2,1)S(1)} %get-tuple-element.19), channel_id=1, source_target_pairs={{0,8},{4,12},{8,0},{12,4},{16,24},{20,28},{24,16},{28,20},{1,9},{5... | collective-permute-start | bytes 258056 | tf_op jit(solution)/shard_map/ppermute | solution.py:245
  9.4 2.6 %shard_map.50 = (f32[4,128]{1,0:T(4,128)S(1)}, f32[128,128]{1,0:T(8,128)S(1)}, bf16[5,4,512,256]{3,2,1,0:T(8,128)(2,1)S(1)}) custom-call(bf16[4,512,2048]{2,1,0:T(8,128)(2,1)} %tensor_ref.3, f32[4,128]{1,0:T(4,128)} %time_ref.1), custom_call_target="tpu_custom_call" | custom-call | tf_op jit(solution)/shard_map/pallas_call | solution.py:249
  12.1 0.0 collective-permute-done.3.part_ref
  12.1 2.6 %collective-permute-start.4 = (bf16[336,128]{1,0:T(8,128)(2,1)S(1)}, bf16[336,128]{1,0:T(8,128)(2,1)S(1)}, u32[]{:S(2)}, u32[]{:S(2)}) collective-permute-start(bf16[336,128]{1,0:T(8,128)(2,1)S(1)} %shard_map.52.refs_4_), channel_id=1, source_target_pairs={{0,12},{4,8},{8,4},{12,0},{16,28},{20,24},{24,20},{28,16},{1,13},{... | collective-permute-start | bytes 258056 | tf_op jit(solution)/shard_map/ppermute | solution.py:245
  14.7 0.5 %collective-permute-start.5 = (bf16[336,128]{1,0:T(8,128)(2,1)S(1)}, bf16[336,128]{1,0:T(8,128)(2,1)S(1)}, u32[]{:S(2)}, u32[]{:S(2)}) collective-permute-start(bf16[336,128]{1,0:T(8,128)(2,1)S(1)} %shard_map.52.refs_4_), channel_id=1, source_target_pairs={{0,4},{4,0},{8,12},{12,8},{16,20},{20,16},{24,28},{28,24},{1,5},{5... | collective-permute-start | bytes 258056 | tf_op jit(solution)/shard_map/ppermute | solution.py:245
  15.2 0.0 collective-permute-done.refs_1_
  15.2 0.5 %collective-permute-start.6 = (bf16[336,128]{1,0:T(8,128)(2,1)S(1)}, bf16[336,128]{1,0:T(8,128)(2,1)S(1)}, u32[]{:S(2)}, u32[]{:S(2)}) collective-permute-start(bf16[336,128]{1,0:T(8,128)(2,1)S(1)} %shard_map.52.refs_4_), channel_id=1, source_target_pairs={{0,8},{4,12},{8,0},{12,4},{16,24},{20,28},{24,16},{28,20},{1,9},{5... | collective-permute-start | bytes 258056 | tf_op jit(solution)/shard_map/ppermute | solution.py:245
  15.6 0.0 collective-permute-done.1.refs_2_
  15.6 0.0 collective-permute-done.2.refs_3_
  15.6 2.4 %shard_map.53 = (f32[512,128]{1,0:T(8,128)S(1)}, f32[80,128]{1,0:T(8,128)S(1)}, bf16[3,4,512,256]{3,2,1,0:T(8,128)(2,1)S(1)}) custom-call(bf16[4,512,2048]{2,1,0:T(8,128)(2,1)} %tensor_ref.3, f32[4,128]{1,0:T(4,128)S(1)} %get-tuple-element.16.ready_ref.time_ref, bf16[5,4,512,256]{3,2,1,0:T(8,128)(2,1)S(1)} %get-tuple-element.17.early_ref, ...), custom_call_target="tpu_custom_call" | custom-call | tf_op jit(solution)/shard_map/pallas_call | solution.py:249
  18.1 0.1 collective-permute-done.4.refs_0_
  18.2 1.0 %collective-permute-done.5.refs_1_ = bf16[336,128]{1,0:T(8,128)(2,1)S(1)} collective-permute-done((bf16[336,128]{1,0:T(8,128)(2,1)S(1)}, bf16[336,128]{1,0:T(8,128)(2,1)S(1)}, u32[]{:S(2)}, u32[]{:S(2)}) %collective-permute-start.5) | collective-permute-done | bytes 86048 | tf_op jit(solution)/shard_map/ppermute | solution.py:245
  19.2 0.5 %collective-permute-done.6.refs_2_ = bf16[336,128]{1,0:T(8,128)(2,1)S(1)} collective-permute-done((bf16[336,128]{1,0:T(8,128)(2,1)S(1)}, bf16[336,128]{1,0:T(8,128)(2,1)S(1)}, u32[]{:S(2)}, u32[]{:S(2)}) %collective-permute-start.6) | collective-permute-done | bytes 86048 | tf_op jit(solution)/shard_map/ppermute | solution.py:245
  19.7 0.7 %shard_map.55.sent_ref = f32[336,128]{1,0:T(8,128)S(1)} custom-call(f32[4,128]{1,0:T(4,128)S(1)} %get-tuple-element.16.ready_ref.time_ref, bf16[5,4,512,256]{3,2,1,0:T(8,128)(2,1)S(1)} %get-tuple-element.17.early_ref, bf16[3,4,512,256]{3,2,1,0:T(8,128)(2,1)S(1)} %get-tuple-element.20.later_ref, f32[512,128]{1,0:T(8,128)S(1)} %get-tuple-element.21.result_ref, ...), custom_call_target="tpu_custom_call" | custom-call | tf_op jit(solution)/shard_map/pallas_call | solution.py:249
  20.4 0.1 collective-permute-start.7
  20.4 0.6 %shard_map.54.keep_ref = f32[256,128]{1,0:T(8,128)S(1)} custom-call(f32[4,128]{1,0:T(4,128)S(1)} %get-tuple-element.16.ready_ref.time_ref, bf16[5,4,512,256]{3,2,1,0:T(8,128)(2,1)S(1)} %get-tuple-element.17.early_ref, bf16[3,4,512,256]{3,2,1,0:T(8,128)(2,1)S(1)} %get-tuple-element.20.later_ref, f32[512,128]{1,0:T(8,128)S(1)} %get-tuple-element.21.result_ref, ...), custom_call_target="tpu_custom_call" | custom-call | flops 1000000000 | tf_op jit(solution)/shard_map/pallas_call | solution.py:249
  21.0 0.8 %collective-permute-done.7.got_ref = f32[336,128]{1,0:T(8,128)S(1)} collective-permute-done((f32[336,128]{1,0:T(8,128)S(1)}, f32[336,128]{1,0:T(8,128)S(1)}, u32[]{:S(2)}, u32[]{:S(2)}) %collective-permute-start.7) | collective-permute-done | bytes 172064 | tf_op jit(solution)/shard_map/ppermute | solution.py:245
  21.9 1.6 %collective-permute-start.8 = (f32[80,128]{1,0:T(8,128)S(1)}, f32[80,128]{1,0:T(8,128)S(1)}, u32[]{:S(2)}, u32[]{:S(2)}) collective-permute-start(f32[80,128]{1,0:T(8,128)S(1)} %get-tuple-element.23.refs_0_), channel_id=1, source_target_pairs={{0,2},{1,3},{2,0},{3,1},{4,6},{5,7},{6,4},{7,5},{8,10},{9,11},{10,... | collective-permute-start | bytes 122888 | tf_op jit(solution)/shard_map/ppermute | solution.py:245
  23.4 0.5 %collective-permute-start.9 = (f32[128,128]{1,0:T(8,128)S(1)}, f32[128,128]{1,0:T(8,128)S(1)}, u32[]{:S(2)}, u32[]{:S(2)}) collective-permute-start(f32[128,128]{1,0:T(8,128)S(1)} %get-tuple-element.25), channel_id=1, source_target_pairs={{0,2},{1,3},{2,0},{3,1},{4,6},{5,7},{6,4},{7,5},{8,10},{9,11},{10,... | collective-permute-start | bytes 196616 | tf_op jit(solution)/shard_map/ppermute | solution.py:245
  24.0 2.1 %collective-permute-done.8.refs_1_ = f32[80,128]{1,0:T(8,128)S(1)} collective-permute-done((f32[80,128]{1,0:T(8,128)S(1)}, f32[80,128]{1,0:T(8,128)S(1)}, u32[]{:S(2)}, u32[]{:S(2)}) %collective-permute-start.8) | collective-permute-done | bytes 40992 | tf_op jit(solution)/shard_map/ppermute | solution.py:245
  26.1 3.3 %shard_map.57.inverse_ref = f32[128,128]{1,0:T(8,128)S(1)} custom-call(f32[128,128]{1,0:T(8,128)S(1)} %get-tuple-element.15.time_gram_ref, f32[80,128]{1,0:T(8,128)S(1)} %get-tuple-element.23.refs_0_, f32[80,128]{1,0:T(8,128)S(1)} %collective-permute-done.8.refs_1_), custom_call_target="tpu_custom_call" | custom-call | flops 2000000000 | tf_op jit(solution)/shard_map/pallas_call | solution.py:249
  29.3 0.0 collective-permute-done.9.refs_1_
  29.3 0.2 shard_map.58
  29.6 10.1 %all_to_all.9 = f32[32,1,128]{2,1,0:T(1,128)S(1)} all-to-all(f32[32,1,128]{2,1,0:T(1,128)S(1)} %bitcast.3), channel_id=1, replica_groups=mesh['row'=8,'col'=4] {'row','col'}, dimensions={0} | all-to-all | bytes 32768 | tf_op jit(solution)/shard_map/all_to_all | solution.py:333
  39.7 0.1 reduce_sum.9
  39.8 0.6 %broadcast_divide_fusion = f32[128,128]{1,0:T(8,128)} fusion(f32[128,128]{1,0:T(8,128)S(1)} %get-tuple-element.26, f32[128]{0:T(128)S(1)} %add_sqrt_fusion), kind=kLoop, calls=%fused_computation | loop fusion | flops 16384 | bytes 131584 | tf_op jit(solution)/shard_map/div | solution.py:335
  40.4 0.0 copy-done.1
  (5 shorter events, 0.0 us)
Async XLA Ops:
  0.6 0.9 %copy-start = (f32[256,128]{1,0:T(8,128)S(1)}, f32[256,128]{1,0:T(8,128)}, u32[]{:S(2)}) copy-start(f32[256,128]{1,0:T(8,128)} %factor_ref.1) | copy-start | bytes 393220
  1.9 10.2 %collective-permute-start.3 = (bf16[336,128]{1,0:T(8,128)(2,1)S(1)}, bf16[336,128]{1,0:T(8,128)(2,1)S(1)}, u32[]{:S(2)}, u32[]{:S(2)}) collective-permute-start(bf16[336,128]{1,0:T(8,128)(2,1)S(1)} %get-tuple-element.19), channel_id=1, source_target_pairs={{0,16},{4,20},{8,24},{12,28},{16,0},{20,4},{24,8},{28,12},{1,17},{... | collective-permute-start | bytes 258056 | tf_op jit(solution)/shard_map/ppermute | solution.py:245
  5.9 9.3 %collective-permute-start = (bf16[336,128]{1,0:T(8,128)(2,1)S(1)}, bf16[336,128]{1,0:T(8,128)(2,1)S(1)}, u32[]{:S(2)}, u32[]{:S(2)}) collective-permute-start(bf16[336,128]{1,0:T(8,128)(2,1)S(1)} %get-tuple-element.19), channel_id=1, source_target_pairs={{0,12},{4,8},{8,4},{12,0},{16,28},{20,24},{24,20},{28,16},{1,13},{... | collective-permute-start | bytes 258056 | tf_op jit(solution)/shard_map/ppermute | solution.py:245
  8.5 7.2 %collective-permute-start.1 = (bf16[336,128]{1,0:T(8,128)(2,1)S(1)}, bf16[336,128]{1,0:T(8,128)(2,1)S(1)}, u32[]{:S(2)}, u32[]{:S(2)}) collective-permute-start(bf16[336,128]{1,0:T(8,128)(2,1)S(1)} %get-tuple-element.19), channel_id=1, source_target_pairs={{0,4},{4,0},{8,12},{12,8},{16,20},{20,16},{24,28},{28,24},{1,5},{5... | collective-permute-start | bytes 258056 | tf_op jit(solution)/shard_map/ppermute | solution.py:245
  9.0 6.7 %collective-permute-start.2 = (bf16[336,128]{1,0:T(8,128)(2,1)S(1)}, bf16[336,128]{1,0:T(8,128)(2,1)S(1)}, u32[]{:S(2)}, u32[]{:S(2)}) collective-permute-start(bf16[336,128]{1,0:T(8,128)(2,1)S(1)} %get-tuple-element.19), channel_id=1, source_target_pairs={{0,8},{4,12},{8,0},{12,4},{16,24},{20,28},{24,16},{28,20},{1,9},{5... | collective-permute-start | bytes 258056 | tf_op jit(solution)/shard_map/ppermute | solution.py:245
  12.1 6.1 %collective-permute-start.4 = (bf16[336,128]{1,0:T(8,128)(2,1)S(1)}, bf16[336,128]{1,0:T(8,128)(2,1)S(1)}, u32[]{:S(2)}, u32[]{:S(2)}) collective-permute-start(bf16[336,128]{1,0:T(8,128)(2,1)S(1)} %shard_map.52.refs_4_), channel_id=1, source_target_pairs={{0,12},{4,8},{8,4},{12,0},{16,28},{20,24},{24,20},{28,16},{1,13},{... | collective-permute-start | bytes 258056 | tf_op jit(solution)/shard_map/ppermute | solution.py:245
  14.7 4.5 %collective-permute-start.5 = (bf16[336,128]{1,0:T(8,128)(2,1)S(1)}, bf16[336,128]{1,0:T(8,128)(2,1)S(1)}, u32[]{:S(2)}, u32[]{:S(2)}) collective-permute-start(bf16[336,128]{1,0:T(8,128)(2,1)S(1)} %shard_map.52.refs_4_), channel_id=1, source_target_pairs={{0,4},{4,0},{8,12},{12,8},{16,20},{20,16},{24,28},{28,24},{1,5},{5... | collective-permute-start | bytes 258056 | tf_op jit(solution)/shard_map/ppermute | solution.py:245
  15.2 4.5 %collective-permute-start.6 = (bf16[336,128]{1,0:T(8,128)(2,1)S(1)}, bf16[336,128]{1,0:T(8,128)(2,1)S(1)}, u32[]{:S(2)}, u32[]{:S(2)}) collective-permute-start(bf16[336,128]{1,0:T(8,128)(2,1)S(1)} %shard_map.52.refs_4_), channel_id=1, source_target_pairs={{0,8},{4,12},{8,0},{12,4},{16,24},{20,28},{24,16},{28,20},{1,9},{5... | collective-permute-start | bytes 258056 | tf_op jit(solution)/shard_map/ppermute | solution.py:245
  20.4 1.5 %collective-permute-start.7 = (f32[336,128]{1,0:T(8,128)S(1)}, f32[336,128]{1,0:T(8,128)S(1)}, u32[]{:S(2)}, u32[]{:S(2)}) collective-permute-start(f32[336,128]{1,0:T(8,128)S(1)} %shard_map.55.sent_ref), channel_id=1, source_target_pairs={{0,1},{1,0},{2,3},{3,2},{4,5},{5,4},{6,7},{7,6},{8,9},{9,8},{10,11... | collective-permute-start | bytes 516104 | tf_op jit(solution)/shard_map/ppermute | solution.py:245
  21.9 4.2 %collective-permute-start.8 = (f32[80,128]{1,0:T(8,128)S(1)}, f32[80,128]{1,0:T(8,128)S(1)}, u32[]{:S(2)}, u32[]{:S(2)}) collective-permute-start(f32[80,128]{1,0:T(8,128)S(1)} %get-tuple-element.23.refs_0_), channel_id=1, source_target_pairs={{0,2},{1,3},{2,0},{3,1},{4,6},{5,7},{6,4},{7,5},{8,10},{9,11},{10,... | collective-permute-start | bytes 122888 | tf_op jit(solution)/shard_map/ppermute | solution.py:245
  23.4 5.9 %collective-permute-start.9 = (f32[128,128]{1,0:T(8,128)S(1)}, f32[128,128]{1,0:T(8,128)S(1)}, u32[]{:S(2)}, u32[]{:S(2)}) collective-permute-start(f32[128,128]{1,0:T(8,128)S(1)} %get-tuple-element.25), channel_id=1, source_target_pairs={{0,2},{1,3},{2,0},{3,1},{4,6},{5,7},{6,4},{7,5},{8,10},{9,11},{10,... | collective-permute-start | bytes 196616 | tf_op jit(solution)/shard_map/ppermute | solution.py:245
  39.8 0.7 %copy-start.1 = (f32[128]{0:T(128)}, f32[128]{0:T(128)S(1)}, u32[]{:S(2)}) copy-start(f32[128]{0:T(128)S(1)} %add_sqrt_fusion) | copy-start | bytes 1540

commit v9 on v8

--- a/solution.py
+++ b/solution.py
@@ -273,7 +273,7 @@
     arrived = {at: shifted(message, "row", at, rows) for at in near}
     in_hbm = pltpu.with_memory_space_constraint(tensor, pltpu.HBM)
     direct = depth % 128 == 0
-    owners, width = ([0, *near, half, *(half + at for at in near)], depth) if direct else ([0], own_cols)
+    owners, width = ([0, *range(1, half), half, *(half + at for at in near)], depth) if direct else ([0], own_cols)
     block = (snaps, own_rows, width)
     begin, split = (half + 1, half + 1) if direct else (1, 1)
     time, time_gram, early = call(

time: 40.6 us -> 40.6 us (level)
  no operation moved by 1% of the time
where the time goes in v9:
time: 40.6 us; the launch traced here: 40.4 us
  starting transfers between devices  13.3 us (33%)
  Pallas kernels  10.1 us (25%)
  blocking collectives  10.1 us (25%)
  waiting for transfers between devices  4.53 us (11%)
  local copies, waits for them, and re-layouts  0.9 us (2%)
  between operations  0.72 us (2%)
  other arithmetic  0.7 us (2%)
    ppermute x10, starting transfers between devices, shifted(): lax.ppermute(value, axis, [(at, at ^ offset) for at in range(groups)])  13.3 us
    pallas_call x9, Pallas kernels, call(): pl.pallas_call(kernel, out_shape=tuple((jax.ShapeDtypeStruct(shape, dtype...  10.1 us
    all_to_all x1, blocking collectives, per_device(): squares = lax.all_to_all(squares, ('row', 'col'), 0, 0, tiled=True)  10.1 us
    ppermute x10, waiting for transfers between devices, shifted(): lax.ppermute(value, axis, [(at, at ^ offset) for at in range(groups)])  4.53 us
    unnamed x4, local copies, waits for them, and re-layouts  0.9 us
  transfers between devices with their start and end apart: 10, of which 5 were waited for; matrix products, arithmetic and copies ran while one was open for 0% of the time, Pallas kernels for 22%

profile of v9, /device:TPU:0, one launch (start us, length us, event | category | flops | bytes accessed | tf_op | source)
XLA Modules:
  0.0 40.4 jit_solution(279871235859200877)
XLA Ops:
  0.6 0.0 copy-start
  0.6 0.9 %copy-done = f32[256,128]{1,0:T(8,128)S(1)} copy-done((f32[256,128]{1,0:T(8,128)S(1)}, f32[256,128]{1,0:T(8,128)}, u32[]{:S(2)}) %copy-start) | copy-done | bytes 131096
  1.5 0.3 shard_map.51
  1.9 4.1 %collective-permute-start.3 = (bf16[336,128]{1,0:T(8,128)(2,1)S(1)}, bf16[336,128]{1,0:T(8,128)(2,1)S(1)}, u32[]{:S(2)}, u32[]{:S(2)}) collective-permute-start(bf16[336,128]{1,0:T(8,128)(2,1)S(1)} %get-tuple-element.19), channel_id=1, source_target_pairs={{0,16},{4,20},{8,24},{12,28},{16,0},{20,4},{24,8},{28,12},{1,17},{... | collective-permute-start | bytes 258056 | tf_op jit(solution)/shard_map/ppermute | solution.py:245
  5.9 1.5 %collective-permute-start = (bf16[336,128]{1,0:T(8,128)(2,1)S(1)}, bf16[336,128]{1,0:T(8,128)(2,1)S(1)}, u32[]{:S(2)}, u32[]{:S(2)}) collective-permute-start(bf16[336,128]{1,0:T(8,128)(2,1)S(1)} %get-tuple-element.19), channel_id=1, source_target_pairs={{0,4},{4,0},{8,12},{12,8},{16,20},{20,16},{24,28},{28,24},{1,5},{5... | collective-permute-start | bytes 258056 | tf_op jit(solution)/shard_map/ppermute | solution.py:245
  7.5 1.6 %collective-permute-start.1 = (bf16[336,128]{1,0:T(8,128)(2,1)S(1)}, bf16[336,128]{1,0:T(8,128)(2,1)S(1)}, u32[]{:S(2)}, u32[]{:S(2)}) collective-permute-start(bf16[336,128]{1,0:T(8,128)(2,1)S(1)} %get-tuple-element.19), channel_id=1, source_target_pairs={{0,8},{4,12},{8,0},{12,4},{16,24},{20,28},{24,16},{28,20},{1,9},{5... | collective-permute-start | bytes 258056 | tf_op jit(solution)/shard_map/ppermute | solution.py:245
  9.0 0.4 collective-permute-start.2
  9.4 2.6 %shard_map.50 = (f32[4,128]{1,0:T(4,128)S(1)}, f32[128,128]{1,0:T(8,128)S(1)}, bf16[5,4,512,256]{3,2,1,0:T(8,128)(2,1)S(1)}) custom-call(bf16[4,512,2048]{2,1,0:T(8,128)(2,1)} %tensor_ref.3, f32[4,128]{1,0:T(4,128)} %time_ref.1), custom_call_target="tpu_custom_call" | custom-call | tf_op jit(solution)/shard_map/pallas_call | solution.py:249
  12.1 0.0 collective-permute-done.3.part_ref
  12.1 2.6 %collective-permute-start.4 = (bf16[336,128]{1,0:T(8,128)(2,1)S(1)}, bf16[336,128]{1,0:T(8,128)(2,1)S(1)}, u32[]{:S(2)}, u32[]{:S(2)}) collective-permute-start(bf16[336,128]{1,0:T(8,128)(2,1)S(1)} %shard_map.52.refs_4_), channel_id=1, source_target_pairs={{0,12},{4,8},{8,4},{12,0},{16,28},{20,24},{24,20},{28,16},{1,13},{... | collective-permute-start | bytes 258056 | tf_op jit(solution)/shard_map/ppermute | solution.py:245
  14.7 0.5 %collective-permute-start.5 = (bf16[336,128]{1,0:T(8,128)(2,1)S(1)}, bf16[336,128]{1,0:T(8,128)(2,1)S(1)}, u32[]{:S(2)}, u32[]{:S(2)}) collective-permute-start(bf16[336,128]{1,0:T(8,128)(2,1)S(1)} %shard_map.52.refs_4_), channel_id=1, source_target_pairs={{0,4},{4,0},{8,12},{12,8},{16,20},{20,16},{24,28},{28,24},{1,5},{5... | collective-permute-start | bytes 258056 | tf_op jit(solution)/shard_map/ppermute | solution.py:245
  15.2 0.0 collective-permute-done.refs_1_
  15.2 0.5 %collective-permute-start.6 = (bf16[336,128]{1,0:T(8,128)(2,1)S(1)}, bf16[336,128]{1,0:T(8,128)(2,1)S(1)}, u32[]{:S(2)}, u32[]{:S(2)}) collective-permute-start(bf16[336,128]{1,0:T(8,128)(2,1)S(1)} %shard_map.52.refs_4_), channel_id=1, source_target_pairs={{0,8},{4,12},{8,0},{12,4},{16,24},{20,28},{24,16},{28,20},{1,9},{5... | collective-permute-start | bytes 258056 | tf_op jit(solution)/shard_map/ppermute | solution.py:245
  15.6 0.0 collective-permute-done.1.refs_2_
  15.6 0.0 collective-permute-done.2.refs_3_
  15.6 2.4 %shard_map.53 = (f32[512,128]{1,0:T(8,128)S(1)}, f32[80,128]{1,0:T(8,128)S(1)}, bf16[3,4,512,256]{3,2,1,0:T(8,128)(2,1)S(1)}) custom-call(bf16[4,512,2048]{2,1,0:T(8,128)(2,1)} %tensor_ref.3, f32[4,128]{1,0:T(4,128)S(1)} %get-tuple-element.16.ready_ref.time_ref, bf16[5,4,512,256]{3,2,1,0:T(8,128)(2,1)S(1)} %get-tuple-element.17.early_ref, ...), custom_call_target="tpu_custom_call" | custom-call | tf_op jit(solution)/shard_map/pallas_call | solution.py:249
  18.1 0.1 collective-permute-done.4.refs_0_
  18.2 1.0 %collective-permute-done.5.refs_1_ = bf16[336,128]{1,0:T(8,128)(2,1)S(1)} collective-permute-done((bf16[336,128]{1,0:T(8,128)(2,1)S(1)}, bf16[336,128]{1,0:T(8,128)(2,1)S(1)}, u32[]{:S(2)}, u32[]{:S(2)}) %collective-permute-start.5) | collective-permute-done | bytes 86048 | tf_op jit(solution)/shard_map/ppermute | solution.py:245
  19.2 0.5 %collective-permute-done.6.refs_2_ = bf16[336,128]{1,0:T(8,128)(2,1)S(1)} collective-permute-done((bf16[336,128]{1,0:T(8,128)(2,1)S(1)}, bf16[336,128]{1,0:T(8,128)(2,1)S(1)}, u32[]{:S(2)}, u32[]{:S(2)}) %collective-permute-start.6) | collective-permute-done | bytes 86048 | tf_op jit(solution)/shard_map/ppermute | solution.py:245
  19.7 0.7 %shard_map.55.sent_ref = f32[336,128]{1,0:T(8,128)S(1)} custom-call(f32[4,128]{1,0:T(4,128)S(1)} %get-tuple-element.16.ready_ref.time_ref, bf16[5,4,512,256]{3,2,1,0:T(8,128)(2,1)S(1)} %get-tuple-element.17.early_ref, bf16[3,4,512,256]{3,2,1,0:T(8,128)(2,1)S(1)} %get-tuple-element.20.later_ref, f32[512,128]{1,0:T(8,128)S(1)} %get-tuple-element.21.result_ref, ...), custom_call_target="tpu_custom_call" | custom-call | tf_op jit(solution)/shard_map/pallas_call | solution.py:249
  20.4 0.1 collective-permute-start.7
  20.4 0.6 %shard_map.54.keep_ref = f32[256,128]{1,0:T(8,128)S(1)} custom-call(f32[4,128]{1,0:T(4,128)S(1)} %get-tuple-element.16.ready_ref.time_ref, bf16[5,4,512,256]{3,2,1,0:T(8,128)(2,1)S(1)} %get-tuple-element.17.early_ref, bf16[3,4,512,256]{3,2,1,0:T(8,128)(2,1)S(1)} %get-tuple-element.20.later_ref, f32[512,128]{1,0:T(8,128)S(1)} %get-tuple-element.21.result_ref, ...), custom_call_target="tpu_custom_call" | custom-call | flops 1000000000 | tf_op jit(solution)/shard_map/pallas_call | solution.py:249
  21.0 0.8 %collective-permute-done.7.got_ref = f32[336,128]{1,0:T(8,128)S(1)} collective-permute-done((f32[336,128]{1,0:T(8,128)S(1)}, f32[336,128]{1,0:T(8,128)S(1)}, u32[]{:S(2)}, u32[]{:S(2)}) %collective-permute-start.7) | collective-permute-done | bytes 172064 | tf_op jit(solution)/shard_map/ppermute | solution.py:245
  21.9 1.6 %collective-permute-start.8 = (f32[80,128]{1,0:T(8,128)S(1)}, f32[80,128]{1,0:T(8,128)S(1)}, u32[]{:S(2)}, u32[]{:S(2)}) collective-permute-start(f32[80,128]{1,0:T(8,128)S(1)} %get-tuple-element.23.refs_0_), channel_id=1, source_target_pairs={{0,2},{1,3},{2,0},{3,1},{4,6},{5,7},{6,4},{7,5},{8,10},{9,11},{10,... | collective-permute-start | bytes 122888 | tf_op jit(solution)/shard_map/ppermute | solution.py:245
  23.4 0.5 %collective-permute-start.9 = (f32[128,128]{1,0:T(8,128)S(1)}, f32[128,128]{1,0:T(8,128)S(1)}, u32[]{:S(2)}, u32[]{:S(2)}) collective-permute-start(f32[128,128]{1,0:T(8,128)S(1)} %get-tuple-element.25), channel_id=1, source_target_pairs={{0,2},{1,3},{2,0},{3,1},{4,6},{5,7},{6,4},{7,5},{8,10},{9,11},{10,... | collective-permute-start | bytes 196616 | tf_op jit(solution)/shard_map/ppermute | solution.py:245
  24.0 2.1 %collective-permute-done.8.refs_1_ = f32[80,128]{1,0:T(8,128)S(1)} collective-permute-done((f32[80,128]{1,0:T(8,128)S(1)}, f32[80,128]{1,0:T(8,128)S(1)}, u32[]{:S(2)}, u32[]{:S(2)}) %collective-permute-start.8) | collective-permute-done | bytes 40992 | tf_op jit(solution)/shard_map/ppermute | solution.py:245
  26.1 3.3 %shard_map.57.inverse_ref = f32[128,128]{1,0:T(8,128)S(1)} custom-call(f32[128,128]{1,0:T(8,128)S(1)} %get-tuple-element.15.time_gram_ref, f32[80,128]{1,0:T(8,128)S(1)} %get-tuple-element.23.refs_0_, f32[80,128]{1,0:T(8,128)S(1)} %collective-permute-done.8.refs_1_), custom_call_target="tpu_custom_call" | custom-call | flops 2000000000 | tf_op jit(solution)/shard_map/pallas_call | solution.py:249
  29.3 0.0 collective-permute-done.9.refs_1_
  29.3 0.2 shard_map.58
  29.6 10.1 %all_to_all.9 = f32[32,1,128]{2,1,0:T(1,128)S(1)} all-to-all(f32[32,1,128]{2,1,0:T(1,128)S(1)} %bitcast.3), channel_id=1, replica_groups=mesh['row'=8,'col'=4] {'row','col'}, dimensions={0} | all-to-all | bytes 32768 | tf_op jit(solution)/shard_map/all_to_all | solution.py:333
  39.7 0.1 reduce_sum.9
  39.8 0.6 %broadcast_divide_fusion = f32[128,128]{1,0:T(8,128)} fusion(f32[128,128]{1,0:T(8,128)S(1)} %get-tuple-element.26, f32[128]{0:T(128)S(1)} %add_sqrt_fusion), kind=kLoop, calls=%fused_computation | loop fusion | flops 16384 | bytes 131584 | tf_op jit(solution)/shard_map/div | solution.py:335
  (5 shorter events, 0.0 us)
Async XLA Ops:
  0.6 0.9 %copy-start = (f32[256,128]{1,0:T(8,128)S(1)}, f32[256,128]{1,0:T(8,128)}, u32[]{:S(2)}) copy-start(f32[256,128]{1,0:T(8,128)} %factor_ref.1) | copy-start | bytes 393220
  1.9 10.2 %collective-permute-start.3 = (bf16[336,128]{1,0:T(8,128)(2,1)S(1)}, bf16[336,128]{1,0:T(8,128)(2,1)S(1)}, u32[]{:S(2)}, u32[]{:S(2)}) collective-permute-start(bf16[336,128]{1,0:T(8,128)(2,1)S(1)} %get-tuple-element.19), channel_id=1, source_target_pairs={{0,16},{4,20},{8,24},{12,28},{16,0},{20,4},{24,8},{28,12},{1,17},{... | collective-permute-start | bytes 258056 | tf_op jit(solution)/shard_map/ppermute | solution.py:245
  5.9 9.3 %collective-permute-start = (bf16[336,128]{1,0:T(8,128)(2,1)S(1)}, bf16[336,128]{1,0:T(8,128)(2,1)S(1)}, u32[]{:S(2)}, u32[]{:S(2)}) collective-permute-start(bf16[336,128]{1,0:T(8,128)(2,1)S(1)} %get-tuple-element.19), channel_id=1, source_target_pairs={{0,4},{4,0},{8,12},{12,8},{16,20},{20,16},{24,28},{28,24},{1,5},{5... | collective-permute-start | bytes 258056 | tf_op jit(solution)/shard_map/ppermute | solution.py:245
  7.5 8.2 %collective-permute-start.1 = (bf16[336,128]{1,0:T(8,128)(2,1)S(1)}, bf16[336,128]{1,0:T(8,128)(2,1)S(1)}, u32[]{:S(2)}, u32[]{:S(2)}) collective-permute-start(bf16[336,128]{1,0:T(8,128)(2,1)S(1)} %get-tuple-element.19), channel_id=1, source_target_pairs={{0,8},{4,12},{8,0},{12,4},{16,24},{20,28},{24,16},{28,20},{1,9},{5... | collective-permute-start | bytes 258056 | tf_op jit(solution)/shard_map/ppermute | solution.py:245
  9.0 6.6 %collective-permute-start.2 = (bf16[336,128]{1,0:T(8,128)(2,1)S(1)}, bf16[336,128]{1,0:T(8,128)(2,1)S(1)}, u32[]{:S(2)}, u32[]{:S(2)}) collective-permute-start(bf16[336,128]{1,0:T(8,128)(2,1)S(1)} %get-tuple-element.19), channel_id=1, source_target_pairs={{0,12},{4,8},{8,4},{12,0},{16,28},{20,24},{24,20},{28,16},{1,13},{... | collective-permute-start | bytes 258056 | tf_op jit(solution)/shard_map/ppermute | solution.py:245
  12.1 6.1 %collective-permute-start.4 = (bf16[336,128]{1,0:T(8,128)(2,1)S(1)}, bf16[336,128]{1,0:T(8,128)(2,1)S(1)}, u32[]{:S(2)}, u32[]{:S(2)}) collective-permute-start(bf16[336,128]{1,0:T(8,128)(2,1)S(1)} %shard_map.52.refs_4_), channel_id=1, source_target_pairs={{0,12},{4,8},{8,4},{12,0},{16,28},{20,24},{24,20},{28,16},{1,13},{... | collective-permute-start | bytes 258056 | tf_op jit(solution)/shard_map/ppermute | solution.py:245
  14.7 4.5 %collective-permute-start.5 = (bf16[336,128]{1,0:T(8,128)(2,1)S(1)}, bf16[336,128]{1,0:T(8,128)(2,1)S(1)}, u32[]{:S(2)}, u32[]{:S(2)}) collective-permute-start(bf16[336,128]{1,0:T(8,128)(2,1)S(1)} %shard_map.52.refs_4_), channel_id=1, source_target_pairs={{0,4},{4,0},{8,12},{12,8},{16,20},{20,16},{24,28},{28,24},{1,5},{5... | collective-permute-start | bytes 258056 | tf_op jit(solution)/shard_map/ppermute | solution.py:245
  15.2 4.5 %collective-permute-start.6 = (bf16[336,128]{1,0:T(8,128)(2,1)S(1)}, bf16[336,128]{1,0:T(8,128)(2,1)S(1)}, u32[]{:S(2)}, u32[]{:S(2)}) collective-permute-start(bf16[336,128]{1,0:T(8,128)(2,1)S(1)} %shard_map.52.refs_4_), channel_id=1, source_target_pairs={{0,8},{4,12},{8,0},{12,4},{16,24},{20,28},{24,16},{28,20},{1,9},{5... | collective-permute-start | bytes 258056 | tf_op jit(solution)/shard_map/ppermute | solution.py:245
  20.4 1.5 %collective-permute-start.7 = (f32[336,128]{1,0:T(8,128)S(1)}, f32[336,128]{1,0:T(8,128)S(1)}, u32[]{:S(2)}, u32[]{:S(2)}) collective-permute-start(f32[336,128]{1,0:T(8,128)S(1)} %shard_map.55.sent_ref), channel_id=1, source_target_pairs={{0,1},{1,0},{2,3},{3,2},{4,5},{5,4},{6,7},{7,6},{8,9},{9,8},{10,11... | collective-permute-start | bytes 516104 | tf_op jit(solution)/shard_map/ppermute | solution.py:245
  21.9 4.2 %collective-permute-start.8 = (f32[80,128]{1,0:T(8,128)S(1)}, f32[80,128]{1,0:T(8,128)S(1)}, u32[]{:S(2)}, u32[]{:S(2)}) collective-permute-start(f32[80,128]{1,0:T(8,128)S(1)} %get-tuple-element.23.refs_0_), channel_id=1, source_target_pairs={{0,2},{1,3},{2,0},{3,1},{4,6},{5,7},{6,4},{7,5},{8,10},{9,11},{10,... | collective-permute-start | bytes 122888 | tf_op jit(solution)/shard_map/ppermute | solution.py:245
  23.4 5.9 %collective-permute-start.9 = (f32[128,128]{1,0:T(8,128)S(1)}, f32[128,128]{1,0:T(8,128)S(1)}, u32[]{:S(2)}, u32[]{:S(2)}) collective-permute-start(f32[128,128]{1,0:T(8,128)S(1)} %get-tuple-element.25), channel_id=1, source_target_pairs={{0,2},{1,3},{2,0},{3,1},{4,6},{5,7},{6,4},{7,5},{8,10},{9,11},{10,... | collective-permute-start | bytes 196616 | tf_op jit(solution)/shard_map/ppermute | solution.py:245
  39.8 0.7 %copy-start.1 = (f32[128]{0:T(128)}, f32[128]{0:T(128)S(1)}, u32[]{:S(2)}) copy-start(f32[128]{0:T(128)S(1)} %add_sqrt_fusion) | copy-start | bytes 1540
